TPU v7x, 32 devices: a whole 2x2x4 slice. The times are simulated.
32 devices in a mesh: seq: 4 (over y, x), dp: 8 (over z, core).
Axes of the slice: x: 2, y: 2, z: 4, core: 2. Of those that a mesh axis runs over, the one named last changes fastest.
Arguments:
- tokens: bfloat16 [8, 2048, 768], P('dp', 'seq'), may hold values from -6 to 6
- ln_gain: bfloat16 [2, 768], P(None, 'dp'), may hold values from 0.5 to 1.5
- ln_bias: bfloat16 [2, 768], P(None, 'dp'), may hold values from -1.25 to 1.25
- w_qkv: bfloat16 [768, 2304], P('dp'), may hold values from -0.21875 to 0.21875
- qv_bias: bfloat16 [2, 768], P(None, 'dp'), may hold values from -1.25 to 1.25
- w_out: bfloat16 [768, 768], P('dp'), may hold values from -0.875 to 0.875
- w_fc: bfloat16 [768, 3072], P('dp'), may hold values from -0.21875 to 0.21875
- fc_bias: bfloat16 [3072], P('dp'), may hold values from -1.25 to 1.25
- w_proj: bfloat16 [3072, 768], P('dp'), may hold values from -0.109375 to 0.109375
- branch_bias: bfloat16 [2, 768], P(None, 'dp'), may hold values from -1.25 to 1.25
- cotangent: bfloat16 [8, 2048, 768], P('dp', 'seq'), may hold values from -8 to 8
Outputs:
- output: bfloat16 [8, 2048, 768], P('dp', 'seq')
- input_grad: bfloat16 [8, 2048, 768], P('dp', 'seq')
- grad_ln_gain: float32 [2, 768], P(None, 'dp')
- grad_ln_bias: float32 [2, 768], P(None, 'dp')
- grad_w_qkv: float32 [768, 2304], P('dp')
- grad_qv_bias: float32 [2, 768], P(None, 'dp')
- grad_w_out: float32 [768, 768], P('dp')
- grad_w_fc: float32 [768, 3072], P('dp')
- grad_fc_bias: float32 [3072], P('dp')
- grad_w_proj: float32 [3072, 768], P('dp')
- grad_branch_bias: float32 [2, 768], P(None, 'dp')
All inputs are finite; a program needn't handle non-finite values.
Results may differ from a plain program's by a relative error of at most 0.013.
Values may be sent and summed in bfloat16 or wider, within the bound.
A program may use at most 128 MiB of HBM per device.

v0:
```python
from functools import partial

import jax
import jax.numpy as jnp
from jax import lax
from jax.sharding import PartitionSpec as P

HEAD_DIM = 64


NORM_EPS = 1e-05


def layer_norm(vector, norm_gain, norm_shift):
    center = vector - jnp.mean(vector, axis=-1, keepdims=True)
    spread = jnp.mean(center * center, axis=-1, keepdims=True)
    return center * lax.rsqrt(spread + NORM_EPS) * norm_gain + norm_shift


def masked_scores(query_block, head_keys, block_index, block_rows, positions):
    scores = jnp.einsum(
        "qhd,khd->hqk", query_block, head_keys, preferred_element_type=jnp.float32
    ) * HEAD_DIM ** (-0.5)
    row_places = block_index * block_rows + jnp.arange(block_rows, dtype=jnp.int32)
    allowed = positions[None, :] <= row_places[:, None]
    return jnp.where(allowed[None], scores, -1e30)


def attend_forward(queries, key_rows, values):
    length = queries.shape[0]
    local_heads = queries.shape[1] // HEAD_DIM
    block_rows = min(512, length)
    num_blocks = length // block_rows
    head_queries = queries.reshape(num_blocks, block_rows, local_heads, HEAD_DIM)
    head_keys = key_rows.reshape(length, local_heads, HEAD_DIM)
    head_values = values.reshape(length, local_heads, HEAD_DIM)
    positions = jnp.arange(length, dtype=jnp.int32)

    def one_block(state_carry, block_item):
        query_block, block_index = block_item
        scores = masked_scores(query_block, head_keys, block_index, block_rows, positions)
        row_max = jnp.max(scores, axis=-1, keepdims=True)
        exp_scores = jnp.exp(scores - row_max)
        row_sum = jnp.sum(exp_scores, axis=-1, keepdims=True)
        weights = (exp_scores / row_sum).astype(jnp.bfloat16)
        block_out = jnp.einsum(
            "hqk,khd->qhd", weights, head_values, preferred_element_type=jnp.float32
        )
        return (state_carry, (block_out.astype(jnp.bfloat16), (row_max + jnp.log(row_sum))[..., 0]))

    _, (block_outs, log_sums) = lax.scan(
        one_block, 0, (head_queries, jnp.arange(num_blocks, dtype=jnp.int32))
    )
    return (block_outs.reshape(length, local_heads * HEAD_DIM), log_sums)


def attend_backward(queries, key_rows, values, log_sums, grad_heads):
    length = queries.shape[0]
    local_heads = queries.shape[1] // HEAD_DIM
    block_rows = min(512, length)
    num_blocks = length // block_rows
    score_scale = HEAD_DIM ** (-0.5)
    head_queries = queries.reshape(num_blocks, block_rows, local_heads, HEAD_DIM)
    grad_blocks = grad_heads.reshape(num_blocks, block_rows, local_heads, HEAD_DIM)
    head_keys = key_rows.reshape(length, local_heads, HEAD_DIM)
    head_values = values.reshape(length, local_heads, HEAD_DIM)
    positions = jnp.arange(length, dtype=jnp.int32)
    zero_sum = jnp.zeros((length, local_heads, HEAD_DIM), jnp.float32)

    def one_block(state_carry, block_item):
        key_total, value_total = state_carry
        query_block, grad_block, block_logs, block_index = block_item
        scores = masked_scores(query_block, head_keys, block_index, block_rows, positions)
        probs = jnp.exp(scores - block_logs[..., None])
        grad_probs = jnp.einsum(
            "qhd,khd->hqk", grad_block, head_values, preferred_element_type=jnp.float32
        )
        row_dot = jnp.sum(probs * grad_probs, axis=-1, keepdims=True)
        grad_scores = (probs * (grad_probs - row_dot)).astype(jnp.bfloat16)
        grad_query = (
            jnp.einsum("hqk,khd->qhd", grad_scores, head_keys, preferred_element_type=jnp.float32)
            * score_scale
        )
        key_total = (
            key_total
            + jnp.einsum(
                "hqk,qhd->khd", grad_scores, query_block, preferred_element_type=jnp.float32
            )
            * score_scale
        )
        value_total = value_total + jnp.einsum(
            "hqk,qhd->khd",
            probs.astype(jnp.bfloat16),
            grad_block,
            preferred_element_type=jnp.float32,
        )
        return ((key_total, value_total), grad_query.astype(jnp.bfloat16))

    (key_total, value_total), grad_query = lax.scan(
        one_block,
        (zero_sum, zero_sum),
        (head_queries, grad_blocks, log_sums, jnp.arange(num_blocks, dtype=jnp.int32)),
    )
    width = local_heads * HEAD_DIM
    return (
        grad_query.reshape(length, width),
        key_total.reshape(length, width).astype(jnp.bfloat16),
        value_total.reshape(length, width).astype(jnp.bfloat16),
    )


def shards(
    tokens, ln_gain, ln_bias, w_qkv, qv_bias, w_out, w_fc, fc_bias, w_proj, branch_bias, cotangent
):
    (
        full_gain,
        full_shift,
        full_qkv,
        full_qv,
        full_out,
        full_fc,
        full_fcb,
        full_proj,
        full_branch,
    ) = (
        lax.all_gather(ln_gain, "dp", axis=1, tiled=True),
        lax.all_gather(ln_bias, "dp", axis=1, tiled=True),
        lax.all_gather(w_qkv, "dp", axis=0, tiled=True),
        lax.all_gather(qv_bias, "dp", axis=1, tiled=True),
        lax.all_gather(w_out, "dp", axis=0, tiled=True),
        lax.all_gather(w_fc, "dp", axis=0, tiled=True),
        lax.all_gather(fc_bias, "dp", axis=0, tiled=True),
        lax.all_gather(w_proj, "dp", axis=0, tiled=True),
        lax.all_gather(branch_bias, "dp", axis=1, tiled=True),
    )
    gain_vals = full_gain.astype(jnp.float32)
    shift_vals = full_shift.astype(jnp.float32)
    qv_vals = full_qv.astype(jnp.float32)
    branch_vals = full_branch.astype(jnp.float32)
    source = tokens[0].astype(jnp.float32)
    width = source.shape[1]
    normed_first = layer_norm(source, gain_vals[0], shift_vals[0]).astype(jnp.bfloat16)
    projected = jnp.dot(normed_first, full_qkv, preferred_element_type=jnp.float32)
    queries = (projected[:, :width] + qv_vals[0]).astype(jnp.bfloat16)
    key_rows = projected[:, width : 2 * width].astype(jnp.bfloat16)
    values = (projected[:, 2 * width :] + qv_vals[1]).astype(jnp.bfloat16)
    seq_queries, seq_keys, seq_values = (
        lax.all_to_all(queries, "seq", split_axis=1, concat_axis=0, tiled=True),
        lax.all_to_all(key_rows, "seq", split_axis=1, concat_axis=0, tiled=True),
        lax.all_to_all(values, "seq", split_axis=1, concat_axis=0, tiled=True),
    )
    seq_heads, log_sums = attend_forward(seq_queries, seq_keys, seq_values)
    head_out = lax.all_to_all(seq_heads, "seq", split_axis=0, concat_axis=1, tiled=True)
    middle = source + (
        jnp.dot(head_out, full_out, preferred_element_type=jnp.float32) + branch_vals[0]
    )
    second = layer_norm(middle, gain_vals[1], shift_vals[1]).astype(jnp.bfloat16)
    hidden = jnp.dot(second, full_fc, preferred_element_type=jnp.float32) + full_fcb.astype(
        jnp.float32
    )
    active = jax.nn.gelu(hidden, approximate=True).astype(jnp.bfloat16)
    result = middle + (
        jnp.dot(active, full_proj, preferred_element_type=jnp.float32) + branch_vals[1]
    )
    back_gain, back_qkv, back_out, back_fc, back_proj = (
        lax.all_gather(ln_gain, "dp", axis=1, tiled=True),
        lax.all_gather(w_qkv, "dp", axis=0, tiled=True),
        lax.all_gather(w_out, "dp", axis=0, tiled=True),
        lax.all_gather(w_fc, "dp", axis=0, tiled=True),
        lax.all_gather(w_proj, "dp", axis=0, tiled=True),
    )
    back_gain_vals = back_gain.astype(jnp.float32)
    upstream = cotangent[0]
    upstream_vals = upstream.astype(jnp.float32)
    grad_proj_bias = jnp.sum(upstream_vals, axis=0)
    grad_proj = jnp.einsum("tf,td->fd", active, upstream, preferred_element_type=jnp.float32)
    grad_active = jnp.einsum("td,fd->tf", upstream, back_proj, preferred_element_type=jnp.float32)
    _, gelu_back = jax.vjp(partial(jax.nn.gelu, approximate=True), hidden)
    grad_hidden = gelu_back(grad_active)[0].astype(jnp.bfloat16)
    grad_fc_bias = jnp.sum(grad_hidden.astype(jnp.float32), axis=0)
    grad_fc = jnp.einsum("td,tf->df", second, grad_hidden, preferred_element_type=jnp.float32)
    grad_second = jnp.einsum("tf,df->td", grad_hidden, back_fc, preferred_element_type=jnp.float32)
    _, second_back = jax.vjp(layer_norm, middle, back_gain_vals[1], shift_vals[1])
    middle_part, grad_gain_two, grad_shift_two = second_back(grad_second)
    grad_middle = upstream_vals + middle_part
    grad_branch = grad_middle.astype(jnp.bfloat16)
    grad_out_bias = jnp.sum(grad_branch.astype(jnp.float32), axis=0)
    grad_out = jnp.einsum("te,td->ed", head_out, grad_branch, preferred_element_type=jnp.float32)
    grad_head_out = jnp.einsum(
        "td,ed->te", grad_branch, back_out, preferred_element_type=jnp.float32
    ).astype(jnp.bfloat16)
    seq_grad_heads = lax.all_to_all(grad_head_out, "seq", split_axis=1, concat_axis=0, tiled=True)
    seq_grad_q, seq_grad_k, seq_grad_v = attend_backward(
        seq_queries, seq_keys, seq_values, log_sums, seq_grad_heads
    )
    grad_query, grad_keys, grad_values = (
        lax.all_to_all(seq_grad_q, "seq", split_axis=0, concat_axis=1, tiled=True),
        lax.all_to_all(seq_grad_k, "seq", split_axis=0, concat_axis=1, tiled=True),
        lax.all_to_all(seq_grad_v, "seq", split_axis=0, concat_axis=1, tiled=True),
    )
    grad_qv = jnp.stack(
        [
            jnp.sum(grad_query.astype(jnp.float32), axis=0),
            jnp.sum(grad_values.astype(jnp.float32), axis=0),
        ]
    )
    grad_projected = jnp.concatenate([grad_query, grad_keys, grad_values], axis=1)
    grad_qkv = jnp.einsum(
        "td,te->de", normed_first, grad_projected, preferred_element_type=jnp.float32
    )
    grad_first = jnp.einsum(
        "te,de->td", grad_projected, back_qkv, preferred_element_type=jnp.float32
    )
    _, first_back = jax.vjp(layer_norm, source, back_gain_vals[0], shift_vals[0])
    source_part, grad_gain_one, grad_shift_one = first_back(grad_first)
    input_grad = (grad_middle + source_part).astype(jnp.bfloat16)
    local_grads = (
        jnp.stack([grad_gain_one, grad_gain_two]),
        jnp.stack([grad_shift_one, grad_shift_two]),
        grad_qkv,
        grad_qv,
        grad_out,
        grad_fc,
        grad_fc_bias,
        grad_proj,
        jnp.stack([grad_out_bias, grad_proj_bias]),
    )
    owned = (
        lax.psum_scatter(local_grads[0], "dp", scatter_dimension=1, tiled=True),
        lax.psum_scatter(local_grads[1], "dp", scatter_dimension=1, tiled=True),
        lax.psum_scatter(local_grads[2], "dp", scatter_dimension=0, tiled=True),
        lax.psum_scatter(local_grads[3], "dp", scatter_dimension=1, tiled=True),
        lax.psum_scatter(local_grads[4], "dp", scatter_dimension=0, tiled=True),
        lax.psum_scatter(local_grads[5], "dp", scatter_dimension=0, tiled=True),
        lax.psum_scatter(local_grads[6], "dp", scatter_dimension=0, tiled=True),
        lax.psum_scatter(local_grads[7], "dp", scatter_dimension=0, tiled=True),
        lax.psum_scatter(local_grads[8], "dp", scatter_dimension=1, tiled=True),
    )
    summed = (
        lax.psum(owned[0].astype(jnp.bfloat16), "seq").astype(jnp.float32),
        lax.psum(owned[1].astype(jnp.bfloat16), "seq").astype(jnp.float32),
        lax.psum(owned[2].astype(jnp.bfloat16), "seq").astype(jnp.float32),
        lax.psum(owned[3].astype(jnp.bfloat16), "seq").astype(jnp.float32),
        lax.psum(owned[4].astype(jnp.bfloat16), "seq").astype(jnp.float32),
        lax.psum(owned[5].astype(jnp.bfloat16), "seq").astype(jnp.float32),
        lax.psum(owned[6].astype(jnp.bfloat16), "seq").astype(jnp.float32),
        lax.psum(owned[7].astype(jnp.bfloat16), "seq").astype(jnp.float32),
        lax.psum(owned[8].astype(jnp.bfloat16), "seq").astype(jnp.float32),
    )
    return (
        result.astype(jnp.bfloat16)[None],
        input_grad[None],
        summed[0],
        summed[1],
        summed[2],
        summed[3],
        summed[4],
        summed[5],
        summed[6],
        summed[7],
        summed[8],
    )


def solution(mesh):
    placed = (
        P("dp", "seq", None),
        P(None, "dp"),
        P(None, "dp"),
        P("dp", None),
        P(None, "dp"),
        P("dp", None),
        P("dp", None),
        P("dp"),
        P("dp", None),
        P(None, "dp"),
        P("dp", "seq", None),
    )
    return jax.shard_map(
        shards,
        mesh=mesh,
        in_specs=placed,
        out_specs=(
            P("dp", "seq", None),
            P("dp", "seq", None),
            P(None, "dp"),
            P(None, "dp"),
            P("dp", None),
            P(None, "dp"),
            P("dp", None),
            P("dp", None),
            P("dp"),
            P("dp", None),
            P(None, "dp"),
        ),
        check_vma=False,
    )
```

profile of v0, /device:TPU:0, one launch (start us, length us, event | category | flops | bytes accessed | tf_op | source)
XLA Modules:
  0.0 934.1 jit_solution(18162046185638918517)
XLA Ops:
  9.4 13.5 %all-gather = bf16[8,96,2]{1,2,0:T(2,128)(2,1)S(1)} all-gather(bf16[1,96,2]{1,2,0:T(2,128)(2,1)} %bitcast.254), channel_id=1, replica_groups=mesh['seq'=4,'dp'=8] {'dp'}, dimensions={0}, use_global_device_ids=true | all-gather | bytes 3456 | tf_op jit(solution)/shard_map/all_gather | solution.py:126
  23.0 9.1 all-gather.1
  32.2 10.1 %all-gather.2 = bf16[8,96,2]{1,2,0:T(2,128)(2,1)S(1)} all-gather(bf16[1,96,2]{1,2,0:T(2,128)(2,1)} %bitcast.256), channel_id=1, replica_groups=mesh['seq'=4,'dp'=8] {'dp'}, dimensions={0}, use_global_device_ids=true | all-gather | bytes 3456 | tf_op jit(solution)/shard_map/all_gather | solution.py:129
  46.3 7.7 all-gather.10.cloned.1.call-done
  54.0 4.4 fusion.85
  68.8 7.9 all-to-all-done.1
  81.4 9.3 all-to-all-done.2
  99.6 5.0 all-to-all-done
  105.5 89.0 %while.28 = (s32[]{:T(128)}, bf16[4,512,3,64]{1,3,2,0:T(8,128)(2,1)}, f32[4,3,512]{2,1,0:T(4,128)S(1)}, s32[4]{0:T(128)S(1)}, bf16[4,512,3,64]{1,3,2,0:T(8,128)(...) while((s32[]{:T(128)}, ...), condition=%wide.region_5.6_spmd.clone, body=%wide.region_2.5_spmd.clone.sunk | while | flops 844200960 | bytes 43968652 | solution.py:51
  107.4 6.1 fusion.136
  113.5 6.9 fusion.137
  120.4 7.3 fusion.138
  129.7 6.0 fusion.136
  135.7 7.1 fusion.137
  142.7 7.4 fusion.138
  152.0 6.1 fusion.136
  158.2 6.9 fusion.137
  165.0 7.4 fusion.138
  174.4 6.1 fusion.136
  180.4 6.8 fusion.137
  187.2 7.3 fusion.138
  194.5 4.2 all-to-all-start.3
  198.8 9.8 %all-gather.3 = bf16[8,96,2]{1,2,0:T(2,128)(2,1)S(1)} all-gather(bf16[1,96,2]{1,2,0:T(2,128)(2,1)S(1)} %bitcast.257), channel_id=1, replica_groups=mesh['seq'=4,'dp'=8] {'dp'}, dimensions={0}, use_global_device_ids=true | all-gather | bytes 3456 | tf_op jit(solution)/shard_map/all_gather | solution.py:134
  208.7 13.0 %all-gather.4 = bf16[8,1,384]{2,1,0:T(2,128)(2,1)S(1)} all-gather(bf16[1,1,384]{2,1,0:T(2,128)(2,1)S(1)} %reshape.259), channel_id=1, replica_groups=mesh['seq'=4,'dp'=8] {'dp'}, dimensions={0}, use_global_device_ids=true | all-gather | bytes 6912 | tf_op jit(solution)/shard_map/all_gather | solution.py:132
  226.3 8.3 fusion.89
  234.6 9.8 %convert_reduce_fusion = (f32[3072]{0:T(1024)}, bf16[512,3072]{1,0:T(8,128)(2,1)S(1)}) fusion(f32[512,3072]{1,0:T(8,128)} %fusion.89, f32[3072]{0:T(1024)S(1)} %bitcast.251, bf16[3072,768]{1,0:T(8,128)(2,1)} %all-gather.16.cloned.1.call-done, bf16[1,512,768]{2,1,0:T(8,128)(2,1)S(1)} %copy-done.18), kind=kOutput, calls=%fused_computation.63 | convolution fusion | flops 2452091904 | bytes 14966784 | tf_op jit(solution)/shard_map/td,fd->tf/dot_general | solution.py:177
  253.5 4.1 all-to-all-start.4
  261.2 7.8 all-to-all-done.4
  269.9 134.4 %while.29 = (s32[]{:T(128)}, f32[2048,3,64]{0,2,1:T(8,128)}, f32[2048,3,64]{0,2,1:T(8,128)}, bf16[4,512,3,64]{1,3,2,0:T(8,128)(2,1)}, bf16[4,512,3,64]{1,3,2,0:T...) while((s32[]{:T(128)}, f32[2048,3,64]{0,2,1:T(8,128)}, ...), condition=%wide.region_12.13_spmd.clone, body=%wide.region_10.12_spmd.clone.sunk | while | flops 2063662080 | bytes 162775504 | solution.py:99
  283.5 4.7 fusion.150
  288.2 5.8 multiply_reduce_fusion.5
  294.0 6.1 multiply_convert_fusion.5
  300.1 5.8 fusion.151
  312.4 6.1 fusion.150
  318.6 5.8 multiply_reduce_fusion.5
  324.3 6.1 multiply_convert_fusion.5
  330.4 5.8 fusion.151
  336.3 4.0 fusion.149
  344.4 6.1 fusion.150
  350.5 5.8 multiply_reduce_fusion.5
  356.2 6.1 multiply_convert_fusion.5
  362.4 5.8 fusion.151
  376.3 6.1 fusion.150
  382.4 5.8 multiply_reduce_fusion.5
  388.1 6.1 multiply_convert_fusion.5
  394.3 5.8 fusion.151
  411.0 7.3 all-to-all-done.5
  418.3 4.2 all-to-all-start.6
  424.9 7.9 all-to-all-done.6
  432.8 13.2 %all_to_all.134 = bf16[4,512,192]{1,2,0:T(8,128)(2,1)S(1)} all-to-all(bf16[4,512,192]{1,2,0:T(8,128)(2,1)S(1)} %copy.84), channel_id=1, replica_groups=mesh['seq'=4,'dp'=8] {'seq'}, dimensions={0} | all-to-all | bytes 1572864 | tf_op jit(solution)/shard_map/all_to_all | solution.py:199
  446.9 6.4 fusion.71
  454.4 10.7 %fusion.74 = f32[3072,768]{1,0:T(8,128)} fusion(bf16[1,512,768]{2,1,0:T(8,128)(2,1)S(1)} %copy-done.19, f32[512,3072]{1,0:T(8,128)} %fusion.89, f32[3072]{0:T(1024)S(1)} %bitcast.252), kind=kOutput, calls=%fused_computation.105 | convolution fusion | flops 2431647744 | bytes 16527360 | tf_op jit(solution)/shard_map/tf,td->fd/dot_general | solution.py:176
  466.6 7.2 fusion.88
  474.5 5.1 fusion.90
  491.5 36.2 %reduce-scatter.17.cloned.1.call-done = f32[96,2304]{1,0:T(8,128)} async-done(((f32[768,2304]{1,0:T(8,128)}), f32[96,2304]{1,0:T(8,128)}) %reduce-scatter.17.cloned.1.call-update) | async-done | bytes 884752 | tf_op jit(solution)/shard_map/reduce_scatter | solution.py:231
  529.7 98.2 %reduce-scatter.23.cloned.1.call-done = f32[384,768]{1,0:T(8,128)} async-done(((f32[3072,768]{1,0:T(8,128)}), f32[384,768]{1,0:T(8,128)}) %reduce-scatter.23.cloned.1.call-update) | async-done | bytes 1179664 | tf_op jit(solution)/shard_map/reduce_scatter | solution.py:236
  630.0 98.1 %reduce-scatter.21.cloned.1.call-done = f32[96,3072]{1,0:T(8,128)} async-done(((f32[768,3072]{1,0:T(8,128)}), f32[96,3072]{1,0:T(8,128)}) %reduce-scatter.21.cloned.1.call-update) | async-done | bytes 1179664 | tf_op jit(solution)/shard_map/reduce_scatter | solution.py:234
  731.5 26.0 %all-reduce = bf16[3072]{0:T(1024)(128)(2,1)S(1)} all-reduce(f32[3072]{0:T(1024)S(1)} %copy-done.41), channel_id=8, replica_groups=mesh['seq'=4,'dp'=8] {'dp'}, use_global_device_ids=true, to_apply=%region_34.35.clone | all-reduce | flops 3072 | bytes 18432
  757.6 9.0 fusion.69
  767.5 22.9 %reduce-scatter.25.cloned.1.call-done = f32[96,2]{1,0:T(8,128)} async-done(((f32[768,2]{1,0:T(8,128)}), f32[96,2]{1,0:T(8,128)}) %reduce-scatter.25.cloned.1.call-update) | async-done | bytes 784
  791.3 30.3 %reduce-scatter.29.cloned.1.call-done = f32[96,2]{1,0:T(8,128)} async-done(((f32[768,2]{1,0:T(8,128)}), f32[96,2]{1,0:T(8,128)}) %reduce-scatter.29.cloned.1.call-update) | async-done | bytes 784
  822.5 30.2 %reduce-scatter.27.cloned.1.call-done = f32[96,2]{1,0:T(8,128)} async-done(((f32[768,2]{1,0:T(8,128)}), f32[96,2]{1,0:T(8,128)}) %reduce-scatter.27.cloned.1.call-update) | async-done | bytes 784
  853.5 9.9 %all-reduce.1 = (bf16[2,96]{1,0:T(2,128)(2,1)S(1)}, bf16[2,96]{1,0:T(2,128)(2,1)S(1)}, bf16[2,96]{1,0:T(2,128)(2,1)S(1)}, bf16[384]{0:T(512)(128)(2,1)S(1)}, bf16[2,96]{1,0:T(2,128)(2,1)S(1)}) all-reduce(bf16[2,96]{1,0:T(2,128)(2,1)S(1)} %copy.88, bf16[2,96]{1,0:T(2,128)(2,1)S(1)} %copy.90, ...), channel_id=1, replica_groups=mesh['seq'=4,'dp'=8] {'seq'}, use_global_device_ids=true, to_apply=%region_18.19 | all-reduce | flops 1152 | bytes 4608 | tf_op jit(solution)/shard_map/psum | solution.py:240
  866.3 53.9 %all-reduce.5.cloned.1.call-done = (bf16[96,2304]{1,0:T(8,128)(2,1)}, bf16[96,768]{1,0:T(8,128)(2,1)}, bf16[96,3072]{1,0:T(8,128)(2,1)}, bf16[384,768]{1,0:T(8,128)(2,1)}) async-done(((bf16[96,2304]{1,0:T(8,128)(2,1)}, bf16[96,768]{1,0:T(8,128)(2,1)}, bf16[96,3072]{1,0:T(8,128)(2,1)}, bf16[384,768]{1,0:T(8,128)(2,1)}), (bf16[96,2304]{1,0:T(8,128)(2,1)}, bf16[96,768]{1,0:T(8,128)(2,1)}, ...) | async-done | bytes 1769488 | tf_op jit(solution)/shard_map/psum | solution.py:242
  (341 shorter events, 123.1 us)
Async XLA Ops:
  7.2 46.8 %all-gather.10.cloned.1.call-start = ((), (), s32[]{:S(2)}) async-start(), calls=%async_computation.16 | async-start | bytes 3981312 | tf_op jit(solution)/shard_map/all_gather | solution.py:128
  7.9 214.4 %all-gather.12.cloned.1.call-start = ((), (), s32[]{:S(2)}) async-start(), calls=%async_computation.17 | async-start | bytes 1327104 | tf_op jit(solution)/shard_map/all_gather | solution.py:130
  8.7 217.6 %all-gather.14.cloned.1.call-start = ((), (), s32[]{:S(2)}) async-start(), calls=%async_computation.18 | async-start | bytes 5308416 | tf_op jit(solution)/shard_map/all_gather | solution.py:131
  42.9 11.1 %copy-start.24 = (f32[768]{0:T(1024)}, f32[768]{0:T(1024)S(1)}, u32[]{:S(2)}) copy-start(f32[768]{0:T(1024)S(1)} %get-tuple-element.245) | copy-start | bytes 9220
  42.9 11.1 %copy-start.47 = (f32[768]{0:T(1024)}, f32[768]{0:T(1024)S(1)}, u32[]{:S(2)}) copy-start(f32[768]{0:T(1024)S(1)} %get-tuple-element.179) | copy-start | bytes 9220
  44.2 9.8 %copy-start.26 = (f32[512]{0:T(512)}, f32[512]{0:T(512)S(1)}, u32[]{:S(2)}) copy-start(f32[512]{0:T(512)S(1)} %broadcast_multiply_fusion.1) | copy-start | bytes 6148
  46.3 7.7 copy-start.28
  61.8 15.0 %all-to-all-start.1 = ((bf16[512,4,192]{0,2,1:T(8,128)(2,1)}), bf16[512,4,192]{0,2,1:T(8,128)(2,1)S(1)}, u32[]{:S(2)}, u32[]{:S(2)}) async-start(bf16[512,4,192]{0,2,1:T(8,128)(2,1)} %bitcast.13), calls=%async_computation.1 | async-start | bytes 1572864 | tf_op jit(solution)/shard_map/all_to_all | solution.py:149
  76.7 14.0 %all-to-all-start.2 = ((bf16[512,4,192]{0,2,1:T(8,128)(2,1)}), bf16[512,4,192]{0,2,1:T(8,128)(2,1)S(1)}, u32[]{:S(2)}, u32[]{:S(2)}) async-start(bf16[512,4,192]{0,2,1:T(8,128)(2,1)} %bitcast.15), calls=%async_computation.2 | async-start | bytes 1572864 | tf_op jit(solution)/shard_map/all_to_all | solution.py:150
  90.7 13.8 %all-to-all-start = ((bf16[512,4,192]{0,2,1:T(8,128)(2,1)}), bf16[512,4,192]{0,2,1:T(8,128)(2,1)S(1)}, u32[]{:S(2)}, u32[]{:S(2)}) async-start(bf16[512,4,192]{0,2,1:T(8,128)(2,1)} %bitcast.235), calls=%async_computation | async-start | bytes 1572864 | tf_op jit(solution)/shard_map/all_to_all | solution.py:148
  94.2 140.4 %all-gather.16.cloned.1.call-start = ((), (), s32[]{:S(2)}) async-start(), calls=%async_computation.19 | async-start | bytes 5308416 | tf_op jit(solution)/shard_map/all_gather | solution.py:133
  105.5 93.3 %copy-start.51 = (bf16[384]{0:T(512)(128)(2,1)S(1)}, bf16[384]{0:T(512)(128)(2,1)}, u32[]{:S(2)}) copy-start(bf16[384]{0:T(512)(128)(2,1)} %param.22) | copy-start | bytes 2308
  105.5 93.3 %copy-start.52 = (bf16[2,96]{1,0:T(2,128)(2,1)S(1)}, bf16[2,96]{1,0:T(2,128)(2,1)}, u32[]{:S(2)}) copy-start(bf16[2,96]{1,0:T(2,128)(2,1)} %param.24) | copy-start | bytes 1156
  105.5 116.8 %copy-start.8 = (bf16[1,512,768]{2,1,0:T(8,128)(2,1)S(1)}, bf16[1,512,768]{2,1,0:T(8,128)(2,1)}, u32[]{:S(2)}) copy-start(bf16[1,512,768]{2,1,0:T(8,128)(2,1)} %param.15) | copy-start | bytes 2359300
  194.5 27.7 %all-to-all-start.3 = ((bf16[4,512,192]{1,2,0:T(8,128)(2,1)}), bf16[4,512,192]{1,2,0:T(8,128)(2,1)}, u32[]{:S(2)}, u32[]{:S(2)}) async-start(bf16[4,512,192]{1,2,0:T(8,128)(2,1)} %bitcast.238), calls=%async_computation.3 | async-start | bytes 1572864 | tf_op jit(solution)/shard_map/all_to_all | solution.py:153
  221.7 12.9 %copy-start.39 = (f32[8,1,384]{2,1,0:T(1,128)}, f32[8,1,384]{2,1,0:T(1,128)S(1)}, u32[]{:S(2)}) copy-start(f32[8,1,384]{2,1,0:T(1,128)S(1)} %convert_element_type.207) | copy-start | bytes 36868
  224.8 23.1 %copy-start.32 = (f32[512]{0:T(512)}, f32[512]{0:T(512)S(1)}, u32[]{:S(2)}) copy-start(f32[512]{0:T(512)S(1)} %broadcast_multiply_fusion) | copy-start | bytes 6148
  226.2 21.7 %copy-start.42 = (f32[512]{0:T(512)}, f32[512]{0:T(512)S(1)}, u32[]{:S(2)}) copy-start(f32[512]{0:T(512)S(1)} %fusion.81) | copy-start | bytes 6148
  226.3 8.3 copy-start.18
  234.6 9.8 %copy-start.13 = (f32[512,768]{1,0:T(8,128)S(1)}, f32[512,768]{1,0:T(8,128)}, u32[]{:S(2)}) copy-start(f32[512,768]{1,0:T(8,128)} %copy-done.12) | copy-start | bytes 4718596
  234.6 9.8 %copy-start.53 = (bf16[768,3072]{1,0:T(8,128)(2,1)S(1)}, bf16[768,3072]{1,0:T(8,128)(2,1)}, u32[]{:S(2)}) copy-start(bf16[768,3072]{1,0:T(8,128)(2,1)} %all-gather.14.cloned.1.call-done) | copy-start | bytes 14155780
  253.5 15.4 %all-to-all-start.4 = ((bf16[512,4,192]{0,2,1:T(8,128)(2,1)}), bf16[512,4,192]{0,2,1:T(8,128)(2,1)S(1)}, u32[]{:S(2)}, u32[]{:S(2)}) async-start(bf16[512,4,192]{0,2,1:T(8,128)(2,1)} %bitcast.236), calls=%async_computation.4 | async-start | bytes 1572864 | tf_op jit(solution)/shard_map/all_to_all | solution.py:192
  257.7 232.2 %reduce-scatter.19.cloned.1.call-start = ((), (), s32[]{:S(2)}) async-start(), calls=%async_computation.21 | async-start | bytes 2654208 | tf_op jit(solution)/shard_map/reduce_scatter | solution.py:233
  279.4 4.0 copy-start.2
  279.4 4.0 copy-start.4
  300.1 5.8 copy-start
  300.1 5.8 copy-start.11
  330.4 5.8 copy-start
  330.4 5.8 copy-start.11
  336.2 4.1 copy-start.3
  336.2 4.1 copy-start.5
  336.3 4.0 copy-start.16
  362.4 5.8 copy-start
  362.4 5.8 copy-start.11
  368.2 4.1 copy-start.3
  368.2 4.1 copy-start.5
  368.2 4.0 copy-start.16
  394.3 5.8 copy-start
  394.3 5.8 copy-start.11
  400.1 4.1 copy-start.3
  400.1 4.1 copy-start.5
  400.1 4.0 copy-start.16
  404.4 13.9 %all-to-all-start.5 = ((bf16[4,512,192]{1,2,0:T(8,128)(2,1)}), bf16[4,512,192]{1,2,0:T(8,128)(2,1)S(1)}, u32[]{:S(2)}, u32[]{:S(2)}) async-start(bf16[4,512,192]{1,2,0:T(8,128)(2,1)} %bitcast.237), calls=%async_computation.5 | async-start | bytes 1572864 | tf_op jit(solution)/shard_map/all_to_all | solution.py:197
  418.3 27.7 %copy-start.20 = (bf16[4,512,192]{1,2,0:T(8,128)(2,1)}, bf16[4,512,192]{1,2,0:T(8,128)(2,1)S(1)}, u32[]{:S(2)}) copy-start(bf16[4,512,192]{1,2,0:T(8,128)(2,1)S(1)} %all-to-all-done.5) | copy-start | bytes 2359300
  418.3 14.6 %all-to-all-start.6 = ((bf16[4,512,192]{1,2,0:T(8,128)(2,1)}), bf16[4,512,192]{1,2,0:T(8,128)(2,1)}, u32[]{:S(2)}, u32[]{:S(2)}) async-start(bf16[4,512,192]{1,2,0:T(8,128)(2,1)} %copy.83), calls=%async_computation.6 | async-start | bytes 1572864 | tf_op jit(solution)/shard_map/all_to_all | solution.py:198
  422.5 105.2 %reduce-scatter.17.cloned.1.call-start = ((), (), s32[]{:S(2)}) async-start(), calls=%async_computation.20 | async-start | bytes 7962624 | tf_op jit(solution)/shard_map/reduce_scatter | solution.py:231
  422.6 24.3 %copy-start.9 = (bf16[1,512,768]{2,1,0:T(8,128)(2,1)S(1)}, bf16[1,512,768]{2,1,0:T(8,128)(2,1)}, u32[]{:S(2)}) copy-start(bf16[1,512,768]{2,1,0:T(8,128)(2,1)} %param.15) | copy-start | bytes 2359300
  422.6 24.3 %copy-start.25 = (f32[768]{0:T(1024)S(1)}, f32[768]{0:T(1024)}, u32[]{:S(2)}) copy-start(f32[768]{0:T(1024)} %copy-done.24) | copy-start | bytes 9220
  422.6 24.3 %copy-start.27 = (f32[512]{0:T(512)S(1)}, f32[512]{0:T(512)}, u32[]{:S(2)}) copy-start(f32[512]{0:T(512)} %copy-done.26) | copy-start | bytes 6148
  422.6 24.3 %copy-start.29 = (f32[512]{0:T(512)S(1)}, f32[512]{0:T(512)}, u32[]{:S(2)}) copy-start(f32[512]{0:T(512)} %copy-done.28) | copy-start | bytes 6148
  422.6 24.3 %copy-start.48 = (f32[768]{0:T(1024)S(1)}, f32[768]{0:T(1024)}, u32[]{:S(2)}) copy-start(f32[768]{0:T(1024)} %copy-done.47) | copy-start | bytes 9220
  453.3 174.6 %reduce-scatter.23.cloned.1.call-start = ((), (), s32[]{:S(2)}) async-start(), calls=%async_computation.23 | async-start | bytes 10616832 | tf_op jit(solution)/shard_map/reduce_scatter | solution.py:236
  465.2 262.9 %reduce-scatter.21.cloned.1.call-start = ((), (), s32[]{:S(2)}) async-start(), calls=%async_computation.22 | async-start | bytes 10616832 | tf_op jit(solution)/shard_map/reduce_scatter | solution.py:234
  473.8 292.8 %reduce-scatter.31.cloned.1.call-start = ((), (), s32[]{:S(2)}) async-start(), calls=%async_computation.27 | async-start | bytes 442368
  474.5 5.2 copy-start.35
  474.5 6.0 copy-start.31
  483.8 306.7 %reduce-scatter.25.cloned.1.call-start = ((), (), s32[]{:S(2)}) async-start(), calls=%async_computation.24 | async-start | bytes 442368
  487.7 333.9 %reduce-scatter.29.cloned.1.call-start = ((), (), s32[]{:S(2)}) async-start(), calls=%async_computation.26 | async-start | bytes 442368
  488.7 363.9 %reduce-scatter.27.cloned.1.call-start = ((), (), s32[]{:S(2)}) async-start(), calls=%async_computation.25 | async-start | bytes 442368
  489.8 430.4 %all-reduce.5.cloned.1.call-start = ((), (), s32[]{:S(2)}) async-start(), calls=%async_computation.28 | async-start | bytes 3538944 | tf_op jit(solution)/shard_map/psum | solution.py:242
  491.5 238.8 %copy-start.55 = (u32[32]{0:T(128)S(1)}, u32[32]{0:T(128)}, u32[]{:S(2)}) copy-start(u32[32]{0:T(128)} %constant.81) | copy-start | bytes 388
  491.5 240.0 %copy-start.41 = (f32[3072]{0:T(1024)S(1)}, f32[3072]{0:T(1024)}, u32[]{:S(2)}) copy-start(f32[3072]{0:T(1024)} %get-tuple-element.243) | copy-start | bytes 36868
  491.5 266.1 %copy-start.44 = (f32[768]{0:T(1024)S(1)}, f32[768]{0:T(1024)}, u32[]{:S(2)}) copy-start(f32[768]{0:T(1024)} %get-tuple-element.180) | copy-start | bytes 9220
  920.2 5.9 copy-start.23
  (43 other events, 109.6 us)
Sparse Core Ops, SparseCore 0:
  9.7 44.2 all-gather.9
  55.6 21.5 all-gather.11
  78.8 51.4 all-gather.13
  131.8 50.5 all-gather.15
  261.3 35.2 reduce-scatter.18
  453.4 74.2 reduce-scatter.16
  530.0 97.8 reduce-scatter.22
  630.2 97.8 reduce-scatter.20
  730.4 29.1 reduce-scatter.30
  761.7 28.6 reduce-scatter.24
  792.7 28.8 reduce-scatter.28
  823.8 28.7 reduce-scatter.26
  857.2 62.9 all-reduce.4
where the time goes:
time: 940 us; the launch traced here: 934 us
  waiting for transfers between devices  425 us (45%)
  matrix products  216 us (23%)
  blocking collectives  105 us (11%)
  other arithmetic  90.3 us (10%)
  local copies, waits for them, and re-layouts  39.1 us (4%)
  starting transfers between devices  27.7 us (3%)
  loops' own time  15.8 us (2%)
  between operations  15.6 us (2%)
    reduce_scatter x1, waiting for transfers between devices, shards(): lax.psum_scatter(local_grads[7], 'dp', scatter_dimension=0, tiled=True)  98.2 us
    reduce_scatter x1, waiting for transfers between devices, shards(): lax.psum_scatter(local_grads[5], 'dp', scatter_dimension=0, tiled=True)  98.1 us
    unnamed x17, waiting for transfers between devices  85.9 us
    psum x1, waiting for transfers between devices, shards(): lax.psum(owned[2].astype(jnp.bfloat16), 'seq').astype(jnp.float32)  53.9 us
    reduce_scatter x1, waiting for transfers between devices, shards(): lax.psum_scatter(local_grads[2], 'dp', scatter_dimension=0, tiled=True)  36.2 us
    dot_general x8, matrix products, masked_scores(): jnp.einsum('qhd,khd->hqk', query_block, head_keys, preferred_element_type...  31.6 us
    dot_general x4, matrix products, one_block(): jnp.einsum('hqk,khd->qhd', weights, head_values, preferred_element_type=j...  29.4 us
    reduce_sum x4, other arithmetic, one_block(): row_sum = jnp.sum(exp_scores, axis=-1, keepdims=True)  27.6 us
  transfers between devices with their start and end apart: 20, of which 14 were waited for; matrix products, arithmetic and copies ran while one was open for 33% of the time, Pallas kernels for 0%

commit v1 on v0

v1 whole, which is shorter than its diff:
```python
from functools import partial

import jax
import jax.numpy as jnp
from jax import lax
from jax.experimental import pallas as pl
from jax.experimental.pallas import tpu as pltpu
from jax.sharding import PartitionSpec as P

HEAD_DIM = 64
NORM_EPS = 1e-05
F32 = jnp.float32
BF16 = jnp.bfloat16
SCALE = HEAD_DIM ** (-0.5)


def layer_norm(vector, norm_gain, norm_shift):
    center = vector - jnp.mean(vector, axis=-1, keepdims=True)
    spread = jnp.mean(center * center, axis=-1, keepdims=True)
    return center * lax.rsqrt(spread + NORM_EPS) * norm_gain + norm_shift


def dot(left, right, left_dim, right_dim):
    return lax.dot_general(
        left, right, (((left_dim,), (right_dim,)), ((), ())), preferred_element_type=F32
    )


def causal(scores):
    keys = lax.broadcasted_iota(jnp.int32, scores.shape, 0)
    rows = lax.broadcasted_iota(jnp.int32, scores.shape, 1)
    return jnp.where(keys <= rows, scores, -1e30)


def forward_kernel(blocks, qkv_ref, out_ref, log_ref):
    for i in range(blocks):
        queries = qkv_ref[0, i] * BF16(SCALE)
        scores = [dot(qkv_ref[1, j], queries, 0, 0) for j in range(i + 1)]
        scores[i] = causal(scores[i])
        top = jnp.max(scores[0], axis=0, keepdims=True)
        for piece in scores[1:]:
            top = jnp.maximum(top, jnp.max(piece, axis=0, keepdims=True))
        total = 0.0
        mixed = 0.0
        for j in range(i + 1):
            weights = jnp.exp(scores[j] - top)
            total = total + jnp.sum(weights, axis=0, keepdims=True)
            mixed = mixed + dot(qkv_ref[2, j], weights.astype(BF16), 1, 0)
        out_ref[i] = (mixed / total).astype(BF16)
        log_ref[0, i] = jnp.broadcast_to(top + jnp.log(total), log_ref.shape[2:])


def backward_kernel(blocks, qkv_ref, out_ref, log_ref, grad_ref, result_ref, key_ref, value_ref):
    for i in range(blocks):
        queries = qkv_ref[0, i] * BF16(SCALE)
        grads = grad_ref[i]
        logs = log_ref[0, i, 0:1]
        spread = jnp.sum(grads.astype(F32) * out_ref[i].astype(F32), axis=0, keepdims=True)
        query_total = 0.0
        for j in range(i + 1):
            keys = qkv_ref[1, j]
            scores = dot(keys, queries, 0, 0)
            if j == i:
                scores = causal(scores)
            probs = jnp.exp(scores - logs)
            grad_probs = dot(qkv_ref[2, j], grads, 0, 0)
            grad_scores = (probs * (grad_probs - spread)).astype(BF16)
            query_total = query_total + dot(keys, grad_scores, 1, 0)
            key_part = dot(queries, grad_scores, 1, 1)
            value_part = dot(grads, probs.astype(BF16), 1, 1)
            if i == j:
                key_ref[j] = key_part
                value_ref[j] = value_part
            else:
                key_ref[j] += key_part
                value_ref[j] += value_part
        result_ref[0, i] = (query_total * SCALE).astype(BF16)
    for j in range(blocks):
        result_ref[1, j] = key_ref[j].astype(BF16)
        result_ref[2, j] = value_ref[j].astype(BF16)


def specs(blocks, rows):
    return (
        pl.BlockSpec((3, blocks, HEAD_DIM, rows), lambda h: (0, 0, h, 0)),
        pl.BlockSpec((blocks, HEAD_DIM, rows), lambda h: (0, h, 0)),
        pl.BlockSpec((1, blocks, 8, rows), lambda h: (h, 0, 0, 0)),
    )


def attend_forward(qkv):
    _, blocks, width, rows = qkv.shape
    heads = width // HEAD_DIM
    wide, narrow, log_spec = specs(blocks, rows)
    pairs = heads * rows * rows * blocks * (blocks + 1) // 2
    return pl.pallas_call(
        partial(forward_kernel, blocks),
        grid=(heads,),
        in_specs=[wide],
        out_specs=[narrow, log_spec],
        out_shape=[
            jax.ShapeDtypeStruct((blocks, width, rows), BF16),
            jax.ShapeDtypeStruct((heads, blocks, 8, rows), F32),
        ],
        compiler_params=pltpu.CompilerParams(vmem_limit_bytes=40 * 2**20),
        cost_estimate=pl.CostEstimate(
            flops=16 * pairs * HEAD_DIM, bytes_accessed=2 * qkv.size * 2, transcendentals=pairs
        ),
        name="attend_forward",
    )(qkv)


def attend_backward(qkv, out, logs, grads):
    _, blocks, width, rows = qkv.shape
    heads = width // HEAD_DIM
    wide, narrow, log_spec = specs(blocks, rows)
    pairs = heads * rows * rows * blocks * (blocks + 1) // 2
    return pl.pallas_call(
        partial(backward_kernel, blocks),
        grid=(heads,),
        in_specs=[wide, narrow, log_spec, narrow],
        out_specs=wide,
        out_shape=jax.ShapeDtypeStruct(qkv.shape, BF16),
        scratch_shapes=[
            pltpu.VMEM((blocks, HEAD_DIM, rows), F32),
            pltpu.VMEM((blocks, HEAD_DIM, rows), F32),
        ],
        compiler_params=pltpu.CompilerParams(vmem_limit_bytes=40 * 2**20),
        cost_estimate=pl.CostEstimate(
            flops=40 * pairs * HEAD_DIM, bytes_accessed=6 * qkv.size * 2, transcendentals=pairs
        ),
        name="attend_backward",
    )(qkv, out, logs, grads)


def swap(value, axis, bit):
    size = lax.axis_size(axis)
    return lax.ppermute(value, axis, [(d, d ^ bit) for d in range(size)])


def halve(value, axis, bit):
    mine = (lax.axis_index(axis) // bit) % 2
    value = value.reshape((value.shape[0] // 2, 2) + value.shape[1:])
    kept = lax.dynamic_index_in_dim(value, mine, 1, keepdims=False)
    sent = lax.dynamic_index_in_dim(value, 1 - mine, 1, keepdims=False)
    return kept.astype(F32) + swap(sent.astype(BF16), axis, bit).astype(F32)


def reduce_owned(value):
    owners = lax.axis_size("dp")
    parts = lax.axis_size("seq")
    rows = value.shape[0] // owners
    value = value.reshape((owners, parts, rows // parts) + value.shape[1:])
    value = halve(value, "dp", 1)
    place = lax.axis_index("seq")
    total = lax.dynamic_index_in_dim(value, place, 1, keepdims=False)
    for other in range(1, parts):
        sent = lax.dynamic_index_in_dim(value, place ^ other, 1, keepdims=False)
        total = total + swap(sent.astype(BF16), "seq", other).astype(F32)
    bit = 2
    while bit < owners:
        total = halve(total, "dp", bit)
        bit *= 2
    own = total[0].astype(BF16)
    return lax.all_gather(own, "seq", axis=0, tiled=True).astype(F32)


def shards(
    tokens, ln_gain, ln_bias, w_qkv, qv_bias, w_out, w_fc, fc_bias, w_proj, branch_bias, cotangent
):
    owners = lax.axis_size("dp")
    parts = lax.axis_size("seq")
    share = ln_gain.shape[1]
    width = share * owners
    packed = jnp.concatenate(
        [ln_gain, ln_bias, qv_bias, branch_bias, fc_bias.reshape(-1, share)], axis=0
    )
    vectors = lax.all_gather(packed, "dp", axis=1, tiled=True).astype(F32)
    full_qkv = lax.all_gather(w_qkv, "dp", axis=0, tiled=True)
    full_out = lax.all_gather(w_out, "dp", axis=0, tiled=True)
    full_fc = lax.all_gather(w_fc, "dp", axis=0, tiled=True)
    full_proj = lax.all_gather(w_proj, "dp", axis=0, tiled=True)
    gain_vals, shift_vals, qv_vals, branch_vals = (
        vectors[0:2], vectors[2:4], vectors[4:6], vectors[6:8],
    )
    fc_vals = vectors[8:].reshape(-1, owners, share).transpose(1, 0, 2).reshape(-1)
    source = tokens[0].astype(F32)
    rows = source.shape[0]
    normed_first = layer_norm(source, gain_vals[0], shift_vals[0]).astype(BF16)
    bias = jnp.concatenate([qv_vals[0], jnp.zeros((width,), F32), qv_vals[1]])
    projected = (dot(full_qkv, normed_first, 0, 1) + bias[:, None]).astype(BF16)
    projected = projected.reshape(3, parts, width // parts, rows)
    qkv = lax.all_to_all(projected, "seq", split_axis=1, concat_axis=1, tiled=True)
    seq_heads, logs = attend_forward(qkv)
    head_out = lax.all_to_all(seq_heads, "seq", split_axis=0, concat_axis=0, tiled=True)
    head_out = head_out.reshape(width, rows)
    middle = source + (dot(head_out, full_out, 0, 0) + branch_vals[0])
    second = layer_norm(middle, gain_vals[1], shift_vals[1]).astype(BF16)
    hidden = dot(second, full_fc, 1, 0) + fc_vals
    active = jax.nn.gelu(hidden, approximate=True).astype(BF16)
    result = middle + (dot(active, full_proj, 1, 0) + branch_vals[1])
    upstream = cotangent[0]
    upstream_vals = upstream.astype(F32)
    grad_proj_bias = jnp.sum(upstream_vals, axis=0)
    grad_active = dot(upstream, full_proj, 1, 1)
    _, gelu_back = jax.vjp(partial(jax.nn.gelu, approximate=True), hidden)
    grad_hidden = gelu_back(grad_active)[0].astype(BF16)
    grad_fc_bias = jnp.sum(grad_hidden.astype(F32), axis=0)
    grad_second = dot(grad_hidden, full_fc, 1, 1)
    _, second_back = jax.vjp(layer_norm, middle, gain_vals[1], shift_vals[1])
    middle_part, grad_gain_two, grad_shift_two = second_back(grad_second)
    grad_middle = upstream_vals + middle_part
    grad_branch = grad_middle.astype(BF16)
    grad_out_bias = jnp.sum(grad_branch.astype(F32), axis=0)
    grad_head_out = dot(full_out, grad_branch, 1, 1).astype(BF16)
    seq_grad = lax.all_to_all(
        grad_head_out.reshape(parts, width // parts, rows),
        "seq", split_axis=0, concat_axis=0, tiled=True,
    )
    grad_proj = dot(active, upstream, 0, 0)
    grad_fc = dot(second, grad_hidden, 0, 0)
    grad_out = dot(head_out, grad_branch, 1, 0)
    seq_dqkv = attend_backward(qkv, seq_heads, logs, seq_grad)
    grad_qkv = lax.all_to_all(seq_dqkv, "seq", split_axis=1, concat_axis=1, tiled=True)
    grad_projected = grad_qkv.reshape(3 * width, rows)
    grad_sums = jnp.sum(grad_projected.astype(F32), axis=1)
    grad_first = dot(grad_projected, full_qkv, 0, 1)
    grad_w_qkv = dot(normed_first, grad_projected, 0, 1)
    _, first_back = jax.vjp(layer_norm, source, gain_vals[0], shift_vals[0])
    source_part, grad_gain_one, grad_shift_one = first_back(grad_first)
    input_grad = (grad_middle + source_part).astype(BF16)
    small = jnp.concatenate(
        [
            jnp.stack(
                [
                    grad_gain_one, grad_gain_two, grad_shift_one, grad_shift_two,
                    grad_sums[:width], grad_sums[2 * width :], grad_out_bias, grad_proj_bias,
                ]
            ),
            grad_fc_bias.reshape(owners, -1, share).transpose(1, 0, 2).reshape(-1, width),
        ],
        axis=0,
    )
    small = lax.psum(small, ("dp", "seq"))
    small = lax.dynamic_slice_in_dim(small, lax.axis_index("dp") * share, share, 1)
    return (
        result.astype(BF16)[None],
        input_grad[None],
        small[0:2],
        small[2:4],
        reduce_owned(grad_w_qkv),
        small[4:6],
        reduce_owned(grad_out),
        reduce_owned(grad_fc),
        small[8:].reshape(-1),
        reduce_owned(grad_proj),
        small[6:8],
    )


def solution(mesh):
    placed = (
        P("dp", "seq", None),
        P(None, "dp"),
        P(None, "dp"),
        P("dp", None),
        P(None, "dp"),
        P("dp", None),
        P("dp", None),
        P("dp"),
        P("dp", None),
        P(None, "dp"),
        P("dp", "seq", None),
    )
    return jax.shard_map(
        shards,
        mesh=mesh,
        in_specs=placed,
        out_specs=(
            P("dp", "seq", None),
            P("dp", "seq", None),
            P(None, "dp"),
            P(None, "dp"),
            P("dp", None),
            P(None, "dp"),
            P("dp", None),
            P("dp", None),
            P("dp"),
            P("dp", None),
            P(None, "dp"),
        ),
        check_vma=False,
    )
```

time: 940 us -> 509 us (0.54)
  waiting for transfers between devices: 425 us -> 131 us
  matrix products: 216 us -> 59.6 us
  other arithmetic: 90.3 us -> 24.9 us
  blocking collectives: 105 us -> 148 us
  Pallas kernels: 0 us -> 36.5 us
  loops' own time: 15.8 us -> 0 us
  local copies, waits for them, and re-layouts: 39.1 us -> 50.5 us
    reduce_scatter x4 -> x0, waiting for transfers between devices: 233 us -> none  [the longest x1 98.2 us: shards(): lax.psum_scatter(local_grads[7], 'dp', scatter_dimension=0, tiled=True)]
    dot_general x40 -> x12, matrix products: 216 us -> 59.6 us  [dot(): lax.dot_general(left, right, (((left_dim,), (right_dim,)), ((), ())), pre...]
    unnamed x17 -> x4, waiting for transfers between devices: 85.9 us -> 2.58 us
    all_gather x4, waiting for transfers between devices: 7.7 us -> 71.5 us  [the longest x1 41.4 us: shards(): full_proj = lax.all_gather(w_proj, 'dp', axis=0, tiled=True)]
    psum x1 -> x0, waiting for transfers between devices: 53.9 us -> none  [shards(): lax.psum(owned[2].astype(jnp.bfloat16), 'seq').astype(jnp.float32)]
    ppermute x0 -> x24, waiting for transfers between devices: none -> 47.3 us  [swap(): return lax.ppermute(value, axis, [(d, d ^ bit) for d in range(size)])]
    psum x1, blocking collectives: 9.95 us -> 56.2 us  [shards(): small = lax.psum(small, ('dp', 'seq'))]
    convert_element_type x25 -> x9, other arithmetic: 47.4 us -> 4.01 us  [the longest x4 3.91 us: reduce_owned(): return lax.all_gather(own, 'seq', axis=0, tiled=True).astype(F32)]
  transfers between devices with their start and end apart: 20 -> 31, of which waited for: 14 -> 12; matrix products, arithmetic and copies ran while one was open for 33% -> 20% of each run, Pallas kernels for 0% -> 7%
where the time goes in v1:
time: 509 us; the launch traced here: 502 us
  blocking collectives  148 us (29%)
  waiting for transfers between devices  131 us (26%)
  matrix products  59.6 us (12%)
  local copies, waits for them, and re-layouts  50.5 us (10%)
  starting transfers between devices  37 us (7%)
  Pallas kernels  36.5 us (7%)
  other arithmetic  24.9 us (5%)
  between operations  14.9 us (3%)
    dot_general x12, matrix products, dot(): lax.dot_general(left, right, (((left_dim,), (right_dim,)), ((), ())), pre...  59.6 us
    psum x1, blocking collectives, shards(): small = lax.psum(small, ('dp', 'seq'))  56.2 us
    ppermute x24, waiting for transfers between devices, swap(): return lax.ppermute(value, axis, [(d, d ^ bit) for d in range(size)])  47.3 us
    all_gather x4, blocking collectives, reduce_owned(): return lax.all_gather(own, 'seq', axis=0, tiled=True).astype(F32)  43.7 us
    all_gather x1, waiting for transfers between devices, shards(): full_proj = lax.all_gather(w_proj, 'dp', axis=0, tiled=True)  41.4 us
    all_to_all x1, blocking collectives, shards(): lax.all_to_all(projected, 'seq', split_axis=1, concat_axis=1, tiled=True)  32 us
    all_gather x1, waiting for transfers between devices, shards(): full_qkv = lax.all_gather(w_qkv, 'dp', axis=0, tiled=True)  26 us
    ppermute x24, starting transfers between devices, swap(): return lax.ppermute(value, axis, [(d, d ^ bit) for d in range(size)])  24.1 us
  transfers between devices with their start and end apart: 31, of which 12 were waited for; matrix products, arithmetic and copies ran while one was open for 20% of the time, Pallas kernels for 7%

profile of v1, /device:TPU:0, one launch (start us, length us, event | category | flops | bytes accessed | tf_op | source)
XLA Modules:
  0.0 502.4 jit_solution(9415037185809086342)
XLA Ops:
  11.5 15.8 %all-gather.4 = bf16[8,96,12]{1,2,0:T(8,128)(2,1)S(1)} all-gather(bf16[1,96,12]{1,2,0:T(8,128)(2,1)S(1)} %bitcast.264), channel_id=1, replica_groups=mesh['seq'=4,'dp'=8] {'dp'}, dimensions={0}, use_global_device_ids=true | all-gather | bytes 20736 | tf_op jit(solution)/shard_map/all_gather | solution.py:178
  28.0 26.0 %all-gather.10.cloned.1.call-done = bf16[768,2304]{1,0:T(8,128)(2,1)} async-done(((bf16[96,2304]{1,0:T(8,128)(2,1)}), bf16[768,2304]{1,0:T(8,128)(2,1)}) %all-gather.10.cloned.1.call-update) | async-done | bytes 3538960 | tf_op jit(solution)/shard_map/all_gather | solution.py:179
  54.0 5.6 %fusion.16 = bf16[2304,512]{0,1:T(8,128)(2,1)} fusion(bf16[768,2304]{1,0:T(8,128)(2,1)} %all-gather.10.cloned.1.call-done, f32[2304]{0:T(1024)S(1)} %pad_maximum_fusion, bf16[1,512,768]{2,1,0:T(8,128)(2,1)S(1)} %copy-done.2, f32[768]{0:T(1024)S(1)} %get-tuple-element.28, f32[768]{0:T(1024)S(1)} %get-tuple-element.29, f32[512]{0:T(512)S(1)} %fusion.71, ...), kind=kOutput, calls=%fused_computation.27 | convolution fusion | flops 1816657920 | bytes 6704128 | tf_op jit(solution)/shard_map/dot_general | solution.py:24
  59.6 2.9 copy.140
  62.6 32.0 %all_to_all.20 = bf16[3,4,192,512]{3,2,0,1:T(8,128)(2,1)S(1)} all-to-all(bf16[3,4,192,512]{3,2,0,1:T(8,128)(2,1)S(1)} %copy.141), channel_id=1, replica_groups=mesh['seq'=4,'dp'=8] {'seq'}, dimensions={1} | all-to-all | bytes 4718592 | tf_op jit(solution)/shard_map/all_to_all | solution.py:193
  94.8 12.6 %attend_forward.1 = (bf16[4,192,512]{2,1,0:T(8,128)(2,1)}, f32[3,4,8,512]{3,2,1,0:T(8,128)S(1)}) custom-call(bf16[3,4,192,512]{3,2,1,0:T(8,128)(2,1)S(1)} %copy.142.qkv_ref), custom_call_target="tpu_custom_call" | custom-call | flops 8053063680 | bytes 4718592 | tf_op jit(solution)/shard_map/attend_forward/pallas_call | solution.py:96
  107.4 4.7 all-to-all-start.1
  112.4 9.9 %all-to-all-done.1 = bf16[4,192,512]{2,1,0:T(8,128)(2,1)} async-done(((bf16[4,192,512]{2,1,0:T(8,128)(2,1)}), bf16[4,192,512]{2,1,0:T(8,128)(2,1)}, u32[]{:S(2)}, u32[]{:S(2)}) %all-to-all-start.1) | async-done | bytes 786464 | tf_op jit(solution)/shard_map/all_to_all | solution.py:195
  122.3 2.4 fusion.86
  126.2 4.2 all-gather.14.cloned.1.call-done
  130.3 10.7 %fusion.14 = (bf16[3072,512]{0,1:T(8,128)(2,1)}, f32[512,3072]{1,0:T(8,128)}) fusion(f32[3072]{0:T(1024)S(1)} %add.304, bf16[768,3072]{1,0:T(8,128)(2,1)} %all-gather.14.cloned.1.call-done, f32[512,768]{1,0:T(8,128)} %copy-done.8, f32[768]{0:T(1024)S(1)} %get-tuple-element.23, f32[768]{0:T(1024)S(1)} %get-tuple-element.24, f32[512]{0:T(512)S(1)} %fusion.72, ...), kind=kOutput, calls=%fused_computation.17 | convolution fusion | flops 2433613824 | bytes 15751168 | tf_op jit(solution)/shard_map/dot_general | solution.py:24
  141.0 41.4 %all-gather.16.cloned.1.call-done = bf16[3072,768]{1,0:T(8,128)(2,1)} async-done(((bf16[384,768]{1,0:T(8,128)(2,1)}), bf16[3072,768]{1,0:T(8,128)(2,1)}) %all-gather.16.cloned.1.call-update) | async-done | bytes 4718608 | tf_op jit(solution)/shard_map/all_gather | solution.py:182
  182.4 9.7 %convert_reduce_fusion = (f32[3072]{0:T(1024)}, bf16[512,3072]{1,0:T(8,128)(2,1)S(1)}) fusion(f32[512,3072]{1,0:T(8,128)} %get-tuple-element.62, f32[3072]{0:T(1024)S(1)} %add.304, bf16[3072,768]{1,0:T(8,128)(2,1)} %all-gather.16.cloned.1.call-done, bf16[1,512,768]{2,1,0:T(8,128)(2,1)S(1)} %copy-done.13), kind=kOutput, calls=%fused_computation.18 | convolution fusion | flops 2452091904 | bytes 14966784 | tf_op jit(solution)/shard_map/dot_general | solution.py:24
  192.2 3.5 multiply_reduce_fusion
  200.7 3.8 all-to-all-start.2
  204.6 2.3 fusion.46
  206.8 1.4 copy-done.7
  209.2 9.1 %fusion.34 = bf16[1,512,768]{2,1,0:T(8,128)(2,1)} fusion(f32[512,768]{1,0:T(8,128)S(1)} %copy-done.10, bf16[3072,768]{1,0:T(8,128)(2,1)} %all-gather.16.cloned.1.call-done, f32[512,3072]{1,0:T(8,128)} %get-tuple-element.62, f32[3072]{0:T(1024)S(1)} %add.304, f32[768]{0:T(1024)S(1)} %get-tuple-element.22), kind=kOutput, calls=%fused_computation.61 | convolution fusion | flops 2432827392 | bytes 13384704 | tf_op jit(solution)/shard_map/dot_general | solution.py:24
  218.3 2.9 fusion.80
  221.3 3.6 copy-done.12
  224.9 1.8 fusion.19
  227.7 4.7 copy.158
  232.4 1.6 bitcast_add_fusion.5
  234.9 2.9 collective-permute-start.9
  238.4 23.8 %attend_backward.1 = bf16[3,4,192,512]{3,2,1,0:T(8,128)(2,1)S(1)} custom-call(bf16[3,4,192,512]{3,2,1,0:T(8,128)(2,1)S(1)} %copy.142.qkv_ref, bf16[4,192,512]{2,1,0:T(8,128)(2,1)} %get-tuple-element.13.out_ref, f32[3,4,8,512]{3,2,1,0:T(8,128)S(1)} %get-tuple-element.14.log_ref, bf16[4,192,512]{2,1,0:T(8,128)(2,1)S(1)} %all-to-all-done.2.grad_ref), custom_call_target="tpu_custom_call" | custom-call | flops 20132659200 | bytes 14155776 | tf_op jit(solution)/shard_map/attend_backward/pallas_call | solution.py:118
  262.2 1.5 copy.146
  263.7 4.3 all-to-all-start.3
  268.7 1.2 fusion.65
  270.1 8.2 %fusion.44 = f32[4,2,4,96,768]{4,3,2,1,0:T(8,128)} fusion(bf16[4,2,4,96,512]{4,3,2,1,0:T(8,128)(2,1)} %bitcast.254, bf16[1,512,768]{2,1,0:T(8,128)(2,1)S(1)} %copy-done.14), kind=kOutput, calls=%fused_computation.85 | convolution fusion | flops 2415919104 | bytes 13369344 | tf_op jit(solution)/shard_map/dot_general | solution.py:24
  280.5 1.7 collective-permute-start.11
  282.2 4.0 fusion.18
  286.3 12.6 %all-gather.1 = bf16[1,96,768]{2,1,0:T(8,128)(2,1)S(1)} all-gather(bf16[1,24,768]{2,1,0:T(8,128)(2,1)S(1)} %add_convert_fusion.6), channel_id=3, replica_groups=mesh['seq'=4,'dp'=8] {'seq'}, dimensions={1}, use_global_device_ids=true | all-gather | bytes 184320 | tf_op jit(solution)/shard_map/all_gather | solution.py:165
  300.9 1.8 copy-done.27
  302.7 2.3 fusion.82
  308.9 3.6 fusion.77
  313.1 1.4 copy.149
  314.5 2.1 fusion.87
  316.7 2.9 copy-done
  319.8 3.7 bitcast_add_fusion.1
  323.6 2.2 copy-done.4
  325.8 1.3 fusion.53
  327.0 1.4 collective-permute-start.15
  329.1 1.5 collective-permute-start.13
  330.5 2.0 concatenate.11
  332.5 56.2 %psum.7 = f32[12,768]{1,0:T(8,128)} all-reduce(f32[12,768]{1,0:T(8,128)} %concatenate.11), channel_id=1, replica_groups=mesh['seq'=4,'dp'=8] {'dp','seq'}, use_global_device_ids=true, to_apply=%region_16.0 | all-reduce | flops 9216 | bytes 73728 | tf_op jit(solution)/shard_map/psum | solution.py:244
  390.1 3.6 bitcast_add_fusion
  393.9 3.2 collective-permute-start.21
  397.1 1.5 fusion.85
  399.4 2.2 fusion.39
  401.7 1.2 collective-permute-start.16
  402.9 8.5 %collective-permute-done.21 = bf16[4,96,768]{2,1,0:T(8,128)(2,1)S(1)} collective-permute-done((bf16[4,96,768]{2,1,0:T(8,128)(2,1)S(1)}, bf16[4,96,768]{2,1,0:T(8,128)(2,1)S(1)}, u32[]{:S(2)}, u32[]{:S(2)}) %collective-permute-start.21) | collective-permute-done | bytes 589856 | tf_op jit(solution)/shard_map/ppermute | solution.py:138
  411.4 10.4 %collective-permute-done.20 = bf16[4,96,768]{2,1,0:T(8,128)(2,1)S(1)} collective-permute-done((bf16[4,96,768]{2,1,0:T(8,128)(2,1)S(1)}, bf16[4,96,768]{2,1,0:T(8,128)(2,1)S(1)}, u32[]{:S(2)}, u32[]{:S(2)}) %collective-permute-start.20) | collective-permute-done | bytes 589856 | tf_op jit(solution)/shard_map/ppermute | solution.py:138
  422.9 1.2 collective-permute-start.22
  424.2 1.8 collective-permute-start.17
  425.9 8.4 %collective-permute-done.22 = bf16[2,96,768]{2,1,0:T(8,128)(2,1)S(1)} collective-permute-done((bf16[2,96,768]{2,1,0:T(8,128)(2,1)S(1)}, bf16[2,96,768]{2,1,0:T(8,128)(2,1)S(1)}, u32[]{:S(2)}, u32[]{:S(2)}) %collective-permute-start.22) | collective-permute-done | bytes 294944 | tf_op jit(solution)/shard_map/ppermute | solution.py:138
  434.8 11.7 %all-gather.2 = bf16[1,96,3072]{2,1,0:T(8,128)(2,1)S(1)} all-gather(bf16[1,24,3072]{2,1,0:T(8,128)(2,1)S(1)} %add_convert_fusion.4), channel_id=4, replica_groups=mesh['seq'=4,'dp'=8] {'seq'}, dimensions={1}, use_global_device_ids=true | all-gather | bytes 737280 | tf_op jit(solution)/shard_map/all_gather | solution.py:165
  447.1 1.5 collective-permute-start.3
  448.6 2.0 collective-permute-start.1
  451.8 9.3 %collective-permute-done.3 = bf16[4,24,2304]{2,1,0:T(8,128)(2,1)S(1)} collective-permute-done((bf16[4,24,2304]{2,1,0:T(8,128)(2,1)S(1)}, bf16[4,24,2304]{2,1,0:T(8,128)(2,1)S(1)}, u32[]{:S(2)}, u32[]{:S(2)}) %collective-permute-start.3) | collective-permute-done | bytes 442400 | tf_op jit(solution)/shard_map/ppermute | solution.py:138
  461.1 4.7 collective-permute-done.2
  466.3 2.3 collective-permute-start.4
  468.6 10.2 %all-gather.3 = bf16[1,384,768]{2,1,0:T(8,128)(2,1)S(1)} all-gather(bf16[1,96,768]{2,1,0:T(8,128)(2,1)S(1)} %add_convert_fusion.3), channel_id=5, replica_groups=mesh['seq'=4,'dp'=8] {'seq'}, dimensions={1}, use_global_device_ids=true | all-gather | bytes 737280 | tf_op jit(solution)/shard_map/all_gather | solution.py:165
  480.4 4.9 collective-permute-done.5
  485.3 9.1 %all-gather = bf16[1,96,2304]{2,1,0:T(8,128)(2,1)S(1)} all-gather(bf16[1,24,2304]{2,1,0:T(8,128)(2,1)S(1)} %add_convert_fusion.5), channel_id=2, replica_groups=mesh['seq'=4,'dp'=8] {'seq'}, dimensions={1}, use_global_device_ids=true | all-gather | bytes 552960 | tf_op jit(solution)/shard_map/all_gather | solution.py:165
  (177 shorter events, 34.6 us)
Async XLA Ops:
  7.2 20.3 %copy-start.2 = (bf16[1,512,768]{2,1,0:T(8,128)(2,1)S(1)}, bf16[1,512,768]{2,1,0:T(8,128)(2,1)}, u32[]{:S(2)}) copy-start(bf16[1,512,768]{2,1,0:T(8,128)(2,1)} %param.11) | copy-start | bytes 2359300
  7.2 46.8 %all-gather.10.cloned.1.call-start = ((), (), s32[]{:S(2)}) async-start(), calls=%async_computation.4 | async-start | bytes 3981312 | tf_op jit(solution)/shard_map/all_gather | solution.py:179
  7.9 104.4 %all-gather.12.cloned.1.call-start = ((), (), s32[]{:S(2)}) async-start(), calls=%async_computation.5 | async-start | bytes 1327104 | tf_op jit(solution)/shard_map/all_gather | solution.py:180
  8.7 121.7 %all-gather.14.cloned.1.call-start = ((), (), s32[]{:S(2)}) async-start(), calls=%async_computation.6 | async-start | bytes 5308416 | tf_op jit(solution)/shard_map/all_gather | solution.py:181
  9.4 173.0 %all-gather.16.cloned.1.call-start = ((), (), s32[]{:S(2)}) async-start(), calls=%async_computation.7 | async-start | bytes 5308416 | tf_op jit(solution)/shard_map/all_gather | solution.py:182
  27.4 32.1 %copy-start.20 = (f32[768]{0:T(1024)}, f32[768]{0:T(1024)S(1)}, u32[]{:S(2)}) copy-start(f32[768]{0:T(1024)S(1)} %get-tuple-element.28) | copy-start | bytes 9220
  107.4 14.8 %all-to-all-start.1 = ((bf16[4,192,512]{2,1,0:T(8,128)(2,1)}), bf16[4,192,512]{2,1,0:T(8,128)(2,1)}, u32[]{:S(2)}, u32[]{:S(2)}) async-start(bf16[4,192,512]{2,1,0:T(8,128)(2,1)} %get-tuple-element.13.out_ref), calls=%async_computation.1 | async-start | bytes 1572864 | tf_op jit(solution)/shard_map/all_to_all | solution.py:195
  124.7 1.2 copy-start.8
  130.3 52.1 %copy-start.13 = (bf16[1,512,768]{2,1,0:T(8,128)(2,1)S(1)}, bf16[1,512,768]{2,1,0:T(8,128)(2,1)}, u32[]{:S(2)}) copy-start(bf16[1,512,768]{2,1,0:T(8,128)(2,1)} %param.21) | copy-start | bytes 2359300
  182.4 9.8 %copy-start.9 = (f32[512,768]{1,0:T(8,128)S(1)}, f32[512,768]{1,0:T(8,128)}, u32[]{:S(2)}) copy-start(f32[512,768]{1,0:T(8,128)} %copy-done.8) | copy-start | bytes 4718596
  182.4 9.8 %copy-start.26 = (bf16[768,3072]{1,0:T(8,128)(2,1)S(1)}, bf16[768,3072]{1,0:T(8,128)(2,1)}, u32[]{:S(2)}) copy-start(bf16[768,3072]{1,0:T(8,128)(2,1)} %all-gather.14.cloned.1.call-done) | copy-start | bytes 14155780
  192.1 3.5 copy-start.29
  196.3 1.2 copy-start.1
  196.3 2.4 copy-start.28
  196.4 3.2 copy-start.18
  197.9 0.9 copy-start.15
  200.7 37.6 %all-to-all-start.2 = ((bf16[4,192,512]{2,1,0:T(8,128)(2,1)}), bf16[4,192,512]{2,1,0:T(8,128)(2,1)S(1)}, u32[]{:S(2)}, u32[]{:S(2)}) async-start(bf16[4,192,512]{2,1,0:T(8,128)(2,1)} %bitcast.255), calls=%async_computation.2 | async-start | bytes 1572864 | tf_op jit(solution)/shard_map/all_to_all | solution.py:216
  204.5 4.6 copy-start.10
  206.8 1.4 copy-start.7
  209.1 23.3 %collective-permute-start.6 = (bf16[4,4,24,768]{3,2,1,0:T(8,128)(2,1)}, bf16[4,4,24,768]{3,2,1,0:T(8,128)(2,1)}, u32[]{:S(2)}, u32[]{:S(2)}) collective-permute-start(bf16[4,4,24,768]{3,2,1,0:T(8,128)(2,1)} %fusion.52), channel_id=1, source_target_pairs={{0,1},{1,0},{2,3},{3,2},{4,5},{5,4},{6,7},{7,6},{8,9},{9,8},{10,11... | collective-permute-start | bytes 1769480 | tf_op jit(solution)/shard_map/ppermute | solution.py:138
  209.2 9.1 %copy-start.30 = (bf16[512,3072]{1,0:T(8,128)(2,1)S(1)}, bf16[512,3072]{1,0:T(8,128)(2,1)}, u32[]{:S(2)}) copy-start(bf16[512,3072]{1,0:T(8,128)(2,1)} %copy-done.29) | copy-start | bytes 9437188
  221.3 3.6 copy-start.12
  227.3 92.6 %collective-permute-start.12 = (bf16[4,4,24,3072]{3,2,0,1:T(8,128)(2,1)}, bf16[4,4,24,3072]{3,2,0,1:T(8,128)(2,1)}, u32[]{:S(2)}, u32[]{:S(2)}) collective-permute-start(bf16[4,4,24,3072]{3,2,0,1:T(8,128)(2,1)} %fusion.19), channel_id=1, source_target_pairs={{0,1},{1,0},{2,3},{3,2},{4,5},{5,4},{6,7},{7,6},{8,9},{9,8},{10,11... | collective-permute-start | bytes 7077896 | tf_op jit(solution)/shard_map/ppermute | solution.py:138
  234.0 4.4 copy-start.16
  234.9 33.2 %collective-permute-start.9 = (bf16[4,24,768]{2,1,0:T(8,128)(2,1)}, bf16[4,24,768]{2,1,0:T(8,128)(2,1)S(1)}, u32[]{:S(2)}, u32[]{:S(2)}) collective-permute-start(bf16[4,24,768]{2,1,0:T(8,128)(2,1)} %get-tuple-element.46), channel_id=1, source_target_pairs={{0,24},{8,16},{16,8},{24,0},{1,25},{9,17},{17,9},{25,1},{2,26},{10... | collective-permute-start | bytes 442376 | tf_op jit(solution)/shard_map/ppermute | solution.py:138
  237.8 30.3 %collective-permute-start.8 = (bf16[4,24,768]{2,1,0:T(8,128)(2,1)}, bf16[4,24,768]{2,1,0:T(8,128)(2,1)}, u32[]{:S(2)}, u32[]{:S(2)}) collective-permute-start(bf16[4,24,768]{2,1,0:T(8,128)(2,1)} %get-tuple-element.47), channel_id=1, source_target_pairs={{0,16},{8,24},{16,0},{24,8},{1,17},{9,25},{17,1},{25,9},{2,18},{10... | collective-permute-start | bytes 442376 | tf_op jit(solution)/shard_map/ppermute | solution.py:138
  238.3 30.4 %collective-permute-start.7 = (bf16[4,24,768]{2,1,0:T(8,128)(2,1)}, bf16[4,24,768]{2,1,0:T(8,128)(2,1)}, u32[]{:S(2)}, u32[]{:S(2)}) collective-permute-start(bf16[4,24,768]{2,1,0:T(8,128)(2,1)} %get-tuple-element.45), channel_id=1, source_target_pairs={{0,8},{8,0},{16,24},{24,16},{1,9},{9,1},{17,25},{25,17},{2,10},{10... | collective-permute-start | bytes 442376 | tf_op jit(solution)/shard_map/ppermute | solution.py:138
  263.7 6.3 %copy-start.14 = (bf16[1,512,768]{2,1,0:T(8,128)(2,1)S(1)}, bf16[1,512,768]{2,1,0:T(8,128)(2,1)}, u32[]{:S(2)}) copy-start(bf16[1,512,768]{2,1,0:T(8,128)(2,1)} %param.21) | copy-start | bytes 2359300
  263.7 35.9 %all-to-all-start.3 = ((bf16[3,4,192,512]{3,2,0,1:T(8,128)(2,1)}), bf16[3,4,192,512]{3,2,0,1:T(8,128)(2,1)S(1)}, u32[]{:S(2)}, u32[]{:S(2)}) async-start(bf16[3,4,192,512]{3,2,0,1:T(8,128)(2,1)} %copy.146), calls=%async_computation.3 | async-start | bytes 4718592 | tf_op jit(solution)/shard_map/all_to_all | solution.py:224
  268.0 0.7 copy-start.17
  270.0 9.6 %collective-permute-start.10 = (bf16[2,24,768]{2,1,0:T(8,128)(2,1)S(1)}, bf16[2,24,768]{2,1,0:T(8,128)(2,1)}, u32[]{:S(2)}, u32[]{:S(2)}) collective-permute-start(bf16[2,24,768]{2,1,0:T(8,128)(2,1)S(1)} %fusion.70), channel_id=1, source_target_pairs={{0,2},{1,3},{2,0},{3,1},{4,6},{5,7},{6,4},{7,5},{8,10},{9,11},{10,... | collective-permute-start | bytes 221192 | tf_op jit(solution)/shard_map/ppermute | solution.py:138
  270.1 8.2 %copy-start.25 = (f32[768]{0:T(1024)S(1)}, f32[768]{0:T(1024)}, u32[]{:S(2)}) copy-start(f32[768]{0:T(1024)} %get-tuple-element.15) | copy-start | bytes 9220
  270.1 8.8 %copy-start.24 = (f32[768]{0:T(1024)S(1)}, f32[768]{0:T(1024)}, u32[]{:S(2)}) copy-start(f32[768]{0:T(1024)} %get-tuple-element.19) | copy-start | bytes 9220
  270.1 9.3 %copy-start.23 = (f32[3072]{0:T(1024)S(1)}, f32[3072]{0:T(1024)}, u32[]{:S(2)}) copy-start(f32[3072]{0:T(1024)} %get-tuple-element.59) | copy-start | bytes 36868
  280.5 5.7 %collective-permute-start.11 = (bf16[1,24,768]{2,1,0:T(8,128)(2,1)S(1)}, bf16[1,24,768]{2,1,0:T(8,128)(2,1)S(1)}, u32[]{:S(2)}, u32[]{:S(2)}) collective-permute-start(bf16[1,24,768]{2,1,0:T(8,128)(2,1)S(1)} %dynamic-slice_convert_fusion.13), channel_id=1, source_target_pairs={{0,4},{1,5},{2,6},{3,7},{4,0},{5,1},{6,2},{7,3},{8,12},{9,13},{10,... | collective-permute-start | bytes 110600 | tf_op jit(solution)/shard_map/ppermute | solution.py:138
  286.2 103.9 %collective-permute-start.18 = (bf16[4,4,96,768]{3,2,1,0:T(8,128)(2,1)}, bf16[4,4,96,768]{3,2,1,0:T(8,128)(2,1)}, u32[]{:S(2)}, u32[]{:S(2)}) collective-permute-start(bf16[4,4,96,768]{3,2,1,0:T(8,128)(2,1)} %fusion.18), channel_id=1, source_target_pairs={{0,1},{1,0},{2,3},{3,2},{4,5},{5,4},{6,7},{7,6},{8,9},{9,8},{10,11... | collective-permute-start | bytes 7077896 | tf_op jit(solution)/shard_map/ppermute | solution.py:138
  299.6 1.3 copy-start.3
  299.6 3.1 copy-start.27
  299.8 5.2 %copy-start.5 = (bf16[3,4,192,512]{3,2,1,0:T(8,128)(2,1)}, bf16[3,4,192,512]{3,2,1,0:T(8,128)(2,1)S(1)}, u32[]{:S(2)}) copy-start(bf16[3,4,192,512]{3,2,1,0:T(8,128)(2,1)S(1)} %copy.147) | copy-start | bytes 7077892
  305.0 2.5 copy-start.11
  305.0 3.9 copy-start.19
  305.1 3.9 copy-start.21
  308.9 5.6 %copy-start.6 = (bf16[3,4,192,512]{3,2,1,0:T(8,128)(2,1)S(1)}, bf16[3,4,192,512]{3,2,1,0:T(8,128)(2,1)}, u32[]{:S(2)}) copy-start(bf16[3,4,192,512]{3,2,1,0:T(8,128)(2,1)} %copy-done.5) | copy-start | bytes 7077892
  316.7 2.9 copy-start
  319.8 126.8 %collective-permute-start = (bf16[4,4,24,2304]{3,2,1,0:T(8,128)(2,1)S(1)}, bf16[4,4,24,2304]{3,2,1,0:T(8,128)(2,1)S(1)}, u32[]{:S(2)}, u32[]{:S(2)}) collective-permute-start(bf16[4,4,24,2304]{3,2,1,0:T(8,128)(2,1)S(1)} %fusion.28), channel_id=1, source_target_pairs={{0,1},{1,0},{2,3},{3,2},{4,5},{5,4},{6,7},{7,6},{8,9},{9,8},{10,11... | collective-permute-start | bytes 5308424 | tf_op jit(solution)/shard_map/ppermute | solution.py:138
  323.5 2.2 copy-start.4
  325.8 4.8 copy-start.22
  327.0 71.6 %collective-permute-start.15 = (bf16[4,24,3072]{2,1,0:T(8,128)(2,1)}, bf16[4,24,3072]{2,1,0:T(8,128)(2,1)}, u32[]{:S(2)}, u32[]{:S(2)}) collective-permute-start(bf16[4,24,3072]{2,1,0:T(8,128)(2,1)} %get-tuple-element.40), channel_id=1, source_target_pairs={{0,24},{8,16},{16,8},{24,0},{1,25},{9,17},{17,9},{25,1},{2,26},{10... | collective-permute-start | bytes 1769480 | tf_op jit(solution)/shard_map/ppermute | solution.py:138
  328.5 70.8 %collective-permute-start.14 = (bf16[4,24,3072]{2,1,0:T(8,128)(2,1)}, bf16[4,24,3072]{2,1,0:T(8,128)(2,1)}, u32[]{:S(2)}, u32[]{:S(2)}) collective-permute-start(bf16[4,24,3072]{2,1,0:T(8,128)(2,1)} %get-tuple-element.41), channel_id=1, source_target_pairs={{0,16},{8,24},{16,0},{24,8},{1,17},{9,25},{17,1},{25,9},{2,18},{10... | collective-permute-start | bytes 1769480 | tf_op jit(solution)/shard_map/ppermute | solution.py:138
  329.1 70.3 %collective-permute-start.13 = (bf16[4,24,3072]{2,1,0:T(8,128)(2,1)}, bf16[4,24,3072]{2,1,0:T(8,128)(2,1)}, u32[]{:S(2)}, u32[]{:S(2)}) collective-permute-start(bf16[4,24,3072]{2,1,0:T(8,128)(2,1)} %get-tuple-element.39), channel_id=1, source_target_pairs={{0,8},{8,0},{16,24},{24,16},{1,9},{9,1},{17,25},{25,17},{2,10},{10... | collective-permute-start | bytes 1769480 | tf_op jit(solution)/shard_map/ppermute | solution.py:138
  393.9 17.5 %collective-permute-start.21 = (bf16[4,96,768]{2,1,0:T(8,128)(2,1)S(1)}, bf16[4,96,768]{2,1,0:T(8,128)(2,1)S(1)}, u32[]{:S(2)}, u32[]{:S(2)}) collective-permute-start(bf16[4,96,768]{2,1,0:T(8,128)(2,1)S(1)} %get-tuple-element.37), channel_id=1, source_target_pairs={{0,24},{8,16},{16,8},{24,0},{1,25},{9,17},{17,9},{25,1},{2,26},{10... | collective-permute-start | bytes 1769480 | tf_op jit(solution)/shard_map/ppermute | solution.py:138
  398.6 23.2 %collective-permute-start.20 = (bf16[4,96,768]{2,1,0:T(8,128)(2,1)S(1)}, bf16[4,96,768]{2,1,0:T(8,128)(2,1)S(1)}, u32[]{:S(2)}, u32[]{:S(2)}) collective-permute-start(bf16[4,96,768]{2,1,0:T(8,128)(2,1)S(1)} %get-tuple-element.38), channel_id=1, source_target_pairs={{0,16},{8,24},{16,0},{24,8},{1,17},{9,25},{17,1},{25,9},{2,18},{10... | collective-permute-start | bytes 1769480 | tf_op jit(solution)/shard_map/ppermute | solution.py:138
  399.3 23.3 %collective-permute-start.19 = (bf16[4,96,768]{2,1,0:T(8,128)(2,1)S(1)}, bf16[4,96,768]{2,1,0:T(8,128)(2,1)S(1)}, u32[]{:S(2)}, u32[]{:S(2)}) collective-permute-start(bf16[4,96,768]{2,1,0:T(8,128)(2,1)S(1)} %get-tuple-element.36), channel_id=1, source_target_pairs={{0,8},{8,0},{16,24},{24,16},{1,9},{9,1},{17,25},{25,17},{2,10},{10... | collective-permute-start | bytes 1769480 | tf_op jit(solution)/shard_map/ppermute | solution.py:138
  399.4 47.2 %slice-start = ((s8[7077888]{0:T(1024)(128)(4,1)}), s8[4194304]{0:T(1024)(128)(4,1)S(1)}, s32[]{:S(2)}) async-start(s8[7077888]{0:T(1024)(128)(4,1)} %bitcast.242), calls=%async_computation.8 | async-start | bytes 8388608
  401.6 44.9 %slice-start.1 = ((s8[7077888]{0:T(1024)(128)(4,1)}), s8[2883584]{0:T(1024)(128)(4,1)S(1)}, s32[]{:S(2)}) async-start(s8[7077888]{0:T(1024)(128)(4,1)} %bitcast.242), calls=%async_computation.9 | async-start | bytes 5767168
  401.7 22.4 %collective-permute-start.16 = (bf16[2,24,3072]{2,1,0:T(8,128)(2,1)S(1)}, bf16[2,24,3072]{2,1,0:T(8,128)(2,1)S(1)}, u32[]{:S(2)}, u32[]{:S(2)}) collective-permute-start(bf16[2,24,3072]{2,1,0:T(8,128)(2,1)S(1)} %fusion.62), channel_id=1, source_target_pairs={{0,2},{1,3},{2,0},{3,1},{4,6},{5,7},{6,4},{7,5},{8,10},{9,11},{10,... | collective-permute-start | bytes 884744 | tf_op jit(solution)/shard_map/ppermute | solution.py:138
  422.9 11.4 %collective-permute-start.22 = (bf16[2,96,768]{2,1,0:T(8,128)(2,1)S(1)}, bf16[2,96,768]{2,1,0:T(8,128)(2,1)S(1)}, u32[]{:S(2)}, u32[]{:S(2)}) collective-permute-start(bf16[2,96,768]{2,1,0:T(8,128)(2,1)S(1)} %fusion.63), channel_id=1, source_target_pairs={{0,2},{1,3},{2,0},{3,1},{4,6},{5,7},{6,4},{7,5},{8,10},{9,11},{10,... | collective-permute-start | bytes 884744 | tf_op jit(solution)/shard_map/ppermute | solution.py:138
  424.2 10.6 %collective-permute-start.17 = (bf16[1,24,3072]{2,1,0:T(8,128)(2,1)S(1)}, bf16[1,24,3072]{2,1,0:T(8,128)(2,1)S(1)}, u32[]{:S(2)}, u32[]{:S(2)}) collective-permute-start(bf16[1,24,3072]{2,1,0:T(8,128)(2,1)S(1)} %dynamic-slice_convert_fusion.10), channel_id=1, source_target_pairs={{0,4},{1,5},{2,6},{3,7},{4,0},{5,1},{6,2},{7,3},{8,12},{9,13},{10,... | collective-permute-start | bytes 442376 | tf_op jit(solution)/shard_map/ppermute | solution.py:138
  434.4 34.2 %collective-permute-start.23 = (bf16[1,96,768]{2,1,0:T(8,128)(2,1)S(1)}, bf16[1,96,768]{2,1,0:T(8,128)(2,1)S(1)}, u32[]{:S(2)}, u32[]{:S(2)}) collective-permute-start(bf16[1,96,768]{2,1,0:T(8,128)(2,1)S(1)} %dynamic-slice_convert_fusion.9), channel_id=1, source_target_pairs={{0,4},{1,5},{2,6},{3,7},{4,0},{5,1},{6,2},{7,3},{8,12},{9,13},{10,... | collective-permute-start | bytes 442376 | tf_op jit(solution)/shard_map/ppermute | solution.py:138
  447.1 14.0 %collective-permute-start.3 = (bf16[4,24,2304]{2,1,0:T(8,128)(2,1)S(1)}, bf16[4,24,2304]{2,1,0:T(8,128)(2,1)S(1)}, u32[]{:S(2)}, u32[]{:S(2)}) collective-permute-start(bf16[4,24,2304]{2,1,0:T(8,128)(2,1)S(1)} %get-tuple-element.43), channel_id=1, source_target_pairs={{0,24},{8,16},{16,8},{24,0},{1,25},{9,17},{17,9},{25,1},{2,26},{10... | collective-permute-start | bytes 1327112 | tf_op jit(solution)/shard_map/ppermute | solution.py:138
  448.6 17.2 %collective-permute-start.2 = (bf16[4,24,2304]{2,1,0:T(8,128)(2,1)S(1)}, bf16[4,24,2304]{2,1,0:T(8,128)(2,1)S(1)}, u32[]{:S(2)}, u32[]{:S(2)}) collective-permute-start(bf16[4,24,2304]{2,1,0:T(8,128)(2,1)S(1)} %get-tuple-element.44), channel_id=1, source_target_pairs={{0,16},{8,24},{16,0},{24,8},{1,17},{9,25},{17,1},{25,9},{2,18},{10... | collective-permute-start | bytes 1327112 | tf_op jit(solution)/shard_map/ppermute | solution.py:138
  448.6 17.4 %collective-permute-start.1 = (bf16[4,24,2304]{2,1,0:T(8,128)(2,1)S(1)}, bf16[4,24,2304]{2,1,0:T(8,128)(2,1)S(1)}, u32[]{:S(2)}, u32[]{:S(2)}) collective-permute-start(bf16[4,24,2304]{2,1,0:T(8,128)(2,1)S(1)} %get-tuple-element.42), channel_id=1, source_target_pairs={{0,8},{8,0},{16,24},{24,16},{1,9},{9,1},{17,25},{25,17},{2,10},{10... | collective-permute-start | bytes 1327112 | tf_op jit(solution)/shard_map/ppermute | solution.py:138
  466.3 12.5 %collective-permute-start.4 = (bf16[2,24,2304]{2,1,0:T(8,128)(2,1)S(1)}, bf16[2,24,2304]{2,1,0:T(8,128)(2,1)S(1)}, u32[]{:S(2)}, u32[]{:S(2)}) collective-permute-start(bf16[2,24,2304]{2,1,0:T(8,128)(2,1)S(1)} %fusion.66), channel_id=1, source_target_pairs={{0,2},{1,3},{2,0},{3,1},{4,6},{5,7},{6,4},{7,5},{8,10},{9,11},{10,... | collective-permute-start | bytes 663560 | tf_op jit(solution)/shard_map/ppermute | solution.py:138
  478.9 6.4 %collective-permute-start.5 = (bf16[1,24,2304]{2,1,0:T(8,128)(2,1)S(1)}, bf16[1,24,2304]{2,1,0:T(8,128)(2,1)S(1)}, u32[]{:S(2)}, u32[]{:S(2)}) collective-permute-start(bf16[1,24,2304]{2,1,0:T(8,128)(2,1)S(1)} %dynamic-slice_convert_fusion.12), channel_id=1, source_target_pairs={{0,4},{1,5},{2,6},{3,7},{4,0},{5,1},{6,2},{7,3},{8,12},{9,13},{10,... | collective-permute-start | bytes 331784 | tf_op jit(solution)/shard_map/ppermute | solution.py:138
Sparse Core Ops, SparseCore 0:
  9.7 44.2 all-gather.9
  55.6 21.4 all-gather.11
  78.8 51.4 all-gather.13
  131.8 50.5 all-gather.15

commit v2 on v1

--- a/solution.py
+++ b/solution.py
@@ -146,12 +146,62 @@
     return kept.astype(F32) + swap(sent.astype(BF16), axis, bit).astype(F32)
 
 
-def reduce_owned(value):
+def join(value, axis, bit, dim):
+    upper = (lax.axis_index(axis) // bit) % 2 == 1
+    other = swap(value, axis, bit)
+    first = jnp.where(upper, other, value)
+    second = jnp.where(upper, value, other)
+    return jnp.stack([first, second], axis=dim)
+
+
+def bits_of(axis):
+    size = lax.axis_size(axis)
+    bits = []
+    bit = 1
+    while bit < size:
+        bits.insert(0, bit)
+        bit *= 2
+    return bits
+
+
+def join_rows(value, axis, bits):
+    for bit in bits:
+        both = join(value, axis, bit, 1)
+        value = both.reshape((-1,) + value.shape[1:])
+    return value
+
+
+def gather_small(value):
+    return join_rows(value[None], "dp", bits_of("dp"))
+
+
+def gather_rows(weight, flip):
+    parts = lax.axis_size("seq")
+    rows = weight.shape[0] // parts
+    share = lax.dynamic_slice_in_dim(weight, lax.axis_index("seq") * rows, rows, 0)
+    value = join_rows(share[None], "dp", bits_of("dp")[:-1])
+    owners = value.shape[0]
+    value = value[:, None]
+    bits = bits_of("seq")
+    for bit in bits[::-1] if flip else bits:
+        both = join(value, "seq", bit, 1 if flip else 2)
+        value = both.reshape((owners, -1) + value.shape[2:])
+    value = value.reshape((owners, parts * rows) + weight.shape[1:])
+    value = join_rows(value, "dp", [1])
+    return value.reshape((-1,) + weight.shape[1:])
+
+
+def reduce_first(value):
     owners = lax.axis_size("dp")
     parts = lax.axis_size("seq")
     rows = value.shape[0] // owners
     value = value.reshape((owners, parts, rows // parts) + value.shape[1:])
-    value = halve(value, "dp", 1)
+    return halve(value, "dp", 1)
+
+
+def reduce_rest(value):
+    owners = lax.axis_size("dp")
+    parts = lax.axis_size("seq")
     place = lax.axis_index("seq")
     total = lax.dynamic_index_in_dim(value, place, 1, keepdims=False)
     for other in range(1, parts):
@@ -161,8 +211,12 @@
     while bit < owners:
         total = halve(total, "dp", bit)
         bit *= 2
-    own = total[0].astype(BF16)
-    return lax.all_gather(own, "seq", axis=0, tiled=True).astype(F32)
+    own = join_rows(total.astype(BF16), "seq", bits_of("seq"))
+    return own.reshape((-1,) + own.shape[2:]).astype(F32)
+
+
+def reduce_owned(value):
+    return reduce_rest(reduce_first(value))
 
 
 def shards(
@@ -175,11 +229,12 @@
     packed = jnp.concatenate(
         [ln_gain, ln_bias, qv_bias, branch_bias, fc_bias.reshape(-1, share)], axis=0
     )
-    vectors = lax.all_gather(packed, "dp", axis=1, tiled=True).astype(F32)
+    lines = packed.shape[0]
+    vectors = gather_small(packed).transpose(1, 0, 2).reshape(lines, -1).astype(F32)
     full_qkv = lax.all_gather(w_qkv, "dp", axis=0, tiled=True)
     full_out = lax.all_gather(w_out, "dp", axis=0, tiled=True)
-    full_fc = lax.all_gather(w_fc, "dp", axis=0, tiled=True)
-    full_proj = lax.all_gather(w_proj, "dp", axis=0, tiled=True)
+    full_fc = gather_rows(w_fc, False)
+    full_proj = gather_rows(w_proj, True)
     gain_vals, shift_vals, qv_vals, branch_vals = (
         vectors[0:2], vectors[2:4], vectors[4:6], vectors[6:8],
     )
@@ -220,6 +275,9 @@
     grad_proj = dot(active, upstream, 0, 0)
     grad_fc = dot(second, grad_hidden, 0, 0)
     grad_out = dot(head_out, grad_branch, 1, 0)
+    early_proj, early_fc, seq_grad = lax.optimization_barrier(
+        (reduce_first(grad_proj), reduce_first(grad_fc), seq_grad)
+    )
     seq_dqkv = attend_backward(qkv, seq_heads, logs, seq_grad)
     grad_qkv = lax.all_to_all(seq_dqkv, "seq", split_axis=1, concat_axis=1, tiled=True)
     grad_projected = grad_qkv.reshape(3 * width, rows)
@@ -241,8 +299,8 @@
         ],
         axis=0,
     )
-    small = lax.psum(small, ("dp", "seq"))
-    small = lax.dynamic_slice_in_dim(small, lax.axis_index("dp") * share, share, 1)
+    small = small.reshape(lines, owners, share).transpose(1, 0, 2).reshape(-1, share)
+    small = reduce_owned(small)
     return (
         result.astype(BF16)[None],
         input_grad[None],
@@ -251,9 +309,9 @@
         reduce_owned(grad_w_qkv),
         small[4:6],
         reduce_owned(grad_out),
-        reduce_owned(grad_fc),
+        reduce_rest(early_fc),
         small[8:].reshape(-1),
-        reduce_owned(grad_proj),
+        reduce_rest(early_proj),
         small[6:8],
     )
 

time: 509 us -> 540 us (1.061)
  blocking collectives: 148 us -> 0 us
  waiting for transfers between devices: 131 us -> 247 us
  starting transfers between devices: 37 us -> 80.1 us
  other arithmetic: 24.9 us -> 50.9 us
  matrix products: 59.6 us -> 47.1 us
    ppermute x24 -> x53, waiting for transfers between devices: 47.3 us -> 204 us  [swap(): return lax.ppermute(value, axis, [(d, d ^ bit) for d in range(size)])]
    all_gather x5 -> x0, blocking collectives: 59.4 us -> none  [the longest x4 43.7 us: reduce_owned(): return lax.all_gather(own, 'seq', axis=0, tiled=True).astype(F32)]
    psum x1 -> x0, blocking collectives: 56.2 us -> none  [shards(): small = lax.psum(small, ('dp', 'seq'))]
    all_gather x2 -> x0, waiting for transfers between devices: 45.5 us -> none  [the longest x1 41.4 us: shards(): full_proj = lax.all_gather(w_proj, 'dp', axis=0, tiled=True)]
    ppermute x24 -> x53, starting transfers between devices: 24.1 us -> 62.9 us  [swap(): return lax.ppermute(value, axis, [(d, d ^ bit) for d in range(size)])]
    all_to_all x1 -> x0, blocking collectives: 32 us -> none  [shards(): lax.all_to_all(projected, 'seq', split_axis=1, concat_axis=1, tiled=True)]
    all_gather x1, waiting for transfers between devices: 26 us -> 0.02 us  [shards(): full_qkv = lax.all_gather(w_qkv, 'dp', axis=0, tiled=True)]
    all_to_all x1, waiting for transfers between devices: 0.01 us -> 22.8 us  [shards(): lax.all_to_all(seq_dqkv, 'seq', split_axis=1, concat_axis=1, tiled=True)]
  transfers between devices with their start and end apart: 31 -> 59, of which waited for: 12 -> 32; matrix products, arithmetic and copies ran while one was open for 20% -> 19% of each run, Pallas kernels for 7% -> 7%
where the time goes in v2:
time: 540 us; the launch traced here: 531 us
  waiting for transfers between devices  247 us (46%)
  starting transfers between devices  80.1 us (15%)
  local copies, waits for them, and re-layouts  53.8 us (10%)
  other arithmetic  50.9 us (9%)
  matrix products  47.1 us (9%)
  Pallas kernels  36.2 us (7%)
  between operations  15.7 us (3%)
    ppermute x53, waiting for transfers between devices, swap(): return lax.ppermute(value, axis, [(d, d ^ bit) for d in range(size)])  204 us
    ppermute x53, starting transfers between devices, swap(): return lax.ppermute(value, axis, [(d, d ^ bit) for d in range(size)])  62.9 us
    dot_general x12, matrix products, dot(): lax.dot_general(left, right, (((left_dim,), (right_dim,)), ((), ())), pre...  47.1 us
    pallas_call x1, Pallas kernels, attend_backward(): pl.pallas_call(partial(backward_kernel, blocks), grid=(heads,), in_specs=...  23.6 us
    all_to_all x1, waiting for transfers between devices, shards(): lax.all_to_all(seq_dqkv, 'seq', split_axis=1, concat_axis=1, tiled=True)  22.8 us
    another operation x30, other arithmetic, join(): return jnp.stack([first, second], axis=dim)  21.2 us
    all_to_all x1, waiting for transfers between devices, shards(): lax.all_to_all(projected, 'seq', split_axis=1, concat_axis=1, tiled=True)  18.1 us
    add x10, other arithmetic, halve(): return kept.astype(F32) + swap(sent.astype(BF16), axis, bit).astype(F32)  15.5 us
  transfers between devices with their start and end apart: 59, of which 32 were waited for; matrix products, arithmetic and copies ran while one was open for 19% of the time, Pallas kernels for 7%

profile of v2, /device:TPU:0, one launch (start us, length us, event | category | flops | bytes accessed | tf_op | source)
XLA Modules:
  0.0 530.6 jit_solution(14338598093002724179)
XLA Ops:
  8.2 4.1 collective-permute-start.3
  14.8 3.0 collective-permute-start.8
  17.8 5.7 %collective-permute-done.3 = bf16[1,24,3072]{2,1,0:T(8,128)(2,1)S(1)} collective-permute-done((bf16[1,24,3072]{2,1,0:T(8,128)(2,1)S(1)}, bf16[1,24,3072]{2,1,0:T(8,128)(2,1)S(1)}, u32[]{:S(2)}, u32[]{:S(2)}) %collective-permute-start.3) | collective-permute-done | bytes 147488 | tf_op jit(solution)/shard_map/ppermute | solution.py:138
  24.4 3.6 collective-permute-start.4
  28.0 4.1 collective-permute-done.8
  33.1 4.7 collective-permute-start.9
  37.8 16.2 %collective-permute-done.4 = bf16[2,24,3072]{2,1,0:T(8,128)(2,1)S(1)} collective-permute-done((bf16[2,24,3072]{2,1,0:T(8,128)(2,1)S(1)}, bf16[2,24,3072]{2,1,0:T(8,128)(2,1)S(1)}, u32[]{:S(2)}, u32[]{:S(2)}) %collective-permute-start.4) | collective-permute-done | bytes 294944 | tf_op jit(solution)/shard_map/ppermute | solution.py:138
  55.3 11.6 %collective-permute-done.9 = bf16[2,96,768]{2,1,0:T(8,128)(2,1)S(1)} collective-permute-done((bf16[2,96,768]{2,1,0:T(8,128)(2,1)S(1)}, bf16[2,96,768]{2,1,0:T(8,128)(2,1)S(1)}, u32[]{:S(2)}, u32[]{:S(2)}) %collective-permute-start.9) | collective-permute-done | bytes 294944 | tf_op jit(solution)/shard_map/ppermute | solution.py:138
  69.8 2.1 collective-permute-start.10
  72.4 36.4 %collective-permute-done.10 = bf16[4,1,96,768]{3,2,0,1:T(8,128)(2,1)S(1)} collective-permute-done((bf16[4,1,96,768]{3,2,0,1:T(8,128)(2,1)S(1)}, bf16[4,1,96,768]{3,2,0,1:T(8,128)(2,1)S(1)}, u32[]{:S(2)}, u32[]{:S(2)}) %collective-permute-start.10) | collective-permute-done | bytes 589856 | tf_op jit(solution)/shard_map/ppermute | solution.py:138
  114.1 20.5 %collective-permute-done.11 = bf16[4,2,96,768]{3,2,0,1:T(8,128)(2,1)S(1)} collective-permute-done((bf16[4,2,96,768]{3,2,0,1:T(8,128)(2,1)S(1)}, bf16[4,2,96,768]{3,2,0,1:T(8,128)(2,1)S(1)}, u32[]{:S(2)}, u32[]{:S(2)}) %collective-permute-start.11) | collective-permute-done | bytes 1179680 | tf_op jit(solution)/shard_map/ppermute | solution.py:138
  137.1 5.5 %fusion.19 = bf16[2304,512]{0,1:T(8,128)(2,1)} fusion(bf16[768,2304]{1,0:T(8,128)(2,1)} %all-gather.3.cloned.1.call-done, f32[2304]{0:T(1024)S(1)} %pad_maximum_fusion.8, bf16[1,512,768]{2,1,0:T(8,128)(2,1)S(1)} %copy-done.3, f32[768]{0:T(1024)S(1)} %add.359, f32[768]{0:T(1024)S(1)} %mul.188, f32[512]{0:T(512)S(1)} %fusion.77, ...), kind=kOutput, calls=%fused_computation.34 | convolution fusion | flops 1816657920 | bytes 6704128 | tf_op jit(solution)/shard_map/dot_general | solution.py:24
  142.6 2.8 copy.315
  147.2 4.5 all-to-all-start
  152.9 4.9 select_bitcast_fusion.3
  157.7 4.8 select_bitcast_fusion.1
  162.5 18.1 %all-to-all-done = bf16[3,4,192,512]{3,2,0,1:T(8,128)(2,1)} async-done(((bf16[3,4,192,512]{3,2,0,1:T(8,128)(2,1)}), bf16[3,4,192,512]{3,2,0,1:T(8,128)(2,1)}, u32[]{:S(2)}, u32[]{:S(2)}) %all-to-all-start) | async-done | bytes 2359328 | tf_op jit(solution)/shard_map/all_to_all | solution.py:248
  182.6 12.6 %attend_forward.1 = (bf16[4,192,512]{2,1,0:T(8,128)(2,1)}, f32[3,4,8,512]{3,2,1,0:T(8,128)S(1)}) custom-call(bf16[3,4,192,512]{3,2,1,0:T(8,128)(2,1)S(1)} %copy.317.qkv_ref), custom_call_target="tpu_custom_call" | custom-call | flops 8053063680 | bytes 4718592 | tf_op jit(solution)/shard_map/attend_forward/pallas_call | solution.py:96
  195.2 4.7 all-to-all-start.1
  199.9 2.8 pad_maximum_fusion.1
  202.7 2.7 copy.324
  207.2 2.7 copy.320
  211.0 2.6 fusion.96
  214.0 5.9 %fusion.14 = (bf16[3072,512]{0,1:T(8,128)(2,1)}, f32[512,3072]{1,0:T(8,128)S(1)}) fusion(f32[3072]{0:T(1024)S(1)} %add.375, bf16[768,3072]{1,0:T(8,128)(2,1)S(1)} %bitcast.451, f32[512,768]{1,0:T(8,128)S(1)} %get-tuple-element.109, f32[768]{0:T(1024)S(1)} %add.369, f32[768]{0:T(1024)S(1)} %mul.194, f32[512]{0:T(512)S(1)} %fusion.78, ...), kind=kOutput, calls=%fused_computation.17 | convolution fusion | flops 2433613824 | bytes 15751168 | tf_op jit(solution)/shard_map/dot_general | solution.py:24
  219.9 6.5 %convert_reduce_fusion = (f32[3072]{0:T(1024)S(1)}, bf16[512,3072]{1,0:T(8,128)(2,1)S(1)}) fusion(f32[512,3072]{1,0:T(8,128)S(1)} %get-tuple-element.111, f32[3072]{0:T(1024)S(1)} %add.375, bf16[3072,768]{1,0:T(8,128)(2,1)S(1)} %bitcast.447, bf16[1,512,768]{2,1,0:T(8,128)(2,1)S(1)} %copy-done.17), kind=kOutput, calls=%fused_computation.23 | convolution fusion | flops 2452091904 | bytes 14966784 | tf_op jit(solution)/shard_map/dot_general | solution.py:24
  226.4 3.0 multiply_reduce_fusion
  230.5 2.4 fusion.47
  234.5 5.8 %fusion.89 = f32[768,3072]{1,0:T(8,128)} fusion(bf16[512,3072]{1,0:T(8,128)(2,1)S(1)} %get-tuple-element.115, f32[512,768]{1,0:T(8,128)S(1)} %get-tuple-element.109, f32[768]{0:T(1024)S(1)} %add.369, f32[768]{0:T(1024)S(1)} %mul.194, f32[512]{0:T(512)S(1)} %fusion.78, f32[512]{0:T(512)S(1)} %broadcast_multiply_fusion), kind=kOutput, calls=%fused_computation.255 | convolution fusion | flops 2417885184 | bytes 14166016 | tf_op jit(solution)/shard_map/dot_general | solution.py:24
  240.3 4.7 copy.325
  245.0 4.2 fusion.22
  254.7 2.6 fusion.49
  258.0 3.1 collective-permute-done.34
  264.4 2.5 collective-permute-done.35
  267.0 5.8 %collective-permute-start.36 = (bf16[1,24,768]{2,1,0:T(8,128)(2,1)S(1)}, bf16[1,24,768]{2,1,0:T(8,128)(2,1)S(1)}, u32[]{:S(2)}, u32[]{:S(2)}) collective-permute-start(bf16[1,24,768]{2,1,0:T(8,128)(2,1)S(1)} %dynamic-slice_convert_fusion.18), channel_id=1, source_target_pairs={{0,4},{1,5},{2,6},{3,7},{4,0},{5,1},{6,2},{7,3},{8,12},{9,13},{10,... | collective-permute-start | bytes 110600 | tf_op jit(solution)/shard_map/ppermute | solution.py:138
  272.9 4.9 fusion.37
  280.6 3.7 all-to-all-start.2
  284.4 2.1 collective-permute-start.38
  286.5 6.4 %bitcast_add_fusion = f32[4,4,24,3072]{3,2,1,0:T(8,128)} fusion(bf16[4,4,24,3072]{3,2,1,0:T(8,128)(2,1)} %collective-permute-done.14, f32[4,2,4,24,3072]{4,3,2,1,0:T(8,128)} %bitcast.444, s32[]{:T(128)S(6)} %select_n.547), kind=kLoop, calls=%fused_computation.28 | loop fusion | flops 2359296 | bytes 11796484 | tf_op jit(solution)/shard_map/add | solution.py:146
  293.6 4.6 bitcast_add_fusion.1
  310.2 8.8 %collective-permute-done.41 = bf16[4,24,3072]{2,1,0:T(8,128)(2,1)S(1)} collective-permute-done((bf16[4,24,3072]{2,1,0:T(8,128)(2,1)S(1)}, bf16[4,24,3072]{2,1,0:T(8,128)(2,1)S(1)}, u32[]{:S(2)}, u32[]{:S(2)}) %collective-permute-start.41) | collective-permute-done | bytes 589856 | tf_op jit(solution)/shard_map/ppermute | solution.py:138
  320.4 11.2 %collective-permute-done.39 = bf16[4,24,3072]{2,1,0:T(8,128)(2,1)S(1)} collective-permute-done((bf16[4,24,3072]{2,1,0:T(8,128)(2,1)S(1)}, bf16[4,24,3072]{2,1,0:T(8,128)(2,1)S(1)}, u32[]{:S(2)}, u32[]{:S(2)}) %collective-permute-start.39) | collective-permute-done | bytes 589856 | tf_op jit(solution)/shard_map/ppermute | solution.py:138
  335.3 9.0 %collective-permute-done.48 = bf16[4,96,768]{2,1,0:T(8,128)(2,1)S(1)} collective-permute-done((bf16[4,96,768]{2,1,0:T(8,128)(2,1)S(1)}, bf16[4,96,768]{2,1,0:T(8,128)(2,1)S(1)}, u32[]{:S(2)}, u32[]{:S(2)}) %collective-permute-start.48) | collective-permute-done | bytes 589856 | tf_op jit(solution)/shard_map/ppermute | solution.py:138
  344.3 10.4 %collective-permute-done.46 = bf16[4,96,768]{2,1,0:T(8,128)(2,1)S(1)} collective-permute-done((bf16[4,96,768]{2,1,0:T(8,128)(2,1)S(1)}, bf16[4,96,768]{2,1,0:T(8,128)(2,1)S(1)}, u32[]{:S(2)}, u32[]{:S(2)}) %collective-permute-start.46) | collective-permute-done | bytes 589856 | tf_op jit(solution)/shard_map/ppermute | solution.py:138
  355.5 11.5 %collective-permute-done.49 = bf16[2,96,768]{2,1,0:T(8,128)(2,1)S(1)} collective-permute-done((bf16[2,96,768]{2,1,0:T(8,128)(2,1)S(1)}, bf16[2,96,768]{2,1,0:T(8,128)(2,1)S(1)}, u32[]{:S(2)}, u32[]{:S(2)}) %collective-permute-start.49) | collective-permute-done | bytes 294944 | tf_op jit(solution)/shard_map/ppermute | solution.py:138
  368.8 6.3 %collective-permute-done.50 = bf16[1,96,768]{2,1,0:T(8,128)(2,1)S(1)} collective-permute-done((bf16[1,96,768]{2,1,0:T(8,128)(2,1)S(1)}, bf16[1,96,768]{2,1,0:T(8,128)(2,1)S(1)}, u32[]{:S(2)}, u32[]{:S(2)}) %collective-permute-start.50) | collective-permute-done | bytes 147488 | tf_op jit(solution)/shard_map/ppermute | solution.py:138
  378.1 2.6 collective-permute-done.51
  382.0 23.6 %attend_backward.1 = bf16[3,4,192,512]{3,2,1,0:T(8,128)(2,1)S(1)} custom-call(bf16[3,4,192,512]{3,2,1,0:T(8,128)(2,1)S(1)} %copy.317.qkv_ref, bf16[4,192,512]{2,1,0:T(8,128)(2,1)} %get-tuple-element.16.out_ref, f32[3,4,8,512]{3,2,1,0:T(8,128)S(1)} %get-tuple-element.17.log_ref, bf16[4,192,512]{2,1,0:T(8,128)(2,1)S(1)} %all-to-all-done.2.grad_ref), custom_call_target="tpu_custom_call" | custom-call | flops 20132659200 | bytes 14155776 | tf_op jit(solution)/shard_map/attend_backward/pallas_call | solution.py:118
  407.2 4.3 all-to-all-start.3
  415.6 22.8 %all-to-all-done.3 = bf16[3,4,192,512]{3,2,0,1:T(8,128)(2,1)S(1)} async-done(((bf16[3,4,192,512]{3,2,0,1:T(8,128)(2,1)}), bf16[3,4,192,512]{3,2,0,1:T(8,128)(2,1)S(1)}, u32[]{:S(2)}, u32[]{:S(2)}) %all-to-all-start.3) | async-done | bytes 2359328 | tf_op jit(solution)/shard_map/all_to_all | solution.py:282
  438.5 2.7 copy-done.29
  441.2 3.4 fusion.91
  444.7 2.3 fusion.34
  447.0 3.1 fusion.86
  451.5 3.7 fusion.97
  455.2 2.8 copy-done
  461.1 2.1 collective-permute-done.15
  466.9 2.4 collective-permute-done.18
  470.0 3.5 collective-permute-done.19
  473.7 2.9 bitcast_add_fusion.2
  482.1 15.0 %collective-permute-done.21 = bf16[1,3,96]{2,0,1:T(2,128)(2,1)S(1)} collective-permute-done((bf16[1,3,96]{2,0,1:T(2,128)(2,1)S(1)}, bf16[1,3,96]{2,0,1:T(2,128)(2,1)S(1)}, u32[]{:S(2)}, u32[]{:S(2)}) %collective-permute-start.21) | collective-permute-done | bytes 608 | tf_op jit(solution)/shard_map/ppermute | solution.py:138
  499.4 5.2 collective-permute-done.27
  506.2 5.1 collective-permute-done.28
  513.6 2.6 collective-permute-done.29
  518.4 3.8 collective-permute-done.30
  (315 shorter events, 95.0 us)
Async XLA Ops:
  7.2 129.9 %all-gather.3.cloned.1.call-start = ((), (), s32[]{:S(2)}) async-start(), calls=%async_computation.4 | async-start | bytes 3981312 | tf_op jit(solution)/shard_map/all_gather | solution.py:234
  8.2 15.3 %collective-permute-start.3 = (bf16[1,24,3072]{2,1,0:T(8,128)(2,1)S(1)}, bf16[1,24,3072]{2,1,0:T(8,128)(2,1)S(1)}, u32[]{:S(2)}, u32[]{:S(2)}) collective-permute-start(bf16[1,24,3072]{2,1,0:T(8,128)(2,1)S(1)} %dynamic-slice_bitcast_fusion.1), channel_id=1, source_target_pairs={{0,4},{1,5},{2,6},{3,7},{4,0},{5,1},{6,2},{7,3},{8,12},{9,13},{10,... | collective-permute-start | bytes 442376 | tf_op jit(solution)/shard_map/ppermute | solution.py:138
  13.8 58.5 %collective-permute-start = (bf16[1,12,96]{2,1,0:T(8,128)(2,1)S(1)}, bf16[1,12,96]{2,1,0:T(8,128)(2,1)S(1)}, u32[]{:S(2)}, u32[]{:S(2)}) collective-permute-start(bf16[1,12,96]{2,1,0:T(8,128)(2,1)S(1)} %bitcast.481), channel_id=1, source_target_pairs={{0,4},{1,5},{2,6},{3,7},{4,0},{5,1},{6,2},{7,3},{8,12},{9,13},{10,... | collective-permute-start | bytes 6920 | tf_op jit(solution)/shard_map/ppermute | solution.py:138
  14.8 17.3 %collective-permute-start.8 = (bf16[1,96,768]{2,1,0:T(8,128)(2,1)S(1)}, bf16[1,96,768]{2,1,0:T(8,128)(2,1)S(1)}, u32[]{:S(2)}, u32[]{:S(2)}) collective-permute-start(bf16[1,96,768]{2,1,0:T(8,128)(2,1)S(1)} %dynamic-slice_bitcast_fusion), channel_id=1, source_target_pairs={{0,4},{1,5},{2,6},{3,7},{4,0},{5,1},{6,2},{7,3},{8,12},{9,13},{10,... | collective-permute-start | bytes 442376 | tf_op jit(solution)/shard_map/ppermute | solution.py:138
  17.8 37.3 %copy-start.3 = (bf16[1,512,768]{2,1,0:T(8,128)(2,1)S(1)}, bf16[1,512,768]{2,1,0:T(8,128)(2,1)}, u32[]{:S(2)}) copy-start(bf16[1,512,768]{2,1,0:T(8,128)(2,1)} %param.11) | copy-start | bytes 2359300
  24.4 29.6 %collective-permute-start.4 = (bf16[2,24,3072]{2,1,0:T(8,128)(2,1)S(1)}, bf16[2,24,3072]{2,1,0:T(8,128)(2,1)S(1)}, u32[]{:S(2)}, u32[]{:S(2)}) collective-permute-start(bf16[2,24,3072]{2,1,0:T(8,128)(2,1)S(1)} %maximum_bitcast_fusion.2), channel_id=1, source_target_pairs={{0,2},{1,3},{2,0},{3,1},{4,6},{5,7},{6,4},{7,5},{8,10},{9,11},{10,... | collective-permute-start | bytes 884744 | tf_op jit(solution)/shard_map/ppermute | solution.py:138
  33.1 33.7 %collective-permute-start.9 = (bf16[2,96,768]{2,1,0:T(8,128)(2,1)S(1)}, bf16[2,96,768]{2,1,0:T(8,128)(2,1)S(1)}, u32[]{:S(2)}, u32[]{:S(2)}) collective-permute-start(bf16[2,96,768]{2,1,0:T(8,128)(2,1)S(1)} %maximum_bitcast_fusion.3), channel_id=1, source_target_pairs={{0,2},{1,3},{2,0},{3,1},{4,6},{5,7},{6,4},{7,5},{8,10},{9,11},{10,... | collective-permute-start | bytes 884744 | tf_op jit(solution)/shard_map/ppermute | solution.py:138
  54.1 14.4 %collective-permute-start.5 = (bf16[4,1,24,3072]{3,2,0,1:T(8,128)(2,1)S(1)}, bf16[4,1,24,3072]{3,2,0,1:T(8,128)(2,1)S(1)}, u32[]{:S(2)}, u32[]{:S(2)}) collective-permute-start(bf16[4,1,24,3072]{3,2,0,1:T(8,128)(2,1)S(1)} %bitcast.462), channel_id=1, source_target_pairs={{0,16},{8,24},{16,0},{24,8},{1,17},{9,25},{17,1},{25,9},{2,18},{10... | collective-permute-start | bytes 1769480 | tf_op jit(solution)/shard_map/ppermute | solution.py:138
  69.8 40.5 %collective-permute-start.6 = (bf16[4,2,24,3072]{3,2,0,1:T(8,128)(2,1)}, bf16[4,2,24,3072]{3,2,0,1:T(8,128)(2,1)}, u32[]{:S(2)}, u32[]{:S(2)}) collective-permute-start(bf16[4,2,24,3072]{3,2,0,1:T(8,128)(2,1)} %maximum_bitcast_fusion), channel_id=1, source_target_pairs={{0,8},{8,0},{16,24},{24,16},{1,9},{9,1},{17,25},{25,17},{2,10},{10... | collective-permute-start | bytes 3538952 | tf_op jit(solution)/shard_map/ppermute | solution.py:138
  69.8 39.0 %collective-permute-start.10 = (bf16[4,1,96,768]{3,2,0,1:T(8,128)(2,1)S(1)}, bf16[4,1,96,768]{3,2,0,1:T(8,128)(2,1)S(1)}, u32[]{:S(2)}, u32[]{:S(2)}) collective-permute-start(bf16[4,1,96,768]{3,2,0,1:T(8,128)(2,1)S(1)} %bitcast.463), channel_id=1, source_target_pairs={{0,8},{8,0},{16,24},{24,16},{1,9},{9,1},{17,25},{25,17},{2,10},{10... | collective-permute-start | bytes 1769480 | tf_op jit(solution)/shard_map/ppermute | solution.py:138
  72.3 41.2 %collective-permute-start.1 = (bf16[2,12,96]{2,1,0:T(8,128)(2,1)S(1)}, bf16[2,12,96]{2,1,0:T(8,128)(2,1)S(1)}, u32[]{:S(2)}, u32[]{:S(2)}) collective-permute-start(bf16[2,12,96]{2,1,0:T(8,128)(2,1)S(1)} %maximum_bitcast_fusion.8), channel_id=1, source_target_pairs={{0,2},{1,3},{2,0},{3,1},{4,6},{5,7},{6,4},{7,5},{8,10},{9,11},{10,... | collective-permute-start | bytes 13832 | tf_op jit(solution)/shard_map/ppermute | solution.py:138
  109.1 25.6 %collective-permute-start.11 = (bf16[4,2,96,768]{3,2,0,1:T(8,128)(2,1)S(1)}, bf16[4,2,96,768]{3,2,0,1:T(8,128)(2,1)S(1)}, u32[]{:S(2)}, u32[]{:S(2)}) collective-permute-start(bf16[4,2,96,768]{3,2,0,1:T(8,128)(2,1)S(1)} %maximum_bitcast_fusion.1), channel_id=1, source_target_pairs={{0,16},{8,24},{16,0},{24,8},{1,17},{9,25},{17,1},{25,9},{2,18},{10... | collective-permute-start | bytes 3538952 | tf_op jit(solution)/shard_map/ppermute | solution.py:138
  113.5 39.4 %collective-permute-start.7 = (bf16[4,96,3072]{2,1,0:T(8,128)(2,1)}, bf16[4,96,3072]{2,1,0:T(8,128)(2,1)}, u32[]{:S(2)}, u32[]{:S(2)}) collective-permute-start(bf16[4,96,3072]{2,1,0:T(8,128)(2,1)} %bitcast.29), channel_id=1, source_target_pairs={{0,1},{1,0},{2,3},{3,2},{4,5},{5,4},{6,7},{7,6},{8,9},{9,8},{10,11... | collective-permute-start | bytes 7077896 | tf_op jit(solution)/shard_map/ppermute | solution.py:138
  113.6 23.1 %collective-permute-start.2 = (bf16[4,12,96]{2,0,1:T(4,128)(2,1)S(1)}, bf16[4,12,96]{2,0,1:T(4,128)(2,1)S(1)}, u32[]{:S(2)}, u32[]{:S(2)}) collective-permute-start(bf16[4,12,96]{2,0,1:T(4,128)(2,1)S(1)} %bitcast.475), channel_id=1, source_target_pairs={{0,1},{1,0},{2,3},{3,2},{4,5},{5,4},{6,7},{7,6},{8,9},{9,8},{10,11... | collective-permute-start | bytes 27656 | tf_op jit(solution)/shard_map/ppermute | solution.py:138
  136.7 21.1 %collective-permute-start.12 = (bf16[4,384,768]{2,1,0:T(8,128)(2,1)}, bf16[4,384,768]{2,1,0:T(8,128)(2,1)}, u32[]{:S(2)}, u32[]{:S(2)}) collective-permute-start(bf16[4,384,768]{2,1,0:T(8,128)(2,1)} %bitcast.47), channel_id=1, source_target_pairs={{0,1},{1,0},{2,3},{3,2},{4,5},{5,4},{6,7},{7,6},{8,9},{9,8},{10,11... | collective-permute-start | bytes 7077896 | tf_op jit(solution)/shard_map/ppermute | solution.py:138
  147.2 33.4 %all-to-all-start = ((bf16[3,4,192,512]{3,2,0,1:T(8,128)(2,1)}), bf16[3,4,192,512]{3,2,0,1:T(8,128)(2,1)}, u32[]{:S(2)}, u32[]{:S(2)}) async-start(bf16[3,4,192,512]{3,2,0,1:T(8,128)(2,1)} %copy.316), calls=%async_computation | async-start | bytes 4718592 | tf_op jit(solution)/shard_map/all_to_all | solution.py:248
  151.7 58.2 %all-gather.5.cloned.1.call-start = ((), (), s32[]{:S(2)}) async-start(), calls=%async_computation.5 | async-start | bytes 1327104 | tf_op jit(solution)/shard_map/all_gather | solution.py:235
  195.2 15.8 %all-to-all-start.1 = ((bf16[4,192,512]{2,1,0:T(8,128)(2,1)}), bf16[4,192,512]{2,1,0:T(8,128)(2,1)}, u32[]{:S(2)}, u32[]{:S(2)}) async-start(bf16[4,192,512]{2,1,0:T(8,128)(2,1)} %get-tuple-element.16.out_ref), calls=%async_computation.1 | async-start | bytes 1572864 | tf_op jit(solution)/shard_map/all_to_all | solution.py:250
  213.6 20.8 %copy-start.11 = (f32[512,768]{1,0:T(8,128)}, f32[512,768]{1,0:T(8,128)S(1)}, u32[]{:S(2)}) copy-start(f32[512,768]{1,0:T(8,128)S(1)} %get-tuple-element.109) | copy-start | bytes 4718596
  234.5 15.2 %collective-permute-start.31 = (bf16[4,4,24,768]{3,2,1,0:T(8,128)(2,1)}, bf16[4,4,24,768]{3,2,1,0:T(8,128)(2,1)}, u32[]{:S(2)}, u32[]{:S(2)}) collective-permute-start(bf16[4,4,24,768]{3,2,1,0:T(8,128)(2,1)} %fusion.52), channel_id=1, source_target_pairs={{0,1},{1,0},{2,3},{3,2},{4,5},{5,4},{6,7},{7,6},{8,9},{9,8},{10,11... | collective-permute-start | bytes 1769480 | tf_op jit(solution)/shard_map/ppermute | solution.py:138
  249.2 37.3 %collective-permute-start.14 = (bf16[4,4,24,3072]{3,2,1,0:T(8,128)(2,1)}, bf16[4,4,24,3072]{3,2,1,0:T(8,128)(2,1)}, u32[]{:S(2)}, u32[]{:S(2)}) collective-permute-start(bf16[4,4,24,3072]{3,2,1,0:T(8,128)(2,1)} %fusion.22), channel_id=1, source_target_pairs={{0,1},{1,0},{2,3},{3,2},{4,5},{5,4},{6,7},{7,6},{8,9},{9,8},{10,11... | collective-permute-start | bytes 7077896 | tf_op jit(solution)/shard_map/ppermute | solution.py:138
  249.7 23.2 %slice-start.2 = ((s8[4718592]{0:T(1024)(128)(4,1)}), s8[4194304]{0:T(1024)(128)(4,1)S(1)}, s32[]{:S(2)}) async-start(s8[4718592]{0:T(1024)(128)(4,1)} %bitcast.448), calls=%async_computation.8 | async-start | bytes 8388608
  251.1 21.7 %slice-start.4 = ((s8[6291456]{0:T(1024)(128)(4,1)}), s8[4194304]{0:T(1024)(128)(4,1)S(1)}, s32[]{:S(2)}) async-start(s8[6291456]{0:T(1024)(128)(4,1)} %bitcast.488), calls=%async_computation.10 | async-start | bytes 8388608
  251.2 6.8 %collective-permute-start.32 = (bf16[4,24,768]{2,1,0:T(8,128)(2,1)S(1)}, bf16[4,24,768]{2,1,0:T(8,128)(2,1)S(1)}, u32[]{:S(2)}, u32[]{:S(2)}) collective-permute-start(bf16[4,24,768]{2,1,0:T(8,128)(2,1)S(1)} %get-tuple-element.49), channel_id=1, source_target_pairs={{0,8},{8,0},{16,24},{24,16},{1,9},{9,1},{17,25},{25,17},{2,10},{10... | collective-permute-start | bytes 442376 | tf_op jit(solution)/shard_map/ppermute | solution.py:138
  252.7 8.4 %collective-permute-start.34 = (bf16[4,24,768]{2,1,0:T(8,128)(2,1)S(1)}, bf16[4,24,768]{2,1,0:T(8,128)(2,1)S(1)}, u32[]{:S(2)}, u32[]{:S(2)}) collective-permute-start(bf16[4,24,768]{2,1,0:T(8,128)(2,1)S(1)} %get-tuple-element.50), channel_id=1, source_target_pairs={{0,24},{8,16},{16,8},{24,0},{1,25},{9,17},{17,9},{25,1},{2,26},{10... | collective-permute-start | bytes 442376 | tf_op jit(solution)/shard_map/ppermute | solution.py:138
  254.1 8.3 %collective-permute-start.33 = (bf16[4,24,768]{2,1,0:T(8,128)(2,1)S(1)}, bf16[4,24,768]{2,1,0:T(8,128)(2,1)S(1)}, u32[]{:S(2)}, u32[]{:S(2)}) collective-permute-start(bf16[4,24,768]{2,1,0:T(8,128)(2,1)S(1)} %get-tuple-element.51), channel_id=1, source_target_pairs={{0,16},{8,24},{16,0},{24,8},{1,17},{9,25},{17,1},{25,9},{2,18},{10... | collective-permute-start | bytes 442376 | tf_op jit(solution)/shard_map/ppermute | solution.py:138
  262.5 4.4 collective-permute-start.35
  264.4 28.5 %collective-permute-start.13 = (bf16[4,4,96,768]{3,2,1,0:T(8,128)(2,1)}, bf16[4,4,96,768]{3,2,1,0:T(8,128)(2,1)}, u32[]{:S(2)}, u32[]{:S(2)}) collective-permute-start(bf16[4,4,96,768]{3,2,1,0:T(8,128)(2,1)} %fusion.21), channel_id=1, source_target_pairs={{0,1},{1,0},{2,3},{3,2},{4,5},{5,4},{6,7},{7,6},{8,9},{9,8},{10,11... | collective-permute-start | bytes 7077896 | tf_op jit(solution)/shard_map/ppermute | solution.py:138
  267.0 10.7 %collective-permute-start.36 = (bf16[1,24,768]{2,1,0:T(8,128)(2,1)S(1)}, bf16[1,24,768]{2,1,0:T(8,128)(2,1)S(1)}, u32[]{:S(2)}, u32[]{:S(2)}) collective-permute-start(bf16[1,24,768]{2,1,0:T(8,128)(2,1)S(1)} %dynamic-slice_convert_fusion.18), channel_id=1, source_target_pairs={{0,4},{1,5},{2,6},{3,7},{4,0},{5,1},{6,2},{7,3},{8,12},{9,13},{10,... | collective-permute-start | bytes 110600 | tf_op jit(solution)/shard_map/ppermute | solution.py:138
  277.8 6.6 %collective-permute-start.37 = (bf16[1,24,768]{2,1,0:T(8,128)(2,1)S(1)}, bf16[1,24,768]{2,1,0:T(8,128)(2,1)S(1)}, u32[]{:S(2)}, u32[]{:S(2)}) collective-permute-start(bf16[1,24,768]{2,1,0:T(8,128)(2,1)S(1)} %add_convert_fusion.6), channel_id=1, source_target_pairs={{0,16},{8,24},{16,0},{24,8},{1,17},{9,25},{17,1},{25,9},{2,18},{10... | collective-permute-start | bytes 110600 | tf_op jit(solution)/shard_map/ppermute | solution.py:138
  280.6 17.6 %all-to-all-start.2 = ((bf16[4,192,512]{2,1,0:T(8,128)(2,1)}), bf16[4,192,512]{2,1,0:T(8,128)(2,1)S(1)}, u32[]{:S(2)}, u32[]{:S(2)}) async-start(bf16[4,192,512]{2,1,0:T(8,128)(2,1)} %bitcast.459), calls=%async_computation.2 | async-start | bytes 1572864 | tf_op jit(solution)/shard_map/all_to_all | solution.py:271
  284.4 20.8 %collective-permute-start.38 = (bf16[2,24,768]{2,1,0:T(8,128)(2,1)S(1)}, bf16[2,24,768]{2,1,0:T(8,128)(2,1)}, u32[]{:S(2)}, u32[]{:S(2)}) collective-permute-start(bf16[2,24,768]{2,1,0:T(8,128)(2,1)S(1)} %maximum_bitcast_fusion.7), channel_id=1, source_target_pairs={{0,8},{8,0},{16,24},{24,16},{1,9},{9,1},{17,25},{25,17},{2,10},{10... | collective-permute-start | bytes 221192 | tf_op jit(solution)/shard_map/ppermute | solution.py:138
  301.7 17.3 %collective-permute-start.41 = (bf16[4,24,3072]{2,1,0:T(8,128)(2,1)S(1)}, bf16[4,24,3072]{2,1,0:T(8,128)(2,1)S(1)}, u32[]{:S(2)}, u32[]{:S(2)}) collective-permute-start(bf16[4,24,3072]{2,1,0:T(8,128)(2,1)S(1)} %fusion.55), channel_id=1, source_target_pairs={{0,24},{8,16},{16,8},{24,0},{1,25},{9,17},{17,9},{25,1},{2,26},{10... | collective-permute-start | bytes 1769480 | tf_op jit(solution)/shard_map/ppermute | solution.py:138
  303.2 28.4 %collective-permute-start.39 = (bf16[4,24,3072]{2,1,0:T(8,128)(2,1)S(1)}, bf16[4,24,3072]{2,1,0:T(8,128)(2,1)S(1)}, u32[]{:S(2)}, u32[]{:S(2)}) collective-permute-start(bf16[4,24,3072]{2,1,0:T(8,128)(2,1)S(1)} %get-tuple-element.43), channel_id=1, source_target_pairs={{0,8},{8,0},{16,24},{24,16},{1,9},{9,1},{17,25},{25,17},{2,10},{10... | collective-permute-start | bytes 1769480 | tf_op jit(solution)/shard_map/ppermute | solution.py:138
  304.7 27.0 %collective-permute-start.40 = (bf16[4,24,3072]{2,1,0:T(8,128)(2,1)S(1)}, bf16[4,24,3072]{2,1,0:T(8,128)(2,1)S(1)}, u32[]{:S(2)}, u32[]{:S(2)}) collective-permute-start(bf16[4,24,3072]{2,1,0:T(8,128)(2,1)S(1)} %get-tuple-element.44), channel_id=1, source_target_pairs={{0,16},{8,24},{16,0},{24,8},{1,17},{9,25},{17,1},{25,9},{2,18},{10... | collective-permute-start | bytes 1769480 | tf_op jit(solution)/shard_map/ppermute | solution.py:138
  307.0 37.3 %collective-permute-start.48 = (bf16[4,96,768]{2,1,0:T(8,128)(2,1)S(1)}, bf16[4,96,768]{2,1,0:T(8,128)(2,1)S(1)}, u32[]{:S(2)}, u32[]{:S(2)}) collective-permute-start(bf16[4,96,768]{2,1,0:T(8,128)(2,1)S(1)} %fusion.58), channel_id=1, source_target_pairs={{0,24},{8,16},{16,8},{24,0},{1,25},{9,17},{17,9},{25,1},{2,26},{10... | collective-permute-start | bytes 1769480 | tf_op jit(solution)/shard_map/ppermute | solution.py:138
  308.6 46.0 %collective-permute-start.46 = (bf16[4,96,768]{2,1,0:T(8,128)(2,1)S(1)}, bf16[4,96,768]{2,1,0:T(8,128)(2,1)S(1)}, u32[]{:S(2)}, u32[]{:S(2)}) collective-permute-start(bf16[4,96,768]{2,1,0:T(8,128)(2,1)S(1)} %get-tuple-element.41), channel_id=1, source_target_pairs={{0,8},{8,0},{16,24},{24,16},{1,9},{9,1},{17,25},{25,17},{2,10},{10... | collective-permute-start | bytes 1769480 | tf_op jit(solution)/shard_map/ppermute | solution.py:138
  319.0 35.7 %collective-permute-start.47 = (bf16[4,96,768]{2,1,0:T(8,128)(2,1)S(1)}, bf16[4,96,768]{2,1,0:T(8,128)(2,1)S(1)}, u32[]{:S(2)}, u32[]{:S(2)}) collective-permute-start(bf16[4,96,768]{2,1,0:T(8,128)(2,1)S(1)} %get-tuple-element.42), channel_id=1, source_target_pairs={{0,16},{8,24},{16,0},{24,8},{1,17},{9,25},{17,1},{25,9},{2,18},{10... | collective-permute-start | bytes 1769480 | tf_op jit(solution)/shard_map/ppermute | solution.py:138
  333.3 21.8 %collective-permute-start.42 = (bf16[2,24,3072]{2,1,0:T(8,128)(2,1)S(1)}, bf16[2,24,3072]{2,1,0:T(8,128)(2,1)S(1)}, u32[]{:S(2)}, u32[]{:S(2)}) collective-permute-start(bf16[2,24,3072]{2,1,0:T(8,128)(2,1)S(1)} %fusion.63), channel_id=1, source_target_pairs={{0,2},{1,3},{2,0},{3,1},{4,6},{5,7},{6,4},{7,5},{8,10},{9,11},{10,... | collective-permute-start | bytes 884744 | tf_op jit(solution)/shard_map/ppermute | solution.py:138
  355.0 12.1 %collective-permute-start.49 = (bf16[2,96,768]{2,1,0:T(8,128)(2,1)S(1)}, bf16[2,96,768]{2,1,0:T(8,128)(2,1)S(1)}, u32[]{:S(2)}, u32[]{:S(2)}) collective-permute-start(bf16[2,96,768]{2,1,0:T(8,128)(2,1)S(1)} %fusion.62), channel_id=1, source_target_pairs={{0,2},{1,3},{2,0},{3,1},{4,6},{5,7},{6,4},{7,5},{8,10},{9,11},{10,... | collective-permute-start | bytes 884744 | tf_op jit(solution)/shard_map/ppermute | solution.py:138
  355.2 12.0 %collective-permute-start.43 = (bf16[1,24,3072]{2,1,0:T(8,128)(2,1)S(1)}, bf16[1,24,3072]{2,1,0:T(8,128)(2,1)S(1)}, u32[]{:S(2)}, u32[]{:S(2)}) collective-permute-start(bf16[1,24,3072]{2,1,0:T(8,128)(2,1)S(1)} %dynamic-slice_convert_fusion.14), channel_id=1, source_target_pairs={{0,4},{1,5},{2,6},{3,7},{4,0},{5,1},{6,2},{7,3},{8,12},{9,13},{10,... | collective-permute-start | bytes 442376 | tf_op jit(solution)/shard_map/ppermute | solution.py:138
  367.1 7.9 %collective-permute-start.50 = (bf16[1,96,768]{2,1,0:T(8,128)(2,1)S(1)}, bf16[1,96,768]{2,1,0:T(8,128)(2,1)S(1)}, u32[]{:S(2)}, u32[]{:S(2)}) collective-permute-start(bf16[1,96,768]{2,1,0:T(8,128)(2,1)S(1)} %dynamic-slice_convert_fusion.13), channel_id=1, source_target_pairs={{0,4},{1,5},{2,6},{3,7},{4,0},{5,1},{6,2},{7,3},{8,12},{9,13},{10,... | collective-permute-start | bytes 442376 | tf_op jit(solution)/shard_map/ppermute | solution.py:138
  367.3 9.5 %collective-permute-start.44 = (bf16[1,24,3072]{2,1,0:T(8,128)(2,1)S(1)}, bf16[1,24,3072]{2,1,0:T(8,128)(2,1)S(1)}, u32[]{:S(2)}, u32[]{:S(2)}) collective-permute-start(bf16[1,24,3072]{2,1,0:T(8,128)(2,1)S(1)} %add_convert_fusion.4), channel_id=1, source_target_pairs={{0,16},{8,24},{16,0},{24,8},{1,17},{9,25},{17,1},{25,9},{2,18},{10... | collective-permute-start | bytes 442376 | tf_op jit(solution)/shard_map/ppermute | solution.py:138
  375.1 5.6 %collective-permute-start.51 = (bf16[1,96,768]{2,1,0:T(8,128)(2,1)S(1)}, bf16[1,96,768]{2,1,0:T(8,128)(2,1)S(1)}, u32[]{:S(2)}, u32[]{:S(2)}) collective-permute-start(bf16[1,96,768]{2,1,0:T(8,128)(2,1)S(1)} %add_convert_fusion.3), channel_id=1, source_target_pairs={{0,16},{8,24},{16,0},{24,8},{1,17},{9,25},{17,1},{25,9},{2,18},{10... | collective-permute-start | bytes 442376 | tf_op jit(solution)/shard_map/ppermute | solution.py:138
  377.5 35.8 %collective-permute-start.45 = (bf16[2,24,3072]{2,1,0:T(8,128)(2,1)}, bf16[2,24,3072]{2,1,0:T(8,128)(2,1)}, u32[]{:S(2)}, u32[]{:S(2)}) collective-permute-start(bf16[2,24,3072]{2,1,0:T(8,128)(2,1)} %maximum_bitcast_fusion.4), channel_id=1, source_target_pairs={{0,8},{8,0},{16,24},{24,16},{1,9},{9,1},{17,25},{25,17},{2,10},{10... | collective-permute-start | bytes 884744 | tf_op jit(solution)/shard_map/ppermute | solution.py:138
  381.5 30.0 %collective-permute-start.52 = (bf16[2,96,768]{2,1,0:T(8,128)(2,1)}, bf16[2,96,768]{2,1,0:T(8,128)(2,1)}, u32[]{:S(2)}, u32[]{:S(2)}) collective-permute-start(bf16[2,96,768]{2,1,0:T(8,128)(2,1)} %maximum_bitcast_fusion.5), channel_id=1, source_target_pairs={{0,8},{8,0},{16,24},{24,16},{1,9},{9,1},{17,25},{25,17},{2,10},{10... | collective-permute-start | bytes 884744 | tf_op jit(solution)/shard_map/ppermute | solution.py:138
  407.2 31.1 %all-to-all-start.3 = ((bf16[3,4,192,512]{3,2,0,1:T(8,128)(2,1)}), bf16[3,4,192,512]{3,2,0,1:T(8,128)(2,1)S(1)}, u32[]{:S(2)}, u32[]{:S(2)}) async-start(bf16[3,4,192,512]{3,2,0,1:T(8,128)(2,1)} %copy.328), calls=%async_computation.3 | async-start | bytes 4718592 | tf_op jit(solution)/shard_map/all_to_all | solution.py:282
  415.6 22.9 %copy-start.4 = (bf16[1,512,768]{2,1,0:T(8,128)(2,1)S(1)}, bf16[1,512,768]{2,1,0:T(8,128)(2,1)}, u32[]{:S(2)}) copy-start(bf16[1,512,768]{2,1,0:T(8,128)(2,1)} %param.11) | copy-start | bytes 2359300
  459.5 14.2 %collective-permute-start.23 = (bf16[4,4,24,2304]{3,2,1,0:T(8,128)(2,1)}, bf16[4,4,24,2304]{3,2,1,0:T(8,128)(2,1)}, u32[]{:S(2)}, u32[]{:S(2)}) collective-permute-start(bf16[4,4,24,2304]{3,2,1,0:T(8,128)(2,1)} %fusion.31), channel_id=1, source_target_pairs={{0,1},{1,0},{2,3},{3,2},{4,5},{5,4},{6,7},{7,6},{8,9},{9,8},{10,11... | collective-permute-start | bytes 5308424 | tf_op jit(solution)/shard_map/ppermute | solution.py:138
  460.5 2.7 collective-permute-start.15
  463.3 3.7 collective-permute-start.17
  464.9 4.5 collective-permute-start.18
  466.3 3.6 collective-permute-start.16
  469.9 3.6 collective-permute-start.19
  473.6 6.7 %collective-permute-start.20 = (bf16[1,3,96]{2,0,1:T(2,128)(2,1)S(1)}, bf16[1,3,96]{2,0,1:T(2,128)(2,1)S(1)}, u32[]{:S(2)}, u32[]{:S(2)}) collective-permute-start(bf16[1,3,96]{2,0,1:T(2,128)(2,1)S(1)} %fusion.81), channel_id=1, source_target_pairs={{0,4},{1,5},{2,6},{3,7},{4,0},{5,1},{6,2},{7,3},{8,12},{9,13},{10,... | collective-permute-start | bytes 1736 | tf_op jit(solution)/shard_map/ppermute | solution.py:138
  476.7 20.4 %collective-permute-start.24 = (bf16[4,24,2304]{2,1,0:T(8,128)(2,1)S(1)}, bf16[4,24,2304]{2,1,0:T(8,128)(2,1)S(1)}, u32[]{:S(2)}, u32[]{:S(2)}) collective-permute-start(bf16[4,24,2304]{2,1,0:T(8,128)(2,1)S(1)} %get-tuple-element.38), channel_id=1, source_target_pairs={{0,8},{8,0},{16,24},{24,16},{1,9},{9,1},{17,25},{25,17},{2,10},{10... | collective-permute-start | bytes 1327112 | tf_op jit(solution)/shard_map/ppermute | solution.py:138
  477.3 19.8 %collective-permute-start.26 = (bf16[4,24,2304]{2,1,0:T(8,128)(2,1)S(1)}, bf16[4,24,2304]{2,1,0:T(8,128)(2,1)S(1)}, u32[]{:S(2)}, u32[]{:S(2)}) collective-permute-start(bf16[4,24,2304]{2,1,0:T(8,128)(2,1)S(1)} %get-tuple-element.39), channel_id=1, source_target_pairs={{0,24},{8,16},{16,8},{24,0},{1,25},{9,17},{17,9},{25,1},{2,26},{10... | collective-permute-start | bytes 1327112 | tf_op jit(solution)/shard_map/ppermute | solution.py:138
  478.8 18.4 %collective-permute-start.25 = (bf16[4,24,2304]{2,1,0:T(8,128)(2,1)S(1)}, bf16[4,24,2304]{2,1,0:T(8,128)(2,1)S(1)}, u32[]{:S(2)}, u32[]{:S(2)}) collective-permute-start(bf16[4,24,2304]{2,1,0:T(8,128)(2,1)S(1)} %get-tuple-element.40), channel_id=1, source_target_pairs={{0,16},{8,24},{16,0},{24,8},{1,17},{9,25},{17,1},{25,9},{2,18},{10... | collective-permute-start | bytes 1327112 | tf_op jit(solution)/shard_map/ppermute | solution.py:138
  480.3 16.8 %collective-permute-start.21 = (bf16[1,3,96]{2,0,1:T(2,128)(2,1)S(1)}, bf16[1,3,96]{2,0,1:T(2,128)(2,1)S(1)}, u32[]{:S(2)}, u32[]{:S(2)}) collective-permute-start(bf16[1,3,96]{2,0,1:T(2,128)(2,1)S(1)} %fusion.80), channel_id=1, source_target_pairs={{0,16},{8,24},{16,0},{24,8},{1,17},{9,25},{17,1},{25,9},{2,18},{10... | collective-permute-start | bytes 1736 | tf_op jit(solution)/shard_map/ppermute | solution.py:138
  497.4 7.2 %collective-permute-start.27 = (bf16[2,24,2304]{2,1,0:T(8,128)(2,1)S(1)}, bf16[2,24,2304]{2,1,0:T(8,128)(2,1)S(1)}, u32[]{:S(2)}, u32[]{:S(2)}) collective-permute-start(bf16[2,24,2304]{2,1,0:T(8,128)(2,1)S(1)} %fusion.66), channel_id=1, source_target_pairs={{0,2},{1,3},{2,0},{3,1},{4,6},{5,7},{6,4},{7,5},{8,10},{9,11},{10,... | collective-permute-start | bytes 663560 | tf_op jit(solution)/shard_map/ppermute | solution.py:138
  497.8 8.4 %collective-permute-start.22 = (bf16[2,3,96]{2,1,0:T(4,128)(2,1)S(1)}, bf16[2,3,96]{2,1,0:T(4,128)(2,1)S(1)}, u32[]{:S(2)}, u32[]{:S(2)}) collective-permute-start(bf16[2,3,96]{2,1,0:T(4,128)(2,1)S(1)} %maximum_bitcast_fusion.9), channel_id=1, source_target_pairs={{0,8},{8,0},{16,24},{24,16},{1,9},{9,1},{17,25},{25,17},{2,10},{10... | collective-permute-start | bytes 3464 | tf_op jit(solution)/shard_map/ppermute | solution.py:138
  504.7 6.6 %collective-permute-start.28 = (bf16[1,24,2304]{2,1,0:T(8,128)(2,1)S(1)}, bf16[1,24,2304]{2,1,0:T(8,128)(2,1)S(1)}, u32[]{:S(2)}, u32[]{:S(2)}) collective-permute-start(bf16[1,24,2304]{2,1,0:T(8,128)(2,1)S(1)} %dynamic-slice_convert_fusion.16), channel_id=1, source_target_pairs={{0,4},{1,5},{2,6},{3,7},{4,0},{5,1},{6,2},{7,3},{8,12},{9,13},{10,... | collective-permute-start | bytes 331784 | tf_op jit(solution)/shard_map/ppermute | solution.py:138
  511.3 4.8 collective-permute-start.29
  516.2 6.0 %collective-permute-start.30 = (bf16[2,24,2304]{2,1,0:T(8,128)(2,1)S(1)}, bf16[2,24,2304]{2,1,0:T(8,128)(2,1)S(1)}, u32[]{:S(2)}, u32[]{:S(2)}) collective-permute-start(bf16[2,24,2304]{2,1,0:T(8,128)(2,1)S(1)} %maximum_bitcast_fusion.6), channel_id=1, source_target_pairs={{0,8},{8,0},{16,24},{24,16},{1,9},{9,1},{17,25},{25,17},{2,10},{10... | collective-permute-start | bytes 663560 | tf_op jit(solution)/shard_map/ppermute | solution.py:138
  (33 other events, 205.8 us)
Sparse Core Ops, SparseCore 0:
  12.4 55.2 all-gather.2
  154.2 28.2 all-gather.4

commit v3 on v2

--- a/solution.py
+++ b/solution.py
@@ -175,20 +175,20 @@
     return join_rows(value[None], "dp", bits_of("dp"))
 
 
-def gather_rows(weight, flip):
+def together(*values):
+    return lax.optimization_barrier(values)
+
+
+def gather_far(weight):
     parts = lax.axis_size("seq")
     rows = weight.shape[0] // parts
     share = lax.dynamic_slice_in_dim(weight, lax.axis_index("seq") * rows, rows, 0)
-    value = join_rows(share[None], "dp", bits_of("dp")[:-1])
-    owners = value.shape[0]
-    value = value[:, None]
-    bits = bits_of("seq")
-    for bit in bits[::-1] if flip else bits:
-        both = join(value, "seq", bit, 1 if flip else 2)
-        value = both.reshape((owners, -1) + value.shape[2:])
-    value = value.reshape((owners, parts * rows) + weight.shape[1:])
+    return join_rows(share[None], "dp", bits_of("dp")[:-1])
+
+
+def gather_core(value):
     value = join_rows(value, "dp", [1])
-    return value.reshape((-1,) + weight.shape[1:])
+    return value.reshape((-1,) + value.shape[2:])
 
 
 def reduce_first(value):
@@ -199,24 +199,46 @@
     return halve(value, "dp", 1)
 
 
-def reduce_rest(value):
-    owners = lax.axis_size("dp")
+def reduce_seq(value):
     parts = lax.axis_size("seq")
     place = lax.axis_index("seq")
     total = lax.dynamic_index_in_dim(value, place, 1, keepdims=False)
     for other in range(1, parts):
         sent = lax.dynamic_index_in_dim(value, place ^ other, 1, keepdims=False)
         total = total + swap(sent.astype(BF16), "seq", other).astype(F32)
-    bit = 2
-    while bit < owners:
-        total = halve(total, "dp", bit)
+    return total
+
+
+def reduce_far(total):
+    owners = lax.axis_size("dp")
+    if owners > 8:
+        bit = 2
+        while bit < owners:
+            total = halve(total, "dp", bit)
+            bit *= 2
+        return total[0]
+    far = lax.axis_index("dp") // 2
+    kept = lax.dynamic_index_in_dim(total, far, 0, keepdims=False)
+    for other in range(1, owners // 2):
+        sent = lax.dynamic_index_in_dim(total, far ^ other, 0, keepdims=False)
+        kept = kept + swap(sent.astype(BF16), "dp", 2 * other).astype(F32)
+    return kept
+
+
+def gather_seq(own):
+    own = own.astype(BF16)
+    parts = lax.axis_size("seq")
+    pieces = [own] + [swap(own, "seq", other) for other in range(1, parts)]
+    bit = 1
+    while bit < parts:
+        upper = (lax.axis_index("seq") // bit) % 2 == 1
+        pieces = [jnp.where(upper, pieces[k ^ bit], pieces[k]) for k in range(parts)]
         bit *= 2
-    own = join_rows(total.astype(BF16), "seq", bits_of("seq"))
-    return own.reshape((-1,) + own.shape[2:]).astype(F32)
-
-
-def reduce_owned(value):
-    return reduce_rest(reduce_first(value))
+    return jnp.stack(pieces).astype(F32)
+
+
+def flat(value):
+    return value.reshape((-1,) + value.shape[2:])
 
 
 def shards(
@@ -233,8 +255,9 @@
     vectors = gather_small(packed).transpose(1, 0, 2).reshape(lines, -1).astype(F32)
     full_qkv = lax.all_gather(w_qkv, "dp", axis=0, tiled=True)
     full_out = lax.all_gather(w_out, "dp", axis=0, tiled=True)
-    full_fc = gather_rows(w_fc, False)
-    full_proj = gather_rows(w_proj, True)
+    full_fc = lax.all_gather(w_fc, "dp", axis=0, tiled=True)
+    far_proj = gather_far(w_proj)
+    full_qkv, far_proj, vectors = together(full_qkv, far_proj, vectors)
     gain_vals, shift_vals, qv_vals, branch_vals = (
         vectors[0:2], vectors[2:4], vectors[4:6], vectors[6:8],
     )
@@ -246,9 +269,20 @@
     projected = (dot(full_qkv, normed_first, 0, 1) + bias[:, None]).astype(BF16)
     projected = projected.reshape(3, parts, width // parts, rows)
     qkv = lax.all_to_all(projected, "seq", split_axis=1, concat_axis=1, tiled=True)
+    qkv, far_proj = together(qkv, far_proj)
+    near_proj = join(far_proj, "seq", 1, 1)
+    near_proj = near_proj.reshape((near_proj.shape[0], -1) + near_proj.shape[3:])
     seq_heads, logs = attend_forward(qkv)
+    seq_heads, logs, near_proj = together(seq_heads, logs, near_proj)
     head_out = lax.all_to_all(seq_heads, "seq", split_axis=0, concat_axis=0, tiled=True)
     head_out = head_out.reshape(width, rows)
+    bit = 2
+    while bit < parts:
+        near_proj = join(near_proj, "seq", bit, 1)
+        near_proj = near_proj.reshape((near_proj.shape[0], -1) + near_proj.shape[3:])
+        bit *= 2
+    head_out, near_proj = together(head_out, near_proj)
+    full_proj = gather_core(near_proj)
     middle = source + (dot(head_out, full_out, 0, 0) + branch_vals[0])
     second = layer_norm(middle, gain_vals[1], shift_vals[1]).astype(BF16)
     hidden = dot(second, full_fc, 1, 0) + fc_vals
@@ -278,7 +312,10 @@
     early_proj, early_fc, seq_grad = lax.optimization_barrier(
         (reduce_first(grad_proj), reduce_first(grad_fc), seq_grad)
     )
+    early_proj = reduce_seq(early_proj)
+    early_fc = reduce_seq(early_fc)
     seq_dqkv = attend_backward(qkv, seq_heads, logs, seq_grad)
+    seq_dqkv, early_proj, early_fc = together(seq_dqkv, early_proj, early_fc)
     grad_qkv = lax.all_to_all(seq_dqkv, "seq", split_axis=1, concat_axis=1, tiled=True)
     grad_projected = grad_qkv.reshape(3 * width, rows)
     grad_sums = jnp.sum(grad_projected.astype(F32), axis=1)
@@ -299,19 +336,27 @@
         ],
         axis=0,
     )
-    small = small.reshape(lines, owners, share).transpose(1, 0, 2).reshape(-1, share)
-    small = reduce_owned(small)
+    count = lines * share // parts
+    small = small.reshape(lines, owners, share).transpose(1, 0, 2).reshape(owners, parts, 1, count)
+    small = jnp.pad(small, ((0, 0), (0, 0), (0, 7), (0, width - count)))
+    bundle = jnp.concatenate([grad_out.reshape(owners, parts, -1, width), small], axis=2)
+    bundle = reduce_first(bundle.reshape(-1, width))
+    first_qkv = reduce_first(grad_w_qkv)
+    bundle = gather_seq(reduce_far(reduce_seq(bundle)))
+    sum_qkv = flat(gather_seq(reduce_far(reduce_seq(first_qkv))))
+    sum_out = flat(bundle[:, :-8])
+    small = bundle[:, -8, :count].reshape(lines, share)
     return (
         result.astype(BF16)[None],
         input_grad[None],
         small[0:2],
         small[2:4],
-        reduce_owned(grad_w_qkv),
+        sum_qkv,
         small[4:6],
-        reduce_owned(grad_out),
-        reduce_rest(early_fc),
+        sum_out,
+        flat(gather_seq(reduce_far(early_fc))),
         small[8:].reshape(-1),
-        reduce_rest(early_proj),
+        flat(gather_seq(reduce_far(early_proj))),
         small[6:8],
     )
 

time: 540 us -> 453 us (0.84)
  waiting for transfers between devices: 247 us -> 173 us
  other arithmetic: 50.9 us -> 40.8 us
  starting transfers between devices: 80.1 us -> 73.1 us
  matrix products: 47.1 us -> 53.8 us
    ppermute x53 -> x48, waiting for transfers between devices: 204 us -> 138 us  [swap(): return lax.ppermute(value, axis, [(d, d ^ bit) for d in range(size)])]
    all_to_all x1, waiting for transfers between devices: 22.8 us -> 0.01 us  [shards(): lax.all_to_all(seq_dqkv, 'seq', split_axis=1, concat_axis=1, tiled=True)]
    another operation x30 -> x13, other arithmetic: 21.2 us -> 6.67 us  [join(): return jnp.stack([first, second], axis=dim)]
    all_to_all x1, waiting for transfers between devices: 18.1 us -> 28.4 us  [shards(): lax.all_to_all(projected, 'seq', split_axis=1, concat_axis=1, tiled=True)]
    dot_general x12, matrix products: 47.1 us -> 53.8 us  [dot(): lax.dot_general(left, right, (((left_dim,), (right_dim,)), ((), ())), pre...]
    ppermute x53 -> x48, starting transfers between devices: 62.9 us -> 56.2 us  [swap(): return lax.ppermute(value, axis, [(d, d ^ bit) for d in range(size)])]
    convert_element_type x10 -> x9, other arithmetic: 1.43 us -> 7.95 us  [the longest x4 4.83 us: gather_seq(): return jnp.stack(pieces).astype(F32)]
    concatenate x9, local copies, waits for them, and re-layouts: 0.7 us -> 6.95 us  [shards(): jnp.concatenate([jnp.stack([grad_gain_one, grad_gain_two, grad_shift_one,...]
  transfers between devices with their start and end apart: 59 -> 55, of which waited for: 32 -> 25; matrix products, arithmetic and copies ran while one was open for 19% -> 28% of each run, Pallas kernels for 7% -> 8%
where the time goes in v3:
time: 453 us; the launch traced here: 445 us
  waiting for transfers between devices  173 us (38%)
  starting transfers between devices  73.1 us (16%)
  matrix products  53.8 us (12%)
  local copies, waits for them, and re-layouts  52.7 us (12%)
  other arithmetic  40.8 us (9%)
  Pallas kernels  36.2 us (8%)
  between operations  15.4 us (3%)
    ppermute x48, waiting for transfers between devices, swap(): return lax.ppermute(value, axis, [(d, d ^ bit) for d in range(size)])  138 us
    ppermute x48, starting transfers between devices, swap(): return lax.ppermute(value, axis, [(d, d ^ bit) for d in range(size)])  56.2 us
    dot_general x12, matrix products, dot(): lax.dot_general(left, right, (((left_dim,), (right_dim,)), ((), ())), pre...  53.8 us
    all_to_all x1, waiting for transfers between devices, shards(): lax.all_to_all(projected, 'seq', split_axis=1, concat_axis=1, tiled=True)  28.4 us
    pallas_call x1, Pallas kernels, attend_backward(): pl.pallas_call(partial(backward_kernel, blocks), grid=(heads,), in_specs=...  23.6 us
    unnamed x104, local copies, waits for them, and re-layouts  13.4 us
    pallas_call x1, Pallas kernels, attend_forward(): pl.pallas_call(partial(forward_kernel, blocks), grid=(heads,), in_specs=[...  12.6 us
    add x4, other arithmetic, halve(): return kept.astype(F32) + swap(sent.astype(BF16), axis, bit).astype(F32)  11 us
  transfers between devices with their start and end apart: 55, of which 25 were waited for; matrix products, arithmetic and copies ran while one was open for 28% of the time, Pallas kernels for 8%

profile of v3, /device:TPU:0, one launch (start us, length us, event | category | flops | bytes accessed | tf_op | source)
XLA Modules:
  0.0 445.2 jit_solution(16954604695373777295)
XLA Ops:
  10.2 4.1 collective-permute-start.2
  17.1 2.0 collective-permute-start.3
  19.1 1.8 collective-permute-done.3
  21.0 7.6 %collective-permute-done = bf16[1,96,768]{2,1,0:T(8,128)(2,1)S(1)} collective-permute-done((bf16[1,96,768]{2,1,0:T(8,128)(2,1)S(1)}, bf16[1,96,768]{2,1,0:T(8,128)(2,1)S(1)}, u32[]{:S(2)}, u32[]{:S(2)}) %collective-permute-start) | collective-permute-done | bytes 147488 | tf_op jit(solution)/shard_map/ppermute | solution.py:138
  29.8 25.0 %collective-permute-done.1 = bf16[2,96,768]{2,1,0:T(8,128)(2,1)S(1)} collective-permute-done((bf16[2,96,768]{2,1,0:T(8,128)(2,1)S(1)}, bf16[2,96,768]{2,1,0:T(8,128)(2,1)S(1)}, u32[]{:S(2)}, u32[]{:S(2)}) %collective-permute-start.1) | collective-permute-done | bytes 294944 | tf_op jit(solution)/shard_map/ppermute | solution.py:138
  55.7 5.4 %all-gather.4.cloned.1.call-done = bf16[768,2304]{1,0:T(8,128)(2,1)} async-done(((bf16[96,2304]{1,0:T(8,128)(2,1)}), bf16[768,2304]{1,0:T(8,128)(2,1)}) %all-gather.4.cloned.1.call-update) | async-done | bytes 3538960 | tf_op jit(solution)/shard_map/all_gather | solution.py:256
  61.2 4.5 %fusion.18 = bf16[2304,512]{1,0:T(8,128)(2,1)S(1)} fusion(bf16[768,2304]{1,0:T(8,128)(2,1)} %all-gather.4.cloned.1.call-done, f32[2304]{0:T(1024)S(1)} %pad_maximum_fusion.11, bf16[1,512,768]{2,1,0:T(8,128)(2,1)S(1)} %copy-done.5, f32[768]{0:T(1024)S(1)} %get-tuple-element.60, f32[768]{0:T(1024)S(1)} %get-tuple-element.61, f32[512]{0:T(512)S(1)} %fusion.94, ...), kind=kOutput, calls=%fused_computation.32 | convolution fusion | flops 1816657920 | bytes 6704128 | tf_op jit(solution)/shard_map/dot_general | solution.py:24
  65.8 1.6 copy.126
  67.3 4.6 %all-to-all-start = ((bf16[3,4,192,512]{3,2,0,1:T(8,128)(2,1)}), bf16[3,4,192,512]{3,2,0,1:T(8,128)(2,1)}, u32[]{:S(2)}, u32[]{:S(2)}) async-start(bf16[3,4,192,512]{3,2,0,1:T(8,128)(2,1)} %copy.126), calls=%async_computation | async-start | bytes 4718592 | tf_op jit(solution)/shard_map/all_to_all | solution.py:271
  71.9 28.4 %all-to-all-done = bf16[3,4,192,512]{3,2,0,1:T(8,128)(2,1)} async-done(((bf16[3,4,192,512]{3,2,0,1:T(8,128)(2,1)}), bf16[3,4,192,512]{3,2,0,1:T(8,128)(2,1)}, u32[]{:S(2)}, u32[]{:S(2)}) %all-to-all-start) | async-done | bytes 2359328 | tf_op jit(solution)/shard_map/all_to_all | solution.py:271
  100.3 2.0 copy.127.qkv_ref
  103.8 12.6 %attend_forward.1 = (bf16[4,192,512]{2,1,0:T(8,128)(2,1)}, f32[3,4,8,512]{3,2,1,0:T(8,128)S(1)}) custom-call(bf16[3,4,192,512]{3,2,1,0:T(8,128)(2,1)S(1)} %copy.127.qkv_ref), custom_call_target="tpu_custom_call" | custom-call | flops 8053063680 | bytes 4718592 | tf_op jit(solution)/shard_map/attend_forward/pallas_call | solution.py:96
  119.9 4.7 %all-to-all-start.1 = ((bf16[4,192,512]{2,1,0:T(8,128)(2,1)}), bf16[4,192,512]{2,1,0:T(8,128)(2,1)}, u32[]{:S(2)}, u32[]{:S(2)}) async-start(bf16[4,192,512]{2,1,0:T(8,128)(2,1)} %get-tuple-element.36.out_ref), calls=%async_computation.1 | async-start | bytes 1572864 | tf_op jit(solution)/shard_map/all_to_all | solution.py:277
  124.8 26.7 %collective-permute-done.6 = bf16[4,192,768]{2,1,0:T(8,128)(2,1)} collective-permute-done((bf16[4,192,768]{2,1,0:T(8,128)(2,1)}, bf16[4,192,768]{2,1,0:T(8,128)(2,1)}, u32[]{:S(2)}, u32[]{:S(2)}) %collective-permute-start.6) | collective-permute-done | bytes 1179680 | tf_op jit(solution)/shard_map/ppermute | solution.py:138
  151.5 1.8 select_bitcast_fusion.3
  155.1 2.4 fusion.109
  159.0 10.5 %fusion.14 = (bf16[3072,512]{0,1:T(8,128)(2,1)}, f32[512,3072]{1,0:T(8,128)}) fusion(f32[3072]{0:T(1024)S(1)} %add.329, bf16[768,3072]{1,0:T(8,128)(2,1)} %all-gather.8.cloned.1.call-done, f32[512,768]{1,0:T(8,128)} %copy-done.11, f32[768]{0:T(1024)S(1)} %get-tuple-element.55, f32[768]{0:T(1024)S(1)} %get-tuple-element.56, f32[512]{0:T(512)S(1)} %fusion.95, ...), kind=kOutput, calls=%fused_computation.17 | convolution fusion | flops 2433613824 | bytes 15751168 | tf_op jit(solution)/shard_map/dot_general | solution.py:24
  169.5 4.8 %copy.132 = bf16[3072,512]{1,0:T(8,128)(2,1)} copy(bf16[3072,512]{0,1:T(8,128)(2,1)} %get-tuple-element.131) | data formatting | bytes 6291456 | tf_op jit(solution)/shard_map/convert_element_type | solution.py:289
  174.3 4.5 %fusion.52 = f32[4,2,4,96,768]{4,3,2,1,0:T(8,128)S(1)} fusion(bf16[4,2,4,96,512]{4,3,2,1,0:T(8,128)(2,1)} %bitcast.367, bf16[1,512,768]{2,1,0:T(8,128)(2,1)S(1)} %copy-done.17), kind=kOutput, calls=%fused_computation.104 | convolution fusion | flops 2415919104 | bytes 13369344 | tf_op jit(solution)/shard_map/dot_general | solution.py:24
  178.8 1.7 fusion.20
  181.0 2.4 copy-done.14
  183.5 2.1 select_bitcast_fusion.1
  187.4 6.7 %convert_reduce_fusion = (f32[3072]{0:T(1024)S(1)}, bf16[512,3072]{1,0:T(8,128)(2,1)S(1)}) fusion(f32[512,3072]{1,0:T(8,128)S(1)} %bitcast.386, f32[3072]{0:T(1024)S(1)} %add.329, bf16[3072,768]{1,0:T(8,128)(2,1)S(1)} %bitcast.364, bf16[1,512,768]{2,1,0:T(8,128)(2,1)S(1)} %copy-done.17), kind=kOutput, calls=%fused_computation.23 | convolution fusion | flops 2452091904 | bytes 14966784 | tf_op jit(solution)/shard_map/dot_general | solution.py:24
  194.1 3.0 fusion.103
  197.1 1.9 fusion.21
  199.5 3.5 multiply_reduce_fusion
  208.0 3.7 all-to-all-start.2
  211.8 6.0 %bitcast_add_fusion.1 = f32[4,4,96,768]{3,2,1,0:T(8,128)} fusion(bf16[4,4,96,768]{3,2,1,0:T(8,128)(2,1)} %collective-permute-done.8, f32[4,2,4,96,768]{4,3,2,1,0:T(8,128)} %copy-done.14, s32[]{:T(128)S(6)} %select_n.440), kind=kLoop, calls=%fused_computation.28 | loop fusion | flops 2359296 | bytes 11796484 | tf_op jit(solution)/shard_map/add | solution.py:146
  217.7 9.1 %fusion.41 = bf16[1,512,768]{2,1,0:T(8,128)(2,1)} fusion(f32[512,768]{1,0:T(8,128)S(1)} %copy-done.13, bf16[3072,768]{1,0:T(8,128)(2,1)} %bitcast.365, f32[512,3072]{1,0:T(8,128)} %get-tuple-element.132, f32[3072]{0:T(1024)S(1)} %add.329, f32[768]{0:T(1024)S(1)} %get-tuple-element.54), kind=kOutput, calls=%fused_computation.78 | convolution fusion | flops 2432827392 | bytes 13384704 | tf_op jit(solution)/shard_map/dot_general | solution.py:24
  226.9 4.5 %bitcast_add_fusion = f32[4,4,24,3072]{3,2,1,0:T(8,128)} fusion(bf16[4,4,24,3072]{3,2,1,0:T(8,128)(2,1)} %collective-permute-done.9, f32[4,2,4,24,3072]{4,3,2,1,0:T(8,128)S(1)} %bitcast.363, s32[]{:T(128)S(6)} %select_n.440), kind=kLoop, calls=%fused_computation.27 | loop fusion | flops 2359296 | bytes 11796484 | tf_op jit(solution)/shard_map/add | solution.py:146
  232.9 1.6 fusion.60
  234.5 3.0 collective-permute-start.15
  237.6 1.8 fusion.55
  239.3 2.0 collective-permute-start.10
  243.6 20.8 %collective-permute-done.12 = bf16[4,96,768]{2,1,0:T(8,128)(2,1)S(1)} collective-permute-done((bf16[4,96,768]{2,1,0:T(8,128)(2,1)S(1)}, bf16[4,96,768]{2,1,0:T(8,128)(2,1)S(1)}, u32[]{:S(2)}, u32[]{:S(2)}) %collective-permute-start.12) | collective-permute-done | bytes 589856 | tf_op jit(solution)/shard_map/ppermute | solution.py:138
  264.4 2.0 collective-permute-start.14
  266.4 23.6 %attend_backward.1 = bf16[3,4,192,512]{3,2,1,0:T(8,128)(2,1)S(1)} custom-call(bf16[3,4,192,512]{3,2,1,0:T(8,128)(2,1)S(1)} %copy.127.qkv_ref, bf16[4,192,512]{2,1,0:T(8,128)(2,1)} %get-tuple-element.36.out_ref, f32[3,4,8,512]{3,2,1,0:T(8,128)S(1)} %get-tuple-element.40.log_ref, bf16[4,192,512]{2,1,0:T(8,128)(2,1)S(1)} %all-to-all-done.2.grad_ref), custom_call_target="tpu_custom_call" | custom-call | flops 20132659200 | bytes 14155776 | tf_op jit(solution)/shard_map/attend_backward/pallas_call | solution.py:118
  290.1 2.3 fusion.46
  297.1 3.3 fusion.110
  304.5 1.7 copy.139
  306.2 3.9 all-to-all-start.3
  310.1 1.8 collective-permute-start.42
  315.0 2.1 collective-permute-start.41
  319.0 4.6 %collective-permute-done.43 = bf16[96,768]{1,0:T(8,128)(2,1)S(1)} collective-permute-done((bf16[96,768]{1,0:T(8,128)(2,1)S(1)}, bf16[96,768]{1,0:T(8,128)(2,1)S(1)}, u32[]{:S(2)}, u32[]{:S(2)}) %collective-permute-start.43) | collective-permute-done | bytes 147488 | tf_op jit(solution)/shard_map/ppermute | solution.py:138
  324.3 1.7 collective-permute-start.47
  327.5 14.8 %collective-permute-done.41 = bf16[24,3072]{1,0:T(8,128)(2,1)S(1)} collective-permute-done((bf16[24,3072]{1,0:T(8,128)(2,1)S(1)}, bf16[24,3072]{1,0:T(8,128)(2,1)S(1)}, u32[]{:S(2)}, u32[]{:S(2)}) %collective-permute-start.41) | collective-permute-done | bytes 147488 | tf_op jit(solution)/shard_map/ppermute | solution.py:138
  347.8 1.9 copy-done.43
  349.7 3.4 fusion.105
  355.1 2.2 fusion.33
  358.0 3.1 fusion.100
  361.1 1.6 copy.146
  365.9 2.1 fusion.111
  375.0 3.3 collective-permute-done.17
  378.3 3.0 collective-permute-done.19
  382.8 1.8 collective-permute-start.20
  387.3 3.2 collective-permute-done.22
  397.1 2.5 collective-permute-start.29
  402.1 7.9 %collective-permute-done.27 = bf16[4,24,2304]{2,1,0:T(8,128)(2,1)} collective-permute-done((bf16[4,24,2304]{2,1,0:T(8,128)(2,1)}, bf16[4,24,2304]{2,1,0:T(8,128)(2,1)}, u32[]{:S(2)}, u32[]{:S(2)}) %collective-permute-start.27) | collective-permute-done | bytes 442400 | tf_op jit(solution)/shard_map/ppermute | solution.py:138
  410.0 5.7 %collective-permute-done.29 = bf16[4,24,2304]{2,1,0:T(8,128)(2,1)} collective-permute-done((bf16[4,24,2304]{2,1,0:T(8,128)(2,1)}, bf16[4,24,2304]{2,1,0:T(8,128)(2,1)}, u32[]{:S(2)}, u32[]{:S(2)}) %collective-permute-start.29) | collective-permute-done | bytes 442400 | tf_op jit(solution)/shard_map/ppermute | solution.py:138
  420.8 1.8 collective-permute-start.31
  423.8 2.0 collective-permute-done.32
  425.9 3.0 collective-permute-done.31
  431.4 2.0 collective-permute-start.33
  435.5 1.6 collective-permute-done.33
  (281 shorter events, 87.4 us)
Async XLA Ops:
  7.2 9.5 %copy-start.5 = (bf16[1,512,768]{2,1,0:T(8,128)(2,1)S(1)}, bf16[1,512,768]{2,1,0:T(8,128)(2,1)}, u32[]{:S(2)}) copy-start(bf16[1,512,768]{2,1,0:T(8,128)(2,1)} %param.11) | copy-start | bytes 2359300
  7.2 53.9 %all-gather.4.cloned.1.call-start = ((), (), s32[]{:S(2)}) async-start(), calls=%async_computation.4 | async-start | bytes 3981312 | tf_op jit(solution)/shard_map/all_gather | solution.py:256
  7.9 147.2 %all-gather.6.cloned.1.call-start = ((), (), s32[]{:S(2)}) async-start(), calls=%async_computation.5 | async-start | bytes 1327104 | tf_op jit(solution)/shard_map/all_gather | solution.py:257
  8.7 150.3 %all-gather.8.cloned.1.call-start = ((), (), s32[]{:S(2)}) async-start(), calls=%async_computation.6 | async-start | bytes 5308416 | tf_op jit(solution)/shard_map/all_gather | solution.py:258
  10.2 6.9 %collective-permute-start.2 = (bf16[1,12,96]{2,1,0:T(8,128)(2,1)S(1)}, bf16[1,12,96]{2,1,0:T(8,128)(2,1)S(1)}, u32[]{:S(2)}, u32[]{:S(2)}) collective-permute-start(bf16[1,12,96]{2,1,0:T(8,128)(2,1)S(1)} %bitcast.382), channel_id=1, source_target_pairs={{0,4},{1,5},{2,6},{3,7},{4,0},{5,1},{6,2},{7,3},{8,12},{9,13},{10,... | collective-permute-start | bytes 6920 | tf_op jit(solution)/shard_map/ppermute | solution.py:138
  15.2 13.3 %collective-permute-start = (bf16[1,96,768]{2,1,0:T(8,128)(2,1)S(1)}, bf16[1,96,768]{2,1,0:T(8,128)(2,1)S(1)}, u32[]{:S(2)}, u32[]{:S(2)}) collective-permute-start(bf16[1,96,768]{2,1,0:T(8,128)(2,1)S(1)} %dynamic-slice_bitcast_fusion), channel_id=1, source_target_pairs={{0,4},{1,5},{2,6},{3,7},{4,0},{5,1},{6,2},{7,3},{8,12},{9,13},{10,... | collective-permute-start | bytes 442376 | tf_op jit(solution)/shard_map/ppermute | solution.py:138
  16.7 44.5 %copy-start.32 = (f32[512]{0:T(512)}, f32[512]{0:T(512)S(1)}, u32[]{:S(2)}) copy-start(f32[512]{0:T(512)S(1)} %broadcast_multiply_fusion.1) | copy-start | bytes 6148
  17.1 3.7 collective-permute-start.3
  19.1 46.6 %copy-start.34 = (f32[512]{0:T(512)}, f32[512]{0:T(512)S(1)}, u32[]{:S(2)}) copy-start(f32[512]{0:T(512)S(1)} %fusion.94) | copy-start | bytes 6148
  20.9 8.7 %collective-permute-start.4 = (bf16[4,12,96]{2,0,1:T(4,128)(2,1)S(1)}, bf16[4,12,96]{2,0,1:T(4,128)(2,1)S(1)}, u32[]{:S(2)}, u32[]{:S(2)}) collective-permute-start(bf16[4,12,96]{2,0,1:T(4,128)(2,1)S(1)} %bitcast.378), channel_id=1, source_target_pairs={{0,1},{1,0},{2,3},{3,2},{4,5},{5,4},{6,7},{7,6},{8,9},{9,8},{10,11... | collective-permute-start | bytes 27656 | tf_op jit(solution)/shard_map/ppermute | solution.py:138
  29.6 25.2 %collective-permute-start.1 = (bf16[2,96,768]{2,1,0:T(8,128)(2,1)S(1)}, bf16[2,96,768]{2,1,0:T(8,128)(2,1)S(1)}, u32[]{:S(2)}, u32[]{:S(2)}) collective-permute-start(bf16[2,96,768]{2,1,0:T(8,128)(2,1)S(1)} %maximum_bitcast_fusion), channel_id=1, source_target_pairs={{0,2},{1,3},{2,0},{3,1},{4,6},{5,7},{6,4},{7,5},{8,10},{9,11},{10,... | collective-permute-start | bytes 884744 | tf_op jit(solution)/shard_map/ppermute | solution.py:138
  67.3 33.0 %all-to-all-start = ((bf16[3,4,192,512]{3,2,0,1:T(8,128)(2,1)}), bf16[3,4,192,512]{3,2,0,1:T(8,128)(2,1)}, u32[]{:S(2)}, u32[]{:S(2)}) async-start(bf16[3,4,192,512]{3,2,0,1:T(8,128)(2,1)} %copy.126), calls=%async_computation | async-start | bytes 4718592 | tf_op jit(solution)/shard_map/all_to_all | solution.py:271
  102.4 14.7 %collective-permute-start.5 = (bf16[4,96,768]{2,1,0:T(8,128)(2,1)S(1)}, bf16[4,96,768]{2,1,0:T(8,128)(2,1)S(1)}, u32[]{:S(2)}, u32[]{:S(2)}) collective-permute-start(bf16[4,96,768]{2,1,0:T(8,128)(2,1)S(1)} %bitcast.370), channel_id=1, source_target_pairs={{0,8},{8,0},{16,24},{24,16},{1,9},{9,1},{17,25},{25,17},{2,10},{10... | collective-permute-start | bytes 1769480 | tf_op jit(solution)/shard_map/ppermute | solution.py:138
  118.4 33.1 %collective-permute-start.6 = (bf16[4,192,768]{2,1,0:T(8,128)(2,1)}, bf16[4,192,768]{2,1,0:T(8,128)(2,1)}, u32[]{:S(2)}, u32[]{:S(2)}) collective-permute-start(bf16[4,192,768]{2,1,0:T(8,128)(2,1)} %bitcast.23), channel_id=1, source_target_pairs={{0,16},{8,24},{16,0},{24,8},{1,17},{9,25},{17,1},{25,9},{2,18},{10... | collective-permute-start | bytes 3538952 | tf_op jit(solution)/shard_map/ppermute | solution.py:138
  119.9 35.2 %all-to-all-start.1 = ((bf16[4,192,512]{2,1,0:T(8,128)(2,1)}), bf16[4,192,512]{2,1,0:T(8,128)(2,1)}, u32[]{:S(2)}, u32[]{:S(2)}) async-start(bf16[4,192,512]{2,1,0:T(8,128)(2,1)} %get-tuple-element.36.out_ref), calls=%async_computation.1 | async-start | bytes 1572864 | tf_op jit(solution)/shard_map/all_to_all | solution.py:277
  155.1 28.4 %collective-permute-start.7 = (bf16[4,384,768]{2,1,0:T(8,128)(2,1)}, bf16[4,384,768]{2,1,0:T(8,128)(2,1)}, u32[]{:S(2)}, u32[]{:S(2)}) collective-permute-start(bf16[4,384,768]{2,1,0:T(8,128)(2,1)} %bitcast.358), channel_id=1, source_target_pairs={{0,1},{1,0},{2,3},{3,2},{4,5},{5,4},{6,7},{7,6},{8,9},{9,8},{10,11... | collective-permute-start | bytes 7077896 | tf_op jit(solution)/shard_map/ppermute | solution.py:138
  180.5 31.2 %collective-permute-start.8 = (bf16[4,4,96,768]{3,2,1,0:T(8,128)(2,1)}, bf16[4,4,96,768]{3,2,1,0:T(8,128)(2,1)}, u32[]{:S(2)}, u32[]{:S(2)}) collective-permute-start(bf16[4,4,96,768]{3,2,1,0:T(8,128)(2,1)} %fusion.20), channel_id=1, source_target_pairs={{0,1},{1,0},{2,3},{3,2},{4,5},{5,4},{6,7},{7,6},{8,9},{9,8},{10,11... | collective-permute-start | bytes 7077896 | tf_op jit(solution)/shard_map/ppermute | solution.py:138
  186.0 13.5 %slice-start.3 = ((s8[4718592]{0:T(1024)(128)(4,1)}), s8[4194304]{0:T(1024)(128)(4,1)S(1)}, s32[]{:S(2)}) async-start(s8[4718592]{0:T(1024)(128)(4,1)} %bitcast.383), calls=%async_computation.10 | async-start | bytes 8388608
  187.4 12.1 %slice-start.4 = ((s8[4718592]{0:T(1024)(128)(4,1)}), s8[524288]{0:T(1024)(128)(4,1)S(1)}, s32[]{:S(2)}) async-start(s8[4718592]{0:T(1024)(128)(4,1)} %bitcast.383), calls=%async_computation.11 | async-start | bytes 1048576
  199.0 27.9 %collective-permute-start.9 = (bf16[4,4,24,3072]{3,2,1,0:T(8,128)(2,1)}, bf16[4,4,24,3072]{3,2,1,0:T(8,128)(2,1)}, u32[]{:S(2)}, u32[]{:S(2)}) collective-permute-start(bf16[4,4,24,3072]{3,2,1,0:T(8,128)(2,1)} %fusion.21), channel_id=1, source_target_pairs={{0,1},{1,0},{2,3},{3,2},{4,5},{5,4},{6,7},{7,6},{8,9},{9,8},{10,11... | collective-permute-start | bytes 7077896 | tf_op jit(solution)/shard_map/ppermute | solution.py:138
  208.0 23.4 %all-to-all-start.2 = ((bf16[4,192,512]{2,1,0:T(8,128)(2,1)}), bf16[4,192,512]{2,1,0:T(8,128)(2,1)S(1)}, u32[]{:S(2)}, u32[]{:S(2)}) async-start(bf16[4,192,512]{2,1,0:T(8,128)(2,1)} %bitcast.368), calls=%async_computation.2 | async-start | bytes 1572864 | tf_op jit(solution)/shard_map/all_to_all | solution.py:305
  211.7 15.1 %slice-start = ((s8[9437184]{0:T(1024)(128)(4,1)}), s8[4194304]{0:T(1024)(128)(4,1)S(1)}, s32[]{:S(2)}) async-start(s8[9437184]{0:T(1024)(128)(4,1)} %bitcast.361), calls=%async_computation.7 | async-start | bytes 8388608
  217.7 9.2 %slice-start.2 = ((s8[9437184]{0:T(1024)(128)(4,1)}), s8[1048576]{0:T(1024)(128)(4,1)S(1)}, s32[]{:S(2)}) async-start(s8[9437184]{0:T(1024)(128)(4,1)} %bitcast.361), calls=%async_computation.9 | async-start | bytes 2097152
  231.4 11.4 %copy-start.7 = (f32[4,4,24,3072]{3,2,1,0:T(8,128)S(1)}, f32[4,4,24,3072]{3,2,1,0:T(8,128)}, u32[]{:S(2)}) copy-start(f32[4,4,24,3072]{3,2,1,0:T(8,128)} %bitcast_add_fusion) | copy-start | bytes 14155780
  234.5 57.9 %collective-permute-start.15 = (bf16[4,24,3072]{2,1,0:T(8,128)(2,1)S(1)}, bf16[4,24,3072]{2,1,0:T(8,128)(2,1)S(1)}, u32[]{:S(2)}, u32[]{:S(2)}) collective-permute-start(bf16[4,24,3072]{2,1,0:T(8,128)(2,1)S(1)} %fusion.60), channel_id=1, source_target_pairs={{0,24},{8,16},{16,8},{24,0},{1,25},{9,17},{17,9},{25,1},{2,26},{10... | collective-permute-start | bytes 1769480 | tf_op jit(solution)/shard_map/ppermute | solution.py:138
  237.5 26.9 %collective-permute-start.12 = (bf16[4,96,768]{2,1,0:T(8,128)(2,1)S(1)}, bf16[4,96,768]{2,1,0:T(8,128)(2,1)S(1)}, u32[]{:S(2)}, u32[]{:S(2)}) collective-permute-start(bf16[4,96,768]{2,1,0:T(8,128)(2,1)S(1)} %fusion.57), channel_id=1, source_target_pairs={{0,24},{8,16},{16,8},{24,0},{1,25},{9,17},{17,9},{25,1},{2,26},{10... | collective-permute-start | bytes 1769480 | tf_op jit(solution)/shard_map/ppermute | solution.py:138
  239.3 50.7 %collective-permute-start.10 = (bf16[4,96,768]{2,1,0:T(8,128)(2,1)S(1)}, bf16[4,96,768]{2,1,0:T(8,128)(2,1)S(1)}, u32[]{:S(2)}, u32[]{:S(2)}) collective-permute-start(bf16[4,96,768]{2,1,0:T(8,128)(2,1)S(1)} %get-tuple-element.75), channel_id=1, source_target_pairs={{0,8},{8,0},{16,24},{24,16},{1,9},{9,1},{17,25},{25,17},{2,10},{10... | collective-permute-start | bytes 1769480 | tf_op jit(solution)/shard_map/ppermute | solution.py:138
  241.4 48.7 %collective-permute-start.11 = (bf16[4,96,768]{2,1,0:T(8,128)(2,1)S(1)}, bf16[4,96,768]{2,1,0:T(8,128)(2,1)S(1)}, u32[]{:S(2)}, u32[]{:S(2)}) collective-permute-start(bf16[4,96,768]{2,1,0:T(8,128)(2,1)S(1)} %get-tuple-element.76), channel_id=1, source_target_pairs={{0,16},{8,24},{16,0},{24,8},{1,17},{9,25},{17,1},{25,9},{2,18},{10... | collective-permute-start | bytes 1769480 | tf_op jit(solution)/shard_map/ppermute | solution.py:138
  243.0 49.5 %collective-permute-start.13 = (bf16[4,24,3072]{2,1,0:T(8,128)(2,1)S(1)}, bf16[4,24,3072]{2,1,0:T(8,128)(2,1)S(1)}, u32[]{:S(2)}, u32[]{:S(2)}) collective-permute-start(bf16[4,24,3072]{2,1,0:T(8,128)(2,1)S(1)} %get-tuple-element.73), channel_id=1, source_target_pairs={{0,8},{8,0},{16,24},{24,16},{1,9},{9,1},{17,25},{25,17},{2,10},{10... | collective-permute-start | bytes 1769480 | tf_op jit(solution)/shard_map/ppermute | solution.py:138
  264.4 28.1 %collective-permute-start.14 = (bf16[4,24,3072]{2,1,0:T(8,128)(2,1)S(1)}, bf16[4,24,3072]{2,1,0:T(8,128)(2,1)S(1)}, u32[]{:S(2)}, u32[]{:S(2)}) collective-permute-start(bf16[4,24,3072]{2,1,0:T(8,128)(2,1)S(1)} %get-tuple-element.74), channel_id=1, source_target_pairs={{0,16},{8,24},{16,0},{24,8},{1,17},{9,25},{17,1},{25,9},{2,18},{10... | collective-permute-start | bytes 1769480 | tf_op jit(solution)/shard_map/ppermute | solution.py:138
  293.6 10.9 %copy-start.1 = (bf16[3,4,192,512]{3,2,1,0:T(8,128)(2,1)S(1)}, bf16[3,4,192,512]{3,2,1,0:T(8,128)(2,1)}, u32[]{:S(2)}) copy-start(bf16[3,4,192,512]{3,2,1,0:T(8,128)(2,1)} %copy-done) | copy-start | bytes 7077892
  293.6 19.7 %collective-permute-start.36 = (bf16[24,3072]{1,0:T(8,128)(2,1)}, bf16[24,3072]{1,0:T(8,128)(2,1)}, u32[]{:S(2)}, u32[]{:S(2)}) collective-permute-start(bf16[24,3072]{1,0:T(8,128)(2,1)} %get-tuple-element.85), channel_id=1, source_target_pairs={{0,2},{1,3},{2,0},{3,1},{4,6},{5,7},{6,4},{7,5},{8,10},{9,11},{10,... | collective-permute-start | bytes 442376 | tf_op jit(solution)/shard_map/ppermute | solution.py:138
  294.5 19.2 %collective-permute-start.38 = (bf16[24,3072]{1,0:T(8,128)(2,1)}, bf16[24,3072]{1,0:T(8,128)(2,1)}, u32[]{:S(2)}, u32[]{:S(2)}) collective-permute-start(bf16[24,3072]{1,0:T(8,128)(2,1)} %get-tuple-element.86), channel_id=1, source_target_pairs={{0,6},{1,7},{2,4},{3,5},{4,2},{5,3},{6,0},{7,1},{8,14},{9,15},{10,... | collective-permute-start | bytes 442376 | tf_op jit(solution)/shard_map/ppermute | solution.py:138
  295.9 17.8 %collective-permute-start.37 = (bf16[24,3072]{1,0:T(8,128)(2,1)}, bf16[24,3072]{1,0:T(8,128)(2,1)}, u32[]{:S(2)}, u32[]{:S(2)}) collective-permute-start(bf16[24,3072]{1,0:T(8,128)(2,1)} %get-tuple-element.87), channel_id=1, source_target_pairs={{0,4},{1,5},{2,6},{3,7},{4,0},{5,1},{6,2},{7,3},{8,12},{9,13},{10,... | collective-permute-start | bytes 442376 | tf_op jit(solution)/shard_map/ppermute | solution.py:138
  306.2 39.9 %all-to-all-start.3 = ((bf16[3,4,192,512]{3,2,0,1:T(8,128)(2,1)}), bf16[3,4,192,512]{3,2,0,1:T(8,128)(2,1)S(1)}, u32[]{:S(2)}, u32[]{:S(2)}) async-start(bf16[3,4,192,512]{3,2,0,1:T(8,128)(2,1)} %copy.139), calls=%async_computation.3 | async-start | bytes 4718592 | tf_op jit(solution)/shard_map/all_to_all | solution.py:319
  310.1 8.3 %collective-permute-start.42 = (bf16[96,768]{1,0:T(8,128)(2,1)S(1)}, bf16[96,768]{1,0:T(8,128)(2,1)S(1)}, u32[]{:S(2)}, u32[]{:S(2)}) collective-permute-start(bf16[96,768]{1,0:T(8,128)(2,1)S(1)} %get-tuple-element.82), channel_id=1, source_target_pairs={{0,2},{1,3},{2,0},{3,1},{4,6},{5,7},{6,4},{7,5},{8,10},{9,11},{10,... | collective-permute-start | bytes 442376 | tf_op jit(solution)/shard_map/ppermute | solution.py:138
  311.9 7.1 %collective-permute-start.44 = (bf16[96,768]{1,0:T(8,128)(2,1)S(1)}, bf16[96,768]{1,0:T(8,128)(2,1)S(1)}, u32[]{:S(2)}, u32[]{:S(2)}) collective-permute-start(bf16[96,768]{1,0:T(8,128)(2,1)S(1)} %get-tuple-element.83), channel_id=1, source_target_pairs={{0,6},{1,7},{2,4},{3,5},{4,2},{5,3},{6,0},{7,1},{8,14},{9,15},{10,... | collective-permute-start | bytes 442376 | tf_op jit(solution)/shard_map/ppermute | solution.py:138
  313.3 10.3 %collective-permute-start.43 = (bf16[96,768]{1,0:T(8,128)(2,1)S(1)}, bf16[96,768]{1,0:T(8,128)(2,1)S(1)}, u32[]{:S(2)}, u32[]{:S(2)}) collective-permute-start(bf16[96,768]{1,0:T(8,128)(2,1)S(1)} %get-tuple-element.84), channel_id=1, source_target_pairs={{0,4},{1,5},{2,6},{3,7},{4,0},{5,1},{6,2},{7,3},{8,12},{9,13},{10,... | collective-permute-start | bytes 442376 | tf_op jit(solution)/shard_map/ppermute | solution.py:138
  315.0 27.3 %collective-permute-start.41 = (bf16[24,3072]{1,0:T(8,128)(2,1)S(1)}, bf16[24,3072]{1,0:T(8,128)(2,1)S(1)}, u32[]{:S(2)}, u32[]{:S(2)}) collective-permute-start(bf16[24,3072]{1,0:T(8,128)(2,1)S(1)} %fusion.71), channel_id=1, source_target_pairs={{0,8},{8,0},{16,24},{24,16},{1,9},{9,1},{17,25},{25,17},{2,10},{10... | collective-permute-start | bytes 442376 | tf_op jit(solution)/shard_map/ppermute | solution.py:138
  317.0 26.8 %collective-permute-start.40 = (bf16[24,3072]{1,0:T(8,128)(2,1)S(1)}, bf16[24,3072]{1,0:T(8,128)(2,1)S(1)}, u32[]{:S(2)}, u32[]{:S(2)}) collective-permute-start(bf16[24,3072]{1,0:T(8,128)(2,1)S(1)} %fusion.71), channel_id=1, source_target_pairs={{0,16},{8,24},{16,0},{24,8},{1,17},{9,25},{17,1},{25,9},{2,18},{10... | collective-permute-start | bytes 442376 | tf_op jit(solution)/shard_map/ppermute | solution.py:138
  318.5 26.6 %collective-permute-start.39 = (bf16[24,3072]{1,0:T(8,128)(2,1)S(1)}, bf16[24,3072]{1,0:T(8,128)(2,1)S(1)}, u32[]{:S(2)}, u32[]{:S(2)}) collective-permute-start(bf16[24,3072]{1,0:T(8,128)(2,1)S(1)} %fusion.71), channel_id=1, source_target_pairs={{0,24},{8,16},{16,8},{24,0},{1,25},{9,17},{17,9},{25,1},{2,26},{10... | collective-permute-start | bytes 442376 | tf_op jit(solution)/shard_map/ppermute | solution.py:138
  324.3 46.7 %collective-permute-start.47 = (bf16[96,768]{1,0:T(8,128)(2,1)}, bf16[96,768]{1,0:T(8,128)(2,1)S(1)}, u32[]{:S(2)}, u32[]{:S(2)}) collective-permute-start(bf16[96,768]{1,0:T(8,128)(2,1)} %fusion.68), channel_id=1, source_target_pairs={{0,8},{8,0},{16,24},{24,16},{1,9},{9,1},{17,25},{25,17},{2,10},{10... | collective-permute-start | bytes 442376 | tf_op jit(solution)/shard_map/ppermute | solution.py:138
  326.0 46.5 %collective-permute-start.46 = (bf16[96,768]{1,0:T(8,128)(2,1)}, bf16[96,768]{1,0:T(8,128)(2,1)S(1)}, u32[]{:S(2)}, u32[]{:S(2)}) collective-permute-start(bf16[96,768]{1,0:T(8,128)(2,1)} %fusion.68), channel_id=1, source_target_pairs={{0,16},{8,24},{16,0},{24,8},{1,17},{9,25},{17,1},{25,9},{2,18},{10... | collective-permute-start | bytes 442376 | tf_op jit(solution)/shard_map/ppermute | solution.py:138
  342.3 31.7 %collective-permute-start.45 = (bf16[96,768]{1,0:T(8,128)(2,1)}, bf16[96,768]{1,0:T(8,128)(2,1)}, u32[]{:S(2)}, u32[]{:S(2)}) collective-permute-start(bf16[96,768]{1,0:T(8,128)(2,1)} %fusion.68), channel_id=1, source_target_pairs={{0,24},{8,16},{16,8},{24,0},{1,25},{9,17},{17,9},{25,1},{2,26},{10... | collective-permute-start | bytes 442376 | tf_op jit(solution)/shard_map/ppermute | solution.py:138
  364.4 5.8 %collective-permute-start.16 = (bf16[4,4,32,768]{3,2,1,0:T(8,128)(2,1)S(1)}, bf16[4,4,32,768]{3,2,1,0:T(8,128)(2,1)S(1)}, u32[]{:S(2)}, u32[]{:S(2)}) collective-permute-start(bf16[4,4,32,768]{3,2,1,0:T(8,128)(2,1)S(1)} %fusion.51), channel_id=1, source_target_pairs={{0,1},{1,0},{2,3},{3,2},{4,5},{5,4},{6,7},{7,6},{8,9},{9,8},{10,11... | collective-permute-start | bytes 2359304 | tf_op jit(solution)/shard_map/ppermute | solution.py:138
  368.2 27.0 %collective-permute-start.26 = (bf16[4,4,24,2304]{3,2,1,0:T(8,128)(2,1)S(1)}, bf16[4,4,24,2304]{3,2,1,0:T(8,128)(2,1)S(1)}, u32[]{:S(2)}, u32[]{:S(2)}) collective-permute-start(bf16[4,4,24,2304]{3,2,1,0:T(8,128)(2,1)S(1)} %fusion.30), channel_id=1, source_target_pairs={{0,1},{1,0},{2,3},{3,2},{4,5},{5,4},{6,7},{7,6},{8,9},{9,8},{10,11... | collective-permute-start | bytes 5308424 | tf_op jit(solution)/shard_map/ppermute | solution.py:138
  370.4 7.9 %collective-permute-start.17 = (bf16[4,32,768]{2,1,0:T(8,128)(2,1)S(1)}, bf16[4,32,768]{2,1,0:T(8,128)(2,1)S(1)}, u32[]{:S(2)}, u32[]{:S(2)}) collective-permute-start(bf16[4,32,768]{2,1,0:T(8,128)(2,1)S(1)} %get-tuple-element.79), channel_id=1, source_target_pairs={{0,8},{8,0},{16,24},{24,16},{1,9},{9,1},{17,25},{25,17},{2,10},{10... | collective-permute-start | bytes 589832 | tf_op jit(solution)/shard_map/ppermute | solution.py:138
  371.0 10.3 %collective-permute-start.19 = (bf16[4,32,768]{2,1,0:T(8,128)(2,1)S(1)}, bf16[4,32,768]{2,1,0:T(8,128)(2,1)S(1)}, u32[]{:S(2)}, u32[]{:S(2)}) collective-permute-start(bf16[4,32,768]{2,1,0:T(8,128)(2,1)S(1)} %get-tuple-element.80), channel_id=1, source_target_pairs={{0,24},{8,16},{16,8},{24,0},{1,25},{9,17},{17,9},{25,1},{2,26},{10... | collective-permute-start | bytes 589832 | tf_op jit(solution)/shard_map/ppermute | solution.py:138
  372.5 10.2 %collective-permute-start.18 = (bf16[4,32,768]{2,1,0:T(8,128)(2,1)S(1)}, bf16[4,32,768]{2,1,0:T(8,128)(2,1)S(1)}, u32[]{:S(2)}, u32[]{:S(2)}) collective-permute-start(bf16[4,32,768]{2,1,0:T(8,128)(2,1)S(1)} %get-tuple-element.81), channel_id=1, source_target_pairs={{0,16},{8,24},{16,0},{24,8},{1,17},{9,25},{17,1},{25,9},{2,18},{10... | collective-permute-start | bytes 589832 | tf_op jit(solution)/shard_map/ppermute | solution.py:138
  382.8 4.5 %collective-permute-start.20 = (bf16[32,768]{1,0:T(8,128)(2,1)S(1)}, bf16[32,768]{1,0:T(8,128)(2,1)S(1)}, u32[]{:S(2)}, u32[]{:S(2)}) collective-permute-start(bf16[32,768]{1,0:T(8,128)(2,1)S(1)} %get-tuple-element.110), channel_id=1, source_target_pairs={{0,2},{1,3},{2,0},{3,1},{4,6},{5,7},{6,4},{7,5},{8,10},{9,11},{10,... | collective-permute-start | bytes 147464 | tf_op jit(solution)/shard_map/ppermute | solution.py:138
  384.7 5.9 %collective-permute-start.22 = (bf16[32,768]{1,0:T(8,128)(2,1)S(1)}, bf16[32,768]{1,0:T(8,128)(2,1)S(1)}, u32[]{:S(2)}, u32[]{:S(2)}) collective-permute-start(bf16[32,768]{1,0:T(8,128)(2,1)S(1)} %get-tuple-element.111), channel_id=1, source_target_pairs={{0,6},{1,7},{2,4},{3,5},{4,2},{5,3},{6,0},{7,1},{8,14},{9,15},{10,... | collective-permute-start | bytes 147464 | tf_op jit(solution)/shard_map/ppermute | solution.py:138
  386.0 5.6 %collective-permute-start.21 = (bf16[32,768]{1,0:T(8,128)(2,1)S(1)}, bf16[32,768]{1,0:T(8,128)(2,1)S(1)}, u32[]{:S(2)}, u32[]{:S(2)}) collective-permute-start(bf16[32,768]{1,0:T(8,128)(2,1)S(1)} %get-tuple-element.112), channel_id=1, source_target_pairs={{0,4},{1,5},{2,6},{3,7},{4,0},{5,1},{6,2},{7,3},{8,12},{9,13},{10,... | collective-permute-start | bytes 147464 | tf_op jit(solution)/shard_map/ppermute | solution.py:138
  391.6 8.0 %collective-permute-start.25 = (bf16[32,768]{1,0:T(8,128)(2,1)S(1)}, bf16[32,768]{1,0:T(8,128)(2,1)S(1)}, u32[]{:S(2)}, u32[]{:S(2)}) collective-permute-start(bf16[32,768]{1,0:T(8,128)(2,1)S(1)} %fusion.90), channel_id=1, source_target_pairs={{0,8},{8,0},{16,24},{24,16},{1,9},{9,1},{17,25},{25,17},{2,10},{10... | collective-permute-start | bytes 147464 | tf_op jit(solution)/shard_map/ppermute | solution.py:138
  392.1 9.2 %collective-permute-start.24 = (bf16[32,768]{1,0:T(8,128)(2,1)S(1)}, bf16[32,768]{1,0:T(8,128)(2,1)S(1)}, u32[]{:S(2)}, u32[]{:S(2)}) collective-permute-start(bf16[32,768]{1,0:T(8,128)(2,1)S(1)} %fusion.90), channel_id=1, source_target_pairs={{0,16},{8,24},{16,0},{24,8},{1,17},{9,25},{17,1},{25,9},{2,18},{10... | collective-permute-start | bytes 147464 | tf_op jit(solution)/shard_map/ppermute | solution.py:138
  393.7 7.6 %collective-permute-start.23 = (bf16[32,768]{1,0:T(8,128)(2,1)S(1)}, bf16[32,768]{1,0:T(8,128)(2,1)S(1)}, u32[]{:S(2)}, u32[]{:S(2)}) collective-permute-start(bf16[32,768]{1,0:T(8,128)(2,1)S(1)} %fusion.90), channel_id=1, source_target_pairs={{0,24},{8,16},{16,8},{24,0},{1,25},{9,17},{17,9},{25,1},{2,26},{10... | collective-permute-start | bytes 147464 | tf_op jit(solution)/shard_map/ppermute | solution.py:138
  396.7 13.3 %collective-permute-start.27 = (bf16[4,24,2304]{2,1,0:T(8,128)(2,1)}, bf16[4,24,2304]{2,1,0:T(8,128)(2,1)}, u32[]{:S(2)}, u32[]{:S(2)}) collective-permute-start(bf16[4,24,2304]{2,1,0:T(8,128)(2,1)} %get-tuple-element.70), channel_id=1, source_target_pairs={{0,8},{8,0},{16,24},{24,16},{1,9},{9,1},{17,25},{25,17},{2,10},{10... | collective-permute-start | bytes 1327112 | tf_op jit(solution)/shard_map/ppermute | solution.py:138
  397.1 18.6 %collective-permute-start.29 = (bf16[4,24,2304]{2,1,0:T(8,128)(2,1)}, bf16[4,24,2304]{2,1,0:T(8,128)(2,1)}, u32[]{:S(2)}, u32[]{:S(2)}) collective-permute-start(bf16[4,24,2304]{2,1,0:T(8,128)(2,1)} %get-tuple-element.71), channel_id=1, source_target_pairs={{0,24},{8,16},{16,8},{24,0},{1,25},{9,17},{17,9},{25,1},{2,26},{10... | collective-permute-start | bytes 1327112 | tf_op jit(solution)/shard_map/ppermute | solution.py:138
  399.6 17.0 %collective-permute-start.28 = (bf16[4,24,2304]{2,1,0:T(8,128)(2,1)}, bf16[4,24,2304]{2,1,0:T(8,128)(2,1)}, u32[]{:S(2)}, u32[]{:S(2)}) collective-permute-start(bf16[4,24,2304]{2,1,0:T(8,128)(2,1)} %get-tuple-element.72), channel_id=1, source_target_pairs={{0,16},{8,24},{16,0},{24,8},{1,17},{9,25},{17,1},{25,9},{2,18},{10... | collective-permute-start | bytes 1327112 | tf_op jit(solution)/shard_map/ppermute | solution.py:138
  419.0 4.8 %collective-permute-start.30 = (bf16[24,2304]{1,0:T(8,128)(2,1)S(1)}, bf16[24,2304]{1,0:T(8,128)(2,1)S(1)}, u32[]{:S(2)}, u32[]{:S(2)}) collective-permute-start(bf16[24,2304]{1,0:T(8,128)(2,1)S(1)} %get-tuple-element.90), channel_id=1, source_target_pairs={{0,2},{1,3},{2,0},{3,1},{4,6},{5,7},{6,4},{7,5},{8,10},{9,11},{10,... | collective-permute-start | bytes 331784 | tf_op jit(solution)/shard_map/ppermute | solution.py:138
  419.2 6.7 %collective-permute-start.32 = (bf16[24,2304]{1,0:T(8,128)(2,1)S(1)}, bf16[24,2304]{1,0:T(8,128)(2,1)S(1)}, u32[]{:S(2)}, u32[]{:S(2)}) collective-permute-start(bf16[24,2304]{1,0:T(8,128)(2,1)S(1)} %get-tuple-element.91), channel_id=1, source_target_pairs={{0,6},{1,7},{2,4},{3,5},{4,2},{5,3},{6,0},{7,1},{8,14},{9,15},{10,... | collective-permute-start | bytes 331784 | tf_op jit(solution)/shard_map/ppermute | solution.py:138
  420.8 8.1 %collective-permute-start.31 = (bf16[24,2304]{1,0:T(8,128)(2,1)S(1)}, bf16[24,2304]{1,0:T(8,128)(2,1)S(1)}, u32[]{:S(2)}, u32[]{:S(2)}) collective-permute-start(bf16[24,2304]{1,0:T(8,128)(2,1)S(1)} %get-tuple-element.92), channel_id=1, source_target_pairs={{0,4},{1,5},{2,6},{3,7},{4,0},{5,1},{6,2},{7,3},{8,12},{9,13},{10,... | collective-permute-start | bytes 331784 | tf_op jit(solution)/shard_map/ppermute | solution.py:138
  429.9 5.1 %collective-permute-start.35 = (bf16[24,2304]{1,0:T(8,128)(2,1)S(1)}, bf16[24,2304]{1,0:T(8,128)(2,1)S(1)}, u32[]{:S(2)}, u32[]{:S(2)}) collective-permute-start(bf16[24,2304]{1,0:T(8,128)(2,1)S(1)} %fusion.74), channel_id=1, source_target_pairs={{0,8},{8,0},{16,24},{24,16},{1,9},{9,1},{17,25},{25,17},{2,10},{10... | collective-permute-start | bytes 331784 | tf_op jit(solution)/shard_map/ppermute | solution.py:138
  430.8 4.7 %collective-permute-start.34 = (bf16[24,2304]{1,0:T(8,128)(2,1)S(1)}, bf16[24,2304]{1,0:T(8,128)(2,1)S(1)}, u32[]{:S(2)}, u32[]{:S(2)}) collective-permute-start(bf16[24,2304]{1,0:T(8,128)(2,1)S(1)} %fusion.74), channel_id=1, source_target_pairs={{0,16},{8,24},{16,0},{24,8},{1,17},{9,25},{17,1},{25,9},{2,18},{10... | collective-permute-start | bytes 331784 | tf_op jit(solution)/shard_map/ppermute | solution.py:138
  431.4 5.6 %collective-permute-start.33 = (bf16[24,2304]{1,0:T(8,128)(2,1)S(1)}, bf16[24,2304]{1,0:T(8,128)(2,1)S(1)}, u32[]{:S(2)}, u32[]{:S(2)}) collective-permute-start(bf16[24,2304]{1,0:T(8,128)(2,1)S(1)} %fusion.74), channel_id=1, source_target_pairs={{0,24},{8,16},{16,8},{24,0},{1,25},{9,17},{17,9},{25,1},{2,26},{10... | collective-permute-start | bytes 331784 | tf_op jit(solution)/shard_map/ppermute | solution.py:138
  (43 other events, 151.6 us)
Sparse Core Ops, SparseCore 0:
  9.7 51.3 all-gather.3
  62.7 21.7 all-gather.5
  86.2 51.3 all-gather.7
